TPU v7x, 32 devices: a whole 2x2x4 slice. The times are simulated.
32 devices in a mesh: row: 4 (over z), col: 8 (over y, x, core).
Axes of the slice: x: 2, y: 2, z: 4, core: 2. Of those that a mesh axis runs over, the one named last changes fastest.
Arguments:
- green_blocks: bfloat16 [4, 8, 12, 2, 288, 288], P('row', 'col'), may hold values from -0.125 to 0.125
- slot_rows: int32 [4, 8, 12], P('row', 'col'), may hold values from 0 to 7, as said below
- slot_cols: int32 [4, 8, 12], P('row', 'col'), may hold values from 0 to 3
- slot_count: int32 [4, 8], P('row', 'col'), may hold values from 2 to 12, as said below
- cell_class: int32 [4, 8, 96], P(None, 'col'), may hold values from 0 to 15
- class_contrast: float32 [16, 2], replicated, may hold values from -0.6 to 0.6
- background: float32 [2, 32, 4, 8, 288], P(None, None, None, 'col'), may hold values from -6 to 6
Outputs:
- total_field: float32 [2, 32, 4, 8, 288], P(None, None, None, 'col')
Inputs may be any that keep to these rules, and one draw needn't show every extreme that they name: slot_rows[r, c, s] and slot_cols[r, c, s] name different block pairs within one device's slots, and every slot, used or not, names a block in the upper triangle: (slot_rows // 2) * 8 + 2 r + slot_rows % 2 is at most slot_cols * 8 + c. Slots from slot_count[r, c] on are not used. `slot_count`: some device holds exactly 12 stored blocks.
All inputs are finite; a program needn't handle non-finite values.
Results may differ from a plain program's by a relative error of at most 0.0033.
Values may be sent and summed in bfloat16 or wider, within the bound.
No kernel may reach another device: no remote copies, remote signals or barrier semaphores. Data moves between devices by JAX's collectives and lax.ppermute only.
A program may use at most 64 MiB of HBM per device.

v0:
```python
import jax
import jax.numpy as jnp
from jax import lax
from jax.sharding import PartitionSpec as P

PRODUCTS = 3


def from_root(array, axis, root):
    mine = lax.axis_index(axis) == root
    return lax.psum(jnp.where(mine, array, jnp.zeros_like(array)), axis)


def complex_scale(field_now, contrast_re, contrast_im):
    real_part = field_now[0]
    imag_part = field_now[1]
    scaled = jnp.stack(
        [
            contrast_re * real_part - contrast_im * imag_part,
            contrast_re * imag_part + contrast_im * real_part,
        ]
    )
    return scaled.astype(jnp.bfloat16)


def combine(products):
    return jnp.stack([products[0, 0] - products[1, 1], products[0, 1] + products[1, 0]])


def local(green_blocks, slot_rows, slot_cols, slot_count, cell_class, class_contrast, background):
    row_index = lax.axis_index("row")
    col_index = lax.axis_index("col")
    stride = lax.axis_size("col")
    green_tiles = green_blocks[0, 0]
    slot_total = green_tiles.shape[0]
    entries = green_tiles.shape[-1]
    sources = background.shape[1]
    col_blocks = background.shape[2]
    row_blocks = 2 * col_blocks
    local_rows = slot_rows[0, 0]
    local_cols = slot_cols[0, 0]
    global_rows = local_rows // 2 * stride + 2 * row_index + local_rows % 2
    global_cols = local_cols * stride + col_index
    off_diagonal = (global_rows != global_cols).astype(jnp.float32)
    living = (jnp.arange(slot_total) < slot_count[0, 0]).astype(jnp.float32)
    row_pick = (local_rows[:, None] == jnp.arange(row_blocks)[None, :]).astype(
        jnp.float32
    ) * living[:, None]
    col_pick = (local_cols[:, None] == jnp.arange(col_blocks)[None, :]).astype(jnp.float32) * (
        living * off_diagonal
    )[:, None]
    classes = class_contrast.shape[0]
    lookup = (cell_class[:, 0, :, None] == jnp.arange(classes)[None, None, :]).astype(jnp.float32)
    values = jnp.einsum("bte,ec->btc", lookup, class_contrast, precision=lax.Precision.HIGHEST)
    contrast_re = jnp.tile(values[:, :, 0], (1, 3))
    contrast_im = jnp.tile(values[:, :, 1], (1, 3))
    start_field = background[:, :, :, 0, :]
    field_now = start_field
    current = complex_scale(field_now, contrast_re, contrast_im)
    for step_index in range(PRODUCTS):
        final_step = step_index + 1 == PRODUCTS
        halves = [from_root(current, "col", 2 * row_index + parity) for parity in range(2)]
        row_current = jnp.stack(halves, axis=3).reshape(2, sources, row_blocks, entries)
        direct_in = jnp.take(current, local_cols, axis=2)
        mirror_in = jnp.take(row_current, local_rows, axis=2)
        direct_terms = combine(
            jnp.einsum(
                "sqoi,pksi->qpkso", green_tiles, direct_in, preferred_element_type=jnp.float32
            )
        )
        mirror_terms = combine(
            jnp.einsum(
                "sqoi,pkso->qpksi", green_tiles, mirror_in, preferred_element_type=jnp.float32
            )
        )
        direct_part = jnp.einsum(
            "pkse,sb->pkbe", direct_terms, row_pick, precision=lax.Precision.HIGHEST
        )
        mirror_part = jnp.einsum(
            "pkse,sb->pkbe", mirror_terms, col_pick, precision=lax.Precision.HIGHEST
        )
        row_total = lax.psum(direct_part, "col")
        owned_part = lax.dynamic_index_in_dim(
            row_total.reshape(2, sources, col_blocks, 2, entries),
            col_index % 2,
            axis=3,
            keepdims=False,
        )
        direct_here = from_root(owned_part, "row", col_index // 2)
        column_total = lax.psum(mirror_part, "row")
        field_now = start_field + column_total + direct_here
        if not final_step:
            current = complex_scale(field_now, contrast_re, contrast_im)
    return field_now[:, :, :, None, :]


def solution(mesh):
    in_specs = (
        P("row", "col", None, None, None, None),
        P("row", "col", None),
        P("row", "col", None),
        P("row", "col"),
        P(None, "col", None),
        P(),
        P(None, None, None, "col", None),
    )
    out_specs = P(None, None, None, "col", None)
    return jax.shard_map(local, mesh=mesh, in_specs=in_specs, out_specs=out_specs, check_vma=False)
```

profile of v0, /device:TPU:0, one launch (start us, length us, event | category | flops | bytes accessed | tf_op | source)
XLA Modules:
  0.0 510.9 jit_solution(10632752438444261856)
XLA Ops:
  6.6 0.7 copy-done
  7.2 0.8 fusion.106
  8.2 1.3 fusion.152
  9.6 1.0 select_bitcast_fusion.8
  10.8 0.7 gather_fusion.1
  11.5 4.6 fusion.15
  17.0 1.5 fusion.42
  18.8 1.5 copy.43
  20.4 47.4 %all-reduce.32.cloned.1.call-done = (bf16[2,32,4,1,288]{4,2,1,0,3:T(4,128)(2,1)}, bf16[2,32,4,1,288]{4,2,1,0,3:T(4,128)(2,1)}) async-done(((bf16[2,32,4,1,288]{4,2,1,0,3:T(4,128)(2,1)}, bf16[2,32,4,1,288]{4,2,1,0,3:T(4,128)(2,1)}), (bf16[2,32,4,1,288]{4,2,1,0,3:T(4,128)(2,1)}, bf16[2,32,4,1,288]{4,2,1,0,3:T(4,128)(2,1)})) %all-reduce.32.cloned.1.call-update) | async-done | bytes 294928 | tf_op jit(solution)/shard_map/psum | solution.py:11
  67.8 1.3 pad_maximum_fusion.6
  69.1 0.7 gather_fusion
  69.8 3.8 fusion.12
  73.9 2.3 fusion.51
  76.2 49.6 %all-reduce.16.cloned.1.call-done = f32[2,32,4,2,288]{4,2,1,0,3:T(4,128)} async-done(((f32[2,32,4,2,288]{4,2,1,0,3:T(4,128)}), f32[2,32,4,2,288]{4,2,1,0,3:T(4,128)}) %all-reduce.16.cloned.1.call-update) | async-done | bytes 589840 | tf_op jit(solution)/shard_map/psum | solution.py:82
  125.8 1.8 select_bitcast_fusion.2
  127.7 43.8 %all-reduce.26.cloned.1.call-done = (f32[2,32,4,288]{3,2,1,0:T(4,128)}, f32[2,32,4,288]{3,2,1,0:T(4,128)}) async-done(((f32[2,32,4,288]{3,2,1,0:T(4,128)}, f32[2,32,4,288]{3,2,1,0:T(4,128)}), (f32[2,32,4,288]{3,2,1,0:T(4,128)}, f32[2,32,4,288]{3,2,1,0:T(4,128)})) %all-reduce.26.cloned.1.call-update) | async-done | bytes 589840 | tf_op jit(solution)/shard_map/psum | solution.py:11
  171.5 1.3 fusion.96
  173.0 1.0 select_bitcast_fusion.6
  174.0 0.7 gather_fusion.3
  174.7 4.6 fusion.21
  179.5 0.2 all-reduce.18.cloned.1.call-start
  179.8 1.5 fusion.45
  181.5 1.5 copy.53
  183.1 50.0 %all-reduce.30.cloned.1.call-done = (bf16[2,32,4,1,288]{4,2,1,0,3:T(4,128)(2,1)}, bf16[2,32,4,1,288]{4,2,1,0,3:T(4,128)(2,1)}) async-done(((bf16[2,32,4,1,288]{4,2,1,0,3:T(4,128)(2,1)}, bf16[2,32,4,1,288]{4,2,1,0,3:T(4,128)(2,1)}), (bf16[2,32,4,1,288]{4,2,1,0,3:T(4,128)(2,1)}, bf16[2,32,4,1,288]{4,2,1,0,3:T(4,128)(2,1)})) %all-reduce.30.cloned.1.call-update) | async-done | bytes 294928 | tf_op jit(solution)/shard_map/psum | solution.py:11
  233.1 1.3 pad_maximum_fusion.7
  234.5 0.7 gather_fusion.2
  235.2 3.8 fusion.18
  239.2 2.3 fusion.54
  241.5 49.4 %all-reduce.18.cloned.1.call-done = f32[2,32,4,2,288]{4,2,1,0,3:T(4,128)} async-done(((f32[2,32,4,2,288]{4,2,1,0,3:T(4,128)}), f32[2,32,4,2,288]{4,2,1,0,3:T(4,128)}) %all-reduce.18.cloned.1.call-update) | async-done | bytes 589840 | tf_op jit(solution)/shard_map/psum | solution.py:82
  291.0 1.8 select_bitcast_fusion.1
  292.9 43.7 %all-reduce.24.cloned.1.call-done = (f32[2,32,4,288]{3,2,1,0:T(4,128)}, f32[2,32,4,288]{3,2,1,0:T(4,128)}) async-done(((f32[2,32,4,288]{3,2,1,0:T(4,128)}, f32[2,32,4,288]{3,2,1,0:T(4,128)}), (f32[2,32,4,288]{3,2,1,0:T(4,128)}, f32[2,32,4,288]{3,2,1,0:T(4,128)})) %all-reduce.24.cloned.1.call-update) | async-done | bytes 589840 | tf_op jit(solution)/shard_map/psum | solution.py:11
  336.6 1.3 fusion.97
  338.0 1.0 select_bitcast_fusion.4
  339.0 0.7 gather_fusion.5
  339.7 4.6 fusion.27
  344.7 1.5 fusion.48
  346.4 1.5 copy.63
  347.9 0.3 all-reduce.22.cloned.1.call-start
  348.1 50.0 %all-reduce.28.cloned.1.call-done = (bf16[2,32,4,1,288]{4,2,1,0,3:T(4,128)(2,1)}, bf16[2,32,4,1,288]{4,2,1,0,3:T(4,128)(2,1)}) async-done(((bf16[2,32,4,1,288]{4,2,1,0,3:T(4,128)(2,1)}, bf16[2,32,4,1,288]{4,2,1,0,3:T(4,128)(2,1)}), (bf16[2,32,4,1,288]{4,2,1,0,3:T(4,128)(2,1)}, bf16[2,32,4,1,288]{4,2,1,0,3:T(4,128)(2,1)})) %all-reduce.28.cloned.1.call-update) | async-done | bytes 294928 | tf_op jit(solution)/shard_map/psum | solution.py:11
  398.1 1.3 pad_maximum_fusion.8
  399.5 0.7 gather_fusion.4
  400.2 3.8 fusion.24
  404.2 2.3 fusion.57
  406.6 49.6 %all-reduce.20.cloned.1.call-done = f32[2,32,4,2,288]{4,2,1,0,3:T(4,128)} async-done(((f32[2,32,4,2,288]{4,2,1,0,3:T(4,128)}), f32[2,32,4,2,288]{4,2,1,0,3:T(4,128)}) %all-reduce.20.cloned.1.call-update) | async-done | bytes 589840 | tf_op jit(solution)/shard_map/psum | solution.py:82
  456.2 1.8 select_bitcast_fusion
  458.0 43.9 %all-reduce.22.cloned.1.call-done = (f32[2,32,4,288]{3,2,1,0:T(4,128)}, f32[2,32,4,288]{3,2,1,0:T(4,128)}) async-done(((f32[2,32,4,288]{3,2,1,0:T(4,128)}, f32[2,32,4,288]{3,2,1,0:T(4,128)}), (f32[2,32,4,288]{3,2,1,0:T(4,128)}, f32[2,32,4,288]{3,2,1,0:T(4,128)})) %all-reduce.22.cloned.1.call-update) | async-done | bytes 589840 | tf_op jit(solution)/shard_map/psum | solution.py:11
  501.9 1.3 fusion.99
  503.2 1.1 copy.64
  (64 shorter events, 3.0 us)
Async XLA Ops:
  6.5 0.7 copy-start
  6.5 4.2 copy-start.3
  6.5 4.2 copy-start.2
  6.5 61.2 %all-reduce.32.cloned.1.call-start = ((), (), s32[]{:S(2)}) async-start(), calls=%async_computation.8 | async-start | bytes 786432 | tf_op jit(solution)/shard_map/psum | solution.py:11
  10.7 115.1 %all-reduce.16.cloned.1.call-start = ((), (), s32[]{:S(2)}) async-start(), calls=%async_computation | async-start | bytes 1572864 | tf_op jit(solution)/shard_map/psum | solution.py:82
  20.2 151.3 %all-reduce.26.cloned.1.call-start = ((), (), s32[]{:S(2)}) async-start(), calls=%async_computation.5 | async-start | bytes 1572864 | tf_op jit(solution)/shard_map/psum | solution.py:11
  73.9 97.7 %copy-start.1 = (f32[2,32,4,1,288]{4,3,2,1,0:T(1,128)S(1)}, f32[2,32,4,1,288]{4,3,2,1,0:T(1,128)}, u32[]{:S(2)}) copy-start(f32[2,32,4,1,288]{4,3,2,1,0:T(1,128)} %param.17) | copy-start | bytes 884740
  127.7 105.4 %all-reduce.30.cloned.1.call-start = ((), (), s32[]{:S(2)}) async-start(), calls=%async_computation.7 | async-start | bytes 786432 | tf_op jit(solution)/shard_map/psum | solution.py:11
  179.5 111.5 %all-reduce.18.cloned.1.call-start = ((), (), s32[]{:S(2)}) async-start(), calls=%async_computation.1 | async-start | bytes 1572864 | tf_op jit(solution)/shard_map/psum | solution.py:82
  183.0 153.6 %all-reduce.24.cloned.1.call-start = ((), (), s32[]{:S(2)}) async-start(), calls=%async_computation.4 | async-start | bytes 1572864 | tf_op jit(solution)/shard_map/psum | solution.py:11
  292.8 105.3 %all-reduce.28.cloned.1.call-start = ((), (), s32[]{:S(2)}) async-start(), calls=%async_computation.6 | async-start | bytes 786432 | tf_op jit(solution)/shard_map/psum | solution.py:11
  344.5 111.6 %all-reduce.20.cloned.1.call-start = ((), (), s32[]{:S(2)}) async-start(), calls=%async_computation.2 | async-start | bytes 1572864 | tf_op jit(solution)/shard_map/psum | solution.py:82
  347.9 154.0 %all-reduce.22.cloned.1.call-start = ((), (), s32[]{:S(2)}) async-start(), calls=%async_computation.3 | async-start | bytes 1572864 | tf_op jit(solution)/shard_map/psum | solution.py:11
Sparse Core Ops, SparseCore 0:
  10.8 56.8 all-reduce.31
  70.9 54.8 all-reduce.15
  128.2 43.2 all-reduce.25
  179.6 53.4 all-reduce.29
  236.1 54.8 all-reduce.17
  293.3 43.2 all-reduce.23
  344.7 53.4 all-reduce.27
  401.3 54.8 all-reduce.19
  458.6 43.2 all-reduce.21
where the time goes:
time: 512 us; the launch traced here: 511 us
  waiting for transfers between devices  428 us (84%)
  matrix products  37.7 us (7%)
  other arithmetic  18.1 us (4%)
  between operations  14.3 us (3%)
  local copies, waits for them, and re-layouts  12.4 us (2%)
    psum x6, waiting for transfers between devices, from_root(): return lax.psum(jnp.where(mine, array, jnp.zeros_like(array)), axis)  279 us
    psum x3, waiting for transfers between devices, local(): row_total = lax.psum(direct_part, 'col')  149 us
    dot_general x3, matrix products, local(): jnp.einsum('sqoi,pksi->qpkso', green_tiles, direct_in, preferred_element_...  13.9 us
    dot_general x3, matrix products, local(): jnp.einsum('sqoi,pkso->qpksi', green_tiles, mirror_in, preferred_element_...  11.4 us
  transfers between devices with their start and end apart: 9, of which 9 were waited for; matrix products, arithmetic and copies ran while one was open for 8% of the time, Pallas kernels for 0%

commit v1 on v0

--- a/solution.py
+++ b/solution.py
@@ -1,9 +1,15 @@
 import jax
 import jax.numpy as jnp
 from jax import lax
+from jax.experimental import pallas as pl
+from jax.experimental.pallas import tpu as pltpu
 from jax.sharding import PartitionSpec as P
 
 PRODUCTS = 3
+LANES = 128
+VMEM_BYTES = 8 * 1024 * 1024
+BF = jnp.bfloat16
+F32 = jnp.float32
 
 
 def from_root(array, axis, root):
@@ -20,14 +26,14 @@
             contrast_re * imag_part + contrast_im * real_part,
         ]
     )
-    return scaled.astype(jnp.bfloat16)
+    return scaled.astype(BF)
 
 
 def combine(products):
     return jnp.stack([products[0, 0] - products[1, 1], products[0, 1] + products[1, 0]])
 
 
-def local(green_blocks, slot_rows, slot_cols, slot_count, cell_class, class_contrast, background):
+def local_general(green_blocks, slot_rows, slot_cols, slot_count, cell_class, class_contrast, background):
     row_index = lax.axis_index("row")
     col_index = lax.axis_index("col")
     stride = lax.axis_size("col")
@@ -41,16 +47,14 @@
     local_cols = slot_cols[0, 0]
     global_rows = local_rows // 2 * stride + 2 * row_index + local_rows % 2
     global_cols = local_cols * stride + col_index
-    off_diagonal = (global_rows != global_cols).astype(jnp.float32)
-    living = (jnp.arange(slot_total) < slot_count[0, 0]).astype(jnp.float32)
-    row_pick = (local_rows[:, None] == jnp.arange(row_blocks)[None, :]).astype(
-        jnp.float32
-    ) * living[:, None]
-    col_pick = (local_cols[:, None] == jnp.arange(col_blocks)[None, :]).astype(jnp.float32) * (
+    off_diagonal = (global_rows != global_cols).astype(F32)
+    living = (jnp.arange(slot_total) < slot_count[0, 0]).astype(F32)
+    row_pick = (local_rows[:, None] == jnp.arange(row_blocks)[None, :]).astype(F32) * living[:, None]
+    col_pick = (local_cols[:, None] == jnp.arange(col_blocks)[None, :]).astype(F32) * (
         living * off_diagonal
     )[:, None]
     classes = class_contrast.shape[0]
-    lookup = (cell_class[:, 0, :, None] == jnp.arange(classes)[None, None, :]).astype(jnp.float32)
+    lookup = (cell_class[:, 0, :, None] == jnp.arange(classes)[None, None, :]).astype(F32)
     values = jnp.einsum("bte,ec->btc", lookup, class_contrast, precision=lax.Precision.HIGHEST)
     contrast_re = jnp.tile(values[:, :, 0], (1, 3))
     contrast_im = jnp.tile(values[:, :, 1], (1, 3))
@@ -64,14 +68,10 @@
         direct_in = jnp.take(current, local_cols, axis=2)
         mirror_in = jnp.take(row_current, local_rows, axis=2)
         direct_terms = combine(
-            jnp.einsum(
-                "sqoi,pksi->qpkso", green_tiles, direct_in, preferred_element_type=jnp.float32
-            )
+            jnp.einsum("sqoi,pksi->qpkso", green_tiles, direct_in, preferred_element_type=F32)
         )
         mirror_terms = combine(
-            jnp.einsum(
-                "sqoi,pkso->qpksi", green_tiles, mirror_in, preferred_element_type=jnp.float32
-            )
+            jnp.einsum("sqoi,pkso->qpksi", green_tiles, mirror_in, preferred_element_type=F32)
         )
         direct_part = jnp.einsum(
             "pkse,sb->pkbe", direct_terms, row_pick, precision=lax.Precision.HIGHEST
@@ -92,6 +92,344 @@
         if not final_step:
             current = complex_scale(field_now, contrast_re, contrast_im)
     return field_now[:, :, :, None, :]
+
+
+def turned(value):
+    shape = value.shape
+    tiles = value.reshape(shape[0] // 8, 8, shape[1])
+    return jnp.concatenate([-tiles[:, 4:], tiles[:, :4]], axis=1).reshape(shape)
+
+
+def put_block(xs_ref, xt_ref, at, piece, value, width):
+    lanes = pl.ds(piece * LANES, width)
+    xs_ref[at, :, lanes] = value[:, :width].astype(BF)
+    xt_ref[at, :, lanes] = turned(value)[:, :width].astype(BF)
+
+
+def unpack_half(msg_ref, q, half, xs_ref, xt_ref, at):
+    groups = xs_ref.shape[1] // 8
+    tail = xs_ref.shape[2] - 2 * LANES
+    for piece in range(2):
+        both = msg_ref[q * groups : (q + 1) * groups, piece * 16 : piece * 16 + 16, :].astype(F32)
+        value = both[:, half * 8 : half * 8 + 8, :].reshape(groups * 8, LANES)
+        put_block(xs_ref, xt_ref, at, piece, value, LANES)
+    ends = msg_ref[q * groups : (q + 1) * groups, 32:40, :].astype(F32).reshape(groups * 8, LANES)
+    if half:
+        ends = pltpu.roll(ends, LANES - tail, 1)
+    put_block(xs_ref, xt_ref, at, 2, ends, tail)
+
+
+def copy_in(x_ref, xs_ref, xt_ref, offset):
+    for q in range(x_ref.shape[0]):
+        value = x_ref[q].astype(F32)
+        xs_ref[offset + q] = x_ref[q]
+        xt_ref[offset + q] = turned(value).astype(BF)
+
+
+def slot_products(table_ref, g_ref, xs_ref, xt_ref, acc_ref, src_row, dst_row):
+    acc_ref[...] = jnp.zeros_like(acc_ref)
+    for s in range(g_ref.shape[0]):
+        src = table_ref[src_row, s]
+        dst = table_ref[dst_row, s]
+        product = jnp.dot(xs_ref[src], g_ref[s, 0], preferred_element_type=F32)
+        product += jnp.dot(xt_ref[src], g_ref[s, 1], preferred_element_type=F32)
+        acc_ref[dst] += product
+
+
+def start_kernel(table_ref, classes_ref, kinds_ref, back_ref, out_ref, extra_ref):
+    r = table_ref[4, 0]
+    blocks, rows, entries = out_ref.shape
+    groups = rows // 8
+    tail = entries - 2 * LANES
+    kinds = kinds_ref[...]
+    real = jnp.zeros(kinds.shape, F32)
+    imag = jnp.zeros(kinds.shape, F32)
+    for k in range(classes_ref.shape[0]):
+        real = jnp.where(kinds == k, classes_ref[k, 0], real)
+        imag = jnp.where(kinds == k, classes_ref[k, 1], imag)
+    real = jnp.concatenate([real] * 3, axis=1)
+    imag = jnp.concatenate([imag] * 3, axis=1)
+    for q in range(blocks):
+        back = back_ref[q]
+        out_ref[q] = (real[q : q + 1] * back + imag[q : q + 1] * turned(back)).astype(BF)
+        marks = []
+        for value in (real[q : q + 1], imag[q : q + 1]):
+            for _ in range(3):
+                part = value.astype(BF).astype(F32)
+                marks.append(part)
+                value = value - part
+        marks = jnp.concatenate(marks + [jnp.zeros((2, entries), F32)], axis=0)
+        ends = jnp.concatenate([marks[:, 2 * LANES :], jnp.zeros((8, LANES - tail), F32)], axis=1)
+        ends = pltpu.roll(ends, tail, 1)
+        lane = lax.broadcasted_iota(jnp.int32, (8, LANES), 1)
+        for g in range(groups):
+            at = slice(g * 8, g * 8 + 8)
+            pieces = [back[at, :LANES], back[at, LANES : 2 * LANES]]
+            last = jnp.concatenate([back[at, 2 * LANES :], jnp.zeros((8, LANES - tail), F32)], axis=1)
+            value = jnp.where(r == 0, pieces[0], jnp.where(r == 1, pieces[1], last))
+            high = value.astype(BF).astype(F32)
+            low = value - high
+            high = jnp.where((r == 2) & (lane >= tail), ends, high)
+            high = jnp.where(r == 3, marks[:, :LANES], high)
+            low = jnp.where(r == 3, marks[:, LANES : 2 * LANES], low)
+            extra_ref[q * groups + g] = jnp.concatenate([high, low], axis=0).astype(BF)
+
+
+def turn_kernel(g_ref, gt_ref):
+    for s in range(g_ref.shape[0]):
+        for part in range(2):
+            gt_ref[s, part] = g_ref[s, part].T
+
+
+def direct_kernel(first, table_ref, gt_ref, x_ref, own_ref, other_ref, xs_ref, xt_ref, acc_ref):
+    blocks = own_ref.shape[0]
+    if first:
+        copy_in(x_ref, xs_ref, xt_ref, 0)
+    else:
+        for q in range(blocks):
+            unpack_half(x_ref, q, 0, xs_ref, xt_ref, q)
+    slot_products(table_ref, gt_ref, xs_ref, xt_ref, acc_ref, 0, 1)
+    for q in range(blocks):
+        own_ref[q] = acc_ref[q]
+        other_ref[q] = acc_ref[blocks + q]
+
+
+def mirror_kernel(first, table_ref, g_ref, x_ref, x_other_ref, out_ref, xs_ref, xt_ref, acc_ref):
+    blocks = out_ref.shape[0]
+    if first:
+        copy_in(x_ref, xs_ref, xt_ref, 0)
+        copy_in(x_other_ref, xs_ref, xt_ref, blocks)
+    else:
+        for q in range(blocks):
+            unpack_half(x_ref, q, 1, xs_ref, xt_ref, q)
+            unpack_half(x_other_ref, q, 1, xs_ref, xt_ref, blocks + q)
+    slot_products(table_ref, g_ref, xs_ref, xt_ref, acc_ref, 2, 3)
+    for q in range(blocks):
+        out_ref[q] = acc_ref[q]
+
+
+def pack_kernel(mirror_ref, own_ref, got_ref, *rest):
+    msg_ref = rest[-1]
+    base = 0
+    if len(rest) == 2:
+        base = rest[0].shape[1]
+        msg_ref[:, 0:base, :] = rest[0][...]
+    blocks, rows, entries = own_ref.shape
+    groups = rows // 8
+    tail = entries - 2 * LANES
+    for q in range(blocks):
+        at = slice(q * groups, (q + 1) * groups)
+        for piece in range(2):
+            lanes = slice(piece * LANES, (piece + 1) * LANES)
+            direct = (own_ref[q, :, lanes] + got_ref[q, :, lanes]).reshape(groups, 8, LANES)
+            mirror = mirror_ref[q, :, lanes].reshape(groups, 8, LANES)
+            start = base + piece * 16
+            msg_ref[at, start : start + 16, :] = jnp.concatenate([direct, mirror], axis=1).astype(BF)
+        lanes = slice(2 * LANES, entries)
+        direct = own_ref[q, :, lanes] + got_ref[q, :, lanes]
+        mirror = mirror_ref[q, :, lanes]
+        filler = jnp.zeros((rows, LANES - 2 * tail), F32)
+        ends = jnp.concatenate([direct, mirror, filler], axis=1).reshape(groups, 8, LANES)
+        msg_ref[at, base + 32 : base + 40, :] = ends.astype(BF)
+
+
+def update_kernel(first, final, rows, cols, tail, *refs):
+    if first:
+        msg_ref, out_ref, back_ref, contrast_ref = refs
+        base = 16
+    else:
+        msg_ref, back_ref, contrast_ref, out_ref = refs
+        base = 0
+    lane = lax.broadcasted_iota(jnp.int32, (8, LANES), 1)
+    sign = jnp.where(lax.broadcasted_iota(jnp.int32, (8, LANES), 0) < 4, -1.0, 1.0)
+    direct = {}
+    mirror = {}
+
+    def add(store, key, value):
+        store[key] = store[key] + value if key in store else value
+
+    for r in range(rows):
+        for c in range(cols):
+            d = r * cols + c
+            j = 2 * r + c % 2
+            for piece in range(2):
+                both = msg_ref[d, base + piece * 16 : base + piece * 16 + 16, :].astype(F32)
+                add(direct, (j, piece), both[:8])
+                add(mirror, (c, piece), both[8:])
+            ends = msg_ref[d, base + 32 : base + 40, :].astype(F32)
+            add(direct, (j, 2), ends)
+            add(mirror, (c, 2), ends)
+    current = {}
+    for j in range(cols):
+        if first:
+            pairs = [msg_ref[r * cols + j, 0:16, :].astype(F32) for r in range(4)]
+            background = [pair[:8] + pair[8:] for pair in pairs[:3]]
+            marks = [pairs[3][:8], pairs[3][8:], pltpu.roll(pairs[2][:8], LANES - tail, 1)]
+        for piece in range(3):
+            total = direct[j, piece]
+            more = mirror[j, piece]
+            total = total + (pltpu.roll(more, LANES - tail, 1) if piece == 2 else more)
+            if first:
+                back = background[piece]
+                back_ref[j, piece] = back
+                mark = marks[piece]
+                real = jnp.broadcast_to(mark[0:1] + mark[1:2] + mark[2:3], (8, LANES))
+                imag = jnp.broadcast_to(mark[3:4] + mark[4:5] + mark[5:6], (8, LANES)) * sign
+                contrast_ref[j, 0, piece] = real
+                contrast_ref[j, 1, piece] = imag
+            else:
+                back = back_ref[j, piece]
+                real = contrast_ref[j, 0, piece]
+                imag = contrast_ref[j, 1, piece]
+            total = total + back
+            if final:
+                current[j, piece] = total
+            else:
+                current[j, piece] = real * total + imag * pltpu.roll(total, 4, 0)
+    for r in range(rows):
+        for c in range(cols):
+            d = r * cols + c
+            if final:
+                for piece in range(3):
+                    out_ref[d, piece * 8 : piece * 8 + 8, :] = current[c, piece]
+                continue
+            k = 2 * r + c % 2
+            for piece in range(2):
+                out_ref[d, piece * 16 : piece * 16 + 16, :] = jnp.concatenate(
+                    [current[c, piece], current[k, piece]], axis=0
+                ).astype(BF)
+            ends = jnp.where(lane < tail, current[c, 2], pltpu.roll(current[k, 2], tail, 1))
+            out_ref[d, 32:40, :] = ends.astype(BF)
+
+
+def whole_call(kernel, out_shape, smem, operands, scratch, name):
+    spaces = [pltpu.SMEM] * smem + [pltpu.VMEM] * (len(operands) - smem)
+    return pl.pallas_call(
+        kernel,
+        out_shape=out_shape,
+        in_specs=[pl.BlockSpec(memory_space=space) for space in spaces],
+        out_specs=jax.tree.map(lambda _: pl.BlockSpec(memory_space=pltpu.VMEM), out_shape),
+        scratch_shapes=scratch,
+        compiler_params=pltpu.CompilerParams(vmem_limit_bytes=VMEM_BYTES),
+        name=name,
+    )(*operands)
+
+
+def local_owners(green_blocks, slot_rows, slot_cols, slot_count, cell_class, class_contrast, background):
+    r = lax.axis_index("row")
+    c = lax.axis_index("col")
+    rows = lax.axis_size("row")
+    cols = lax.axis_size("col")
+    parity = c % 2
+    green = green_blocks[0, 0]
+    slots, _, entries, _ = green.shape
+    sources, blocks = background.shape[1:3]
+    groups = sources // 4
+    tail = entries - 2 * LANES
+    both = ("row", "col")
+
+    local_rows = slot_rows[0, 0]
+    local_cols = slot_cols[0, 0]
+    living = jnp.arange(slots) < slot_count[0, 0]
+    off_diagonal = (local_rows // 2 * cols + 2 * r + local_rows % 2) != (local_cols * cols + c)
+    place = (local_rows % 2 ^ parity) * blocks + local_rows // 2
+    table = jnp.stack(
+        [
+            local_cols,
+            jnp.where(living, place, 2 * blocks),
+            place,
+            jnp.where(living & off_diagonal, local_cols, blocks),
+            jnp.full_like(local_cols, r),
+        ]
+    ).astype(jnp.int32)
+
+    block = (groups * 8, entries)
+    back = background[:, :, :, 0, :].reshape(2, groups, 4, blocks, entries)
+    back = back.transpose(3, 1, 0, 2, 4).reshape((blocks,) + block)
+    start, extra = whole_call(
+        start_kernel,
+        (
+            jax.ShapeDtypeStruct((blocks,) + block, BF),
+            jax.ShapeDtypeStruct((rows * cols, 16, LANES), BF),
+        ),
+        2,
+        (table, class_contrast, cell_class[:, 0, :], back),
+        [],
+        "start",
+    )
+
+    core_pairs = [(i, i ^ 1) for i in range(cols)]
+    arrived = []
+    for hop in range(1, cols // 2):
+        pairs = [
+            (a * cols + 2 * a + p, a * cols + 2 * ((a + hop) % (cols // 2)) + p)
+            for a in range(rows)
+            for p in range(2)
+        ]
+        arrived.append(lax.ppermute(start, both, pairs))
+    row_mine = jnp.where(c // 2 == r, start, sum(arrived))
+    row_other = lax.ppermute(row_mine, "col", core_pairs)
+
+    green_turned = whole_call(turn_kernel, jax.ShapeDtypeStruct(green.shape, BF), 0, (green,), [], "turn")
+    part = jax.ShapeDtypeStruct((blocks,) + block, F32)
+    message = jax.ShapeDtypeStruct((rows * cols, 40, LANES), BF)
+    for step in range(PRODUCTS):
+        first = step == 0
+        final = step + 1 == PRODUCTS
+        if first:
+            direct_in, mirror_in = start, (row_mine, row_other)
+        else:
+            direct_in, mirror_in = x_msg, (x_msg, lax.ppermute(x_msg, "col", core_pairs))
+        own, other = whole_call(
+            lambda *refs, first=first: direct_kernel(first, *refs),
+            (part, part),
+            1,
+            (table, green_turned, direct_in),
+            [
+                pltpu.VMEM((blocks,) + block, BF),
+                pltpu.VMEM((blocks,) + block, BF),
+                pltpu.VMEM((2 * blocks + 1,) + block, F32),
+            ],
+            f"direct_{step}",
+        )
+        got = lax.ppermute(other, "col", core_pairs)
+        mirror = whole_call(
+            lambda *refs, first=first: mirror_kernel(first, *refs),
+            part,
+            1,
+            (table, green) + mirror_in,
+            [
+                pltpu.VMEM((2 * blocks,) + block, BF),
+                pltpu.VMEM((2 * blocks,) + block, BF),
+                pltpu.VMEM((blocks + 1,) + block, F32),
+            ],
+            f"mirror_{step}",
+        )
+        y_shape = jax.ShapeDtypeStruct((rows * cols, 56, LANES), BF) if first else message
+        operands = (mirror, own, got) + ((extra,) if first else ())
+        y_msg = whole_call(pack_kernel, y_shape, 0, operands, [], f"pack_{step}")
+        y_msg = lax.all_to_all(y_msg, both, 0, 0, tiled=True)
+        run = lambda *refs, first=first, final=final: update_kernel(first, final, rows, cols, tail, *refs)
+        if first:
+            x_msg, owner_back, owner_contrast = whole_call(
+                run,
+                (
+                    message,
+                    jax.ShapeDtypeStruct((cols, 3, 8, LANES), F32),
+                    jax.ShapeDtypeStruct((cols, 2, 3, 8, LANES), F32),
+                ),
+                0,
+                (y_msg,),
+                [],
+                f"update_{step}",
+            )
+        else:
+            x_shape = jax.ShapeDtypeStruct((rows * cols, 24, LANES), F32) if final else message
+            x_msg = whole_call(run, x_shape, 0, (y_msg, owner_back, owner_contrast), [], f"update_{step}")
+        x_msg = lax.all_to_all(x_msg, both, 0, 0, tiled=True)
+    field = x_msg.reshape(blocks, groups, 3, 2, 4, LANES).transpose(3, 1, 4, 0, 2, 5)
+    field = field.reshape(2, sources, blocks, 3 * LANES)[..., :entries]
+    return field[:, :, :, None, :]
 
 
 def solution(mesh):
@@ -105,4 +443,18 @@
         P(None, None, None, "col", None),
     )
     out_specs = P(None, None, None, "col", None)
+    rows, cols = mesh.shape["row"], mesh.shape["col"]
+
+    def local(*args):
+        sources, blocks = args[6].shape[1:3]
+        entries = args[6].shape[4]
+        owners = (
+            rows == blocks == 4
+            and cols == 2 * rows
+            and sources == 4 * cols
+            and 2 * LANES < entries <= 2 * LANES + LANES // 2
+            and args[5].shape[0] <= 256
+        )
+        return (local_owners if owners else local_general)(*args)
+
     return jax.shard_map(local, mesh=mesh, in_specs=in_specs, out_specs=out_specs, check_vma=False)

time: 512 us -> 133 us (0.26)
  waiting for transfers between devices: 428 us -> 1.36 us
  blocking collectives: 0 us -> 90.8 us
  matrix products: 37.7 us -> 0 us
  other arithmetic: 18.1 us -> 1.41 us
  Pallas kernels: 0 us -> 15.9 us
  between operations: 14.3 us -> 0.91 us
  starting transfers between devices: 0.74 us -> 10.1 us
    psum x9 -> x0, waiting for transfers between devices: 427 us -> none  [the longest x6 279 us: from_root(): return lax.psum(jnp.where(mine, array, jnp.zeros_like(array)), axis)]
    all_to_all x0 -> x6, blocking collectives: none -> 90.8 us  [the longest x3 46.5 us: local_owners(): y_msg = lax.all_to_all(y_msg, both, 0, 0, tiled=True)]
    dot_general x13 -> x0, matrix products: 37.7 us -> none  [the longest x3 13.9 us: local(): jnp.einsum('sqoi,pksi->qpkso', green_tiles, direct_in, preferred_element_...]
    pallas_call x0 -> x14, Pallas kernels: none -> 15.9 us  [whole_call(): pl.pallas_call(kernel, out_shape=out_shape, in_specs=[pl.BlockSpec(memory...]
    ppermute x0 -> x9, starting transfers between devices: none -> 10.1 us  [the longest x3 8.41 us: local_owners(): arrived.append(lax.ppermute(start, both, pairs))]
    unnamed x8 -> x18, local copies, waits for them, and re-layouts: 0.67 us -> 9.89 us
    another operation x15 -> x0, other arithmetic: 7.82 us -> none  [the longest x6 7.02 us: local(): jnp.stack(halves, axis=3).reshape(2, sources, row_blocks, entries)]
  transfers between devices with their start and end apart: 9 -> 9, of which waited for: 9 -> 1; matrix products, arithmetic and copies ran while one was open for 8% -> 0% of each run, Pallas kernels for 0% -> 11%
where the time goes in v1:
time: 133 us
  blocking collectives  90.8 us (68%)
  Pallas kernels  15.9 us (12%)
  local copies, waits for them, and re-layouts  12.3 us (9%)
  starting transfers between devices  10.1 us (8%)
  other arithmetic  1.41 us (1%)
  waiting for transfers between devices  1.36 us (1%)
    all_to_all x3, blocking collectives, local_owners(): y_msg = lax.all_to_all(y_msg, both, 0, 0, tiled=True)  46.5 us
    all_to_all x3, blocking collectives, local_owners(): x_msg = lax.all_to_all(x_msg, both, 0, 0, tiled=True)  44.3 us
    pallas_call x14, Pallas kernels, whole_call(): pl.pallas_call(kernel, out_shape=out_shape, in_specs=[pl.BlockSpec(memory...  15.9 us
    unnamed x18, local copies, waits for them, and re-layouts  9.89 us
    ppermute x3, starting transfers between devices, local_owners(): arrived.append(lax.ppermute(start, both, pairs))  8.41 us
  transfers between devices with their start and end apart: 9, of which 1 were waited for; matrix products, arithmetic and copies ran while one was open for 0% of the time, Pallas kernels for 11%

profile of v1, /device:TPU:0, one launch (start us, length us, event | category | flops | bytes accessed | tf_op | source)
XLA Modules:
  0.0 132.8 jit_solution(12326450041802399320)
XLA Ops:
  0.7 0.8 copy.12.classes_ref
  1.4 1.1 copy.15
  2.5 0.1 copy.19
  2.6 0.1 reshape.193.back_ref
  2.8 0.7 and_select_fusion
  3.5 0.7 compare_select_fusion.3
  4.1 0.7 stack.2.table_ref.refs_0_
  4.8 0.7 copy-done.3
  5.5 0.9 start.1
  6.4 5.8 %collective-permute-start.2 = (bf16[4,64,288]{2,1,0:T(8,128)(2,1)S(1)}, bf16[4,64,288]{2,1,0:T(8,128)(2,1)S(1)}, u32[]{:S(2)}, u32[]{:S(2)}) collective-permute-start(bf16[4,64,288]{2,1,0:T(8,128)(2,1)S(1)} %get-tuple-element.16.refs_2_), channel_id=1, source_target_pairs={{0,6},{1,7},{10,8},{11,9},{20,18},{21,19},{30,28},{31,29}} | collective-permute-start | bytes 442376 | tf_op jit(solution)/shard_map/ppermute | solution.py:369
  12.2 1.3 collective-permute-start.1
  13.6 1.3 collective-permute-start
  14.9 0.0 copy-start.1
  14.9 2.5 %copy-done.1 = bf16[1,1,12,2,288,288]{5,4,3,2,1,0:T(8,128)(2,1)S(1)} copy-done((bf16[1,1,12,2,288,288]{5,4,3,2,1,0:T(8,128)(2,1)S(1)}, bf16[1,1,12,2,288,288]{5,4,3,2,1,0:T(8,128)(2,1)}, u32[]{:S(2)}) %copy-start.1) | copy-done | bytes 3981336
  17.4 1.7 %turn.1.refs_1_ = bf16[12,2,288,288]{3,2,1,0:T(8,128)(2,1)S(1)} custom-call(bf16[12,2,288,288]{3,2,1,0:T(8,128)(2,1)S(1)} %bitcast.40), custom_call_target="tpu_custom_call" | custom-call | tf_op jit(solution)/shard_map/turn/pallas_call | solution.py:307
  19.1 2.0 %direct_0.1 = (f32[4,64,288]{2,1,0:T(8,128)S(1)}, f32[4,64,288]{2,1,0:T(8,128)S(1)}) custom-call(s32[5,12]{1,0:T(8,128)S(1)} %stack.2.table_ref.refs_0_, bf16[12,2,288,288]{3,2,1,0:T(8,128)(2,1)S(1)} %turn.1.refs_1_, bf16[4,64,288]{2,1,0:T(8,128)(2,1)S(1)} %get-tuple-element.16.refs_2_), custom_call_target="tpu_custom_call" | custom-call | tf_op jit(solution)/shard_map/direct_0/pallas_call | solution.py:307
  21.2 2.3 %copy-done = bf16[12,2,288,288]{3,2,1,0:T(8,128)(2,1)} copy-done((bf16[12,2,288,288]{3,2,1,0:T(8,128)(2,1)}, bf16[12,2,288,288]{3,2,1,0:T(8,128)(2,1)S(1)}, u32[]{:S(2)}) %copy-start) | copy-done | bytes 3981336
  23.5 0.0 collective-permute-start.4
  23.5 0.0 collective-permute-done.2
  23.5 0.0 collective-permute-done
  23.6 0.6 collective-permute-start.3
  24.2 1.3 %collective-permute-done.3.refs_3_ = bf16[4,64,288]{2,1,0:T(8,128)(2,1)S(1)} collective-permute-done((bf16[4,64,288]{2,1,0:T(8,128)(2,1)S(1)}, bf16[4,64,288]{2,1,0:T(8,128)(2,1)S(1)}, u32[]{:S(2)}, u32[]{:S(2)}) %collective-permute-start.3) | collective-permute-done | bytes 147488 | tf_op jit(solution)/shard_map/ppermute | solution.py:371
  25.5 2.5 %copy-done.2 = bf16[1,1,12,2,288,288]{5,4,3,2,1,0:T(8,128)(2,1)S(1)} copy-done((bf16[1,1,12,2,288,288]{5,4,3,2,1,0:T(8,128)(2,1)S(1)}, bf16[1,1,12,2,288,288]{5,4,3,2,1,0:T(8,128)(2,1)}, u32[]{:S(2)}) %copy-start.2) | copy-done | bytes 3981336
  28.0 2.1 %mirror_0.1.mirror_ref = f32[4,64,288]{2,1,0:T(8,128)S(1)} custom-call(s32[5,12]{1,0:T(8,128)S(1)} %stack.2.table_ref.refs_0_, bf16[12,2,288,288]{3,2,1,0:T(8,128)(2,1)S(1)} %bitcast.41, bf16[4,64,288]{2,1,0:T(8,128)(2,1)S(1)} %add_select_fusion.refs_2_, bf16[4,64,288]{2,1,0:T(8,128)(2,1)S(1)} %collective-permute-done.3.refs_3_), custom_call_target="tpu_custom_call" | custom-call | tf_op jit(solution)/shard_map/mirror_0/pallas_call | solution.py:307
  30.1 0.0 collective-permute-done.4.got_ref
  30.1 0.0 slice-start.3
  30.1 0.1 pack_0.1
  30.2 18.1 %all_to_all.30.refs_0_ = bf16[32,56,128]{2,1,0:T(8,128)(2,1)S(1)} all-to-all(bf16[32,56,128]{2,1,0:T(8,128)(2,1)S(1)} %pack_0.1), channel_id=1, replica_groups=mesh['row'=4,'col'=8] {'row','col'}, dimensions={0} | all-to-all | bytes 917504 | tf_op jit(solution)/shard_map/all_to_all | solution.py:411
  48.3 0.2 update_0.1
  48.6 14.7 %all_to_all.31.refs_2_ = bf16[32,40,128]{2,1,0:T(8,128)(2,1)S(1)} all-to-all(bf16[32,40,128]{2,1,0:T(8,128)(2,1)S(1)} %get-tuple-element.20), channel_id=1, replica_groups=mesh['row'=4,'col'=8] {'row','col'}, dimensions={0} | all-to-all | bytes 655360 | tf_op jit(solution)/shard_map/all_to_all | solution.py:429
  63.2 0.0 collective-permute-start.5
  63.2 2.0 %direct_1.1 = (f32[4,64,288]{2,1,0:T(8,128)S(1)}, f32[4,64,288]{2,1,0:T(8,128)S(1)}) custom-call(s32[5,12]{1,0:T(8,128)S(1)} %stack.2.table_ref.refs_0_, bf16[12,2,288,288]{3,2,1,0:T(8,128)(2,1)S(1)} %bitcast.39, bf16[32,40,128]{2,1,0:T(8,128)(2,1)S(1)} %all_to_all.31.refs_2_), custom_call_target="tpu_custom_call" | custom-call | tf_op jit(solution)/shard_map/direct_1/pallas_call | solution.py:307
  65.3 0.6 collective-permute-start.6
  65.9 2.1 %mirror_1.1.mirror_ref = f32[4,64,288]{2,1,0:T(8,128)S(1)} custom-call(s32[5,12]{1,0:T(8,128)S(1)} %stack.2.table_ref.refs_0_, bf16[12,2,288,288]{3,2,1,0:T(8,128)(2,1)S(1)} %bitcast.44, bf16[32,40,128]{2,1,0:T(8,128)(2,1)S(1)} %all_to_all.31.refs_2_, bf16[32,40,128]{2,1,0:T(8,128)(2,1)S(1)} %collective-permute-done.5.refs_3_), custom_call_target="tpu_custom_call" | custom-call | tf_op jit(solution)/shard_map/mirror_1/pallas_call | solution.py:307
  68.0 0.1 pack_1.1
  68.1 14.2 %all_to_all.32.refs_0_ = bf16[32,40,128]{2,1,0:T(8,128)(2,1)S(1)} all-to-all(bf16[32,40,128]{2,1,0:T(8,128)(2,1)S(1)} %pack_1.1), channel_id=1, replica_groups=mesh['row'=4,'col'=8] {'row','col'}, dimensions={0} | all-to-all | bytes 655360 | tf_op jit(solution)/shard_map/all_to_all | solution.py:411
  82.3 0.2 update_1.1
  82.5 14.2 %all_to_all.33.refs_2_ = bf16[32,40,128]{2,1,0:T(8,128)(2,1)S(1)} all-to-all(bf16[32,40,128]{2,1,0:T(8,128)(2,1)S(1)} %update_1.1), channel_id=1, replica_groups=mesh['row'=4,'col'=8] {'row','col'}, dimensions={0} | all-to-all | bytes 655360 | tf_op jit(solution)/shard_map/all_to_all | solution.py:429
  96.7 2.0 %direct_2.1 = (f32[4,64,288]{2,1,0:T(8,128)S(1)}, f32[4,64,288]{2,1,0:T(8,128)S(1)}) custom-call(s32[5,12]{1,0:T(8,128)S(1)} %stack.2.table_ref.refs_0_, bf16[12,2,288,288]{3,2,1,0:T(8,128)(2,1)S(1)} %bitcast.39, bf16[32,40,128]{2,1,0:T(8,128)(2,1)S(1)} %all_to_all.33.refs_2_), custom_call_target="tpu_custom_call" | custom-call | tf_op jit(solution)/shard_map/direct_2/pallas_call | solution.py:307
  98.8 0.6 collective-permute-start.8
  99.3 2.1 %mirror_2.1.mirror_ref = f32[4,64,288]{2,1,0:T(8,128)S(1)} custom-call(s32[5,12]{1,0:T(8,128)S(1)} %stack.2.table_ref.refs_0_, bf16[12,2,288,288]{3,2,1,0:T(8,128)(2,1)S(1)} %bitcast.45, bf16[32,40,128]{2,1,0:T(8,128)(2,1)S(1)} %all_to_all.33.refs_2_, bf16[32,40,128]{2,1,0:T(8,128)(2,1)S(1)} %collective-permute-done.7.refs_3_), custom_call_target="tpu_custom_call" | custom-call | tf_op jit(solution)/shard_map/mirror_2/pallas_call | solution.py:307
  101.5 0.1 pack_2.1
  101.6 14.2 %all_to_all.34.refs_0_ = bf16[32,40,128]{2,1,0:T(8,128)(2,1)S(1)} all-to-all(bf16[32,40,128]{2,1,0:T(8,128)(2,1)S(1)} %pack_2.1), channel_id=1, replica_groups=mesh['row'=4,'col'=8] {'row','col'}, dimensions={0} | all-to-all | bytes 655360 | tf_op jit(solution)/shard_map/all_to_all | solution.py:411
  115.8 0.1 update_2.1
  115.9 15.4 %all_to_all.35 = f32[32,24,128]{2,1,0:T(8,128)S(1)} all-to-all(f32[32,24,128]{2,1,0:T(8,128)S(1)} %update_2.1), channel_id=1, replica_groups=mesh['row'=4,'col'=8] {'row','col'}, dimensions={0} | all-to-all | bytes 786432 | tf_op jit(solution)/shard_map/all_to_all | solution.py:429
  131.3 0.1 copy.18
  131.4 0.2 reshape.195
  131.7 1.2 copy.14
  (21 shorter events, 0.1 us)
Async XLA Ops:
  4.8 0.7 copy-start.3
  6.4 17.1 %collective-permute-start.2 = (bf16[4,64,288]{2,1,0:T(8,128)(2,1)S(1)}, bf16[4,64,288]{2,1,0:T(8,128)(2,1)S(1)}, u32[]{:S(2)}, u32[]{:S(2)}) collective-permute-start(bf16[4,64,288]{2,1,0:T(8,128)(2,1)S(1)} %get-tuple-element.16.refs_2_), channel_id=1, source_target_pairs={{0,6},{1,7},{10,8},{11,9},{20,18},{21,19},{30,28},{31,29}} | collective-permute-start | bytes 442376 | tf_op jit(solution)/shard_map/ppermute | solution.py:369
  12.2 11.3 %collective-permute-start.1 = (bf16[4,64,288]{2,1,0:T(8,128)(2,1)S(1)}, bf16[4,64,288]{2,1,0:T(8,128)(2,1)S(1)}, u32[]{:S(2)}, u32[]{:S(2)}) collective-permute-start(bf16[4,64,288]{2,1,0:T(8,128)(2,1)S(1)} %get-tuple-element.16.refs_2_), channel_id=1, source_target_pairs={{0,4},{1,5},{10,14},{11,15},{20,16},{21,17},{30,26},{31,27}} | collective-permute-start | bytes 442376 | tf_op jit(solution)/shard_map/ppermute | solution.py:369
  13.6 10.0 %collective-permute-start = (bf16[4,64,288]{2,1,0:T(8,128)(2,1)S(1)}, bf16[4,64,288]{2,1,0:T(8,128)(2,1)S(1)}, u32[]{:S(2)}, u32[]{:S(2)}) collective-permute-start(bf16[4,64,288]{2,1,0:T(8,128)(2,1)S(1)} %get-tuple-element.16.refs_2_), channel_id=1, source_target_pairs={{0,2},{1,3},{10,12},{11,13},{20,22},{21,23},{30,24},{31,25}} | collective-permute-start | bytes 442376 | tf_op jit(solution)/shard_map/ppermute | solution.py:369
  14.9 2.5 %copy-start.1 = (bf16[1,1,12,2,288,288]{5,4,3,2,1,0:T(8,128)(2,1)S(1)}, bf16[1,1,12,2,288,288]{5,4,3,2,1,0:T(8,128)(2,1)}, u32[]{:S(2)}) copy-start(bf16[1,1,12,2,288,288]{5,4,3,2,1,0:T(8,128)(2,1)} %param.7) | copy-start | bytes 11943940
  21.2 2.3 %copy-start = (bf16[12,2,288,288]{3,2,1,0:T(8,128)(2,1)}, bf16[12,2,288,288]{3,2,1,0:T(8,128)(2,1)S(1)}, u32[]{:S(2)}) copy-start(bf16[12,2,288,288]{3,2,1,0:T(8,128)(2,1)S(1)} %turn.1.refs_1_) | copy-start | bytes 11943940
  23.5 6.6 %collective-permute-start.4 = (f32[4,64,288]{2,1,0:T(8,128)S(1)}, f32[4,64,288]{2,1,0:T(8,128)S(1)}, u32[]{:S(2)}, u32[]{:S(2)}) collective-permute-start(f32[4,64,288]{2,1,0:T(8,128)S(1)} %get-tuple-element.18), channel_id=1, source_target_pairs={{0,1},{1,0},{2,3},{3,2},{4,5},{5,4},{6,7},{7,6},{8,9},{9,8},{10,11... | collective-permute-start | bytes 884744 | tf_op jit(solution)/shard_map/ppermute | solution.py:395
  23.5 39.7 %slice-start = ((s8[5308416]{0:T(1024)(128)(4,1)}), s8[4194304]{0:T(1024)(128)(4,1)S(1)}, s32[]{:S(2)}) async-start(s8[5308416]{0:T(1024)(128)(4,1)} %bitcast.38), calls=%async_computation.6 | async-start | bytes 8388608
  23.6 39.7 %slice-start.1 = ((s8[5308416]{0:T(1024)(128)(4,1)}), s8[1114112]{0:T(1024)(128)(4,1)S(1)}, s32[]{:S(2)}) async-start(s8[5308416]{0:T(1024)(128)(4,1)} %bitcast.38), calls=%async_computation.7 | async-start | bytes 2228224
  23.6 1.9 %collective-permute-start.3 = (bf16[4,64,288]{2,1,0:T(8,128)(2,1)S(1)}, bf16[4,64,288]{2,1,0:T(8,128)(2,1)S(1)}, u32[]{:S(2)}, u32[]{:S(2)}) collective-permute-start(bf16[4,64,288]{2,1,0:T(8,128)(2,1)S(1)} %add_select_fusion.refs_2_), channel_id=1, source_target_pairs={{0,1},{1,0},{2,3},{3,2},{4,5},{5,4},{6,7},{7,6},{8,9},{9,8},{10,11... | collective-permute-start | bytes 442376 | tf_op jit(solution)/shard_map/ppermute | solution.py:371
  25.5 2.5 %copy-start.2 = (bf16[1,1,12,2,288,288]{5,4,3,2,1,0:T(8,128)(2,1)S(1)}, bf16[1,1,12,2,288,288]{5,4,3,2,1,0:T(8,128)(2,1)}, u32[]{:S(2)}) copy-start(bf16[1,1,12,2,288,288]{5,4,3,2,1,0:T(8,128)(2,1)} %param.7) | copy-start | bytes 11943940
  28.0 37.8 %slice-start.2 = ((s8[5308416]{0:T(1024)(128)(4,1)}), s8[4194304]{0:T(1024)(128)(4,1)S(1)}, s32[]{:S(2)}) async-start(s8[5308416]{0:T(1024)(128)(4,1)} %bitcast.42), calls=%async_computation.8 | async-start | bytes 8388608
  30.1 35.7 %slice-start.3 = ((s8[5308416]{0:T(1024)(128)(4,1)}), s8[1114112]{0:T(1024)(128)(4,1)S(1)}, s32[]{:S(2)}) async-start(s8[5308416]{0:T(1024)(128)(4,1)} %bitcast.42), calls=%async_computation.9 | async-start | bytes 2228224
  63.2 2.6 %collective-permute-start.5 = (bf16[32,40,128]{2,1,0:T(8,128)(2,1)S(1)}, bf16[32,40,128]{2,1,0:T(8,128)(2,1)S(1)}, u32[]{:S(2)}, u32[]{:S(2)}) collective-permute-start(bf16[32,40,128]{2,1,0:T(8,128)(2,1)S(1)} %all_to_all.31.refs_2_), channel_id=1, source_target_pairs={{0,1},{1,0},{2,3},{3,2},{4,5},{5,4},{6,7},{7,6},{8,9},{9,8},{10,11... | collective-permute-start | bytes 983048 | tf_op jit(solution)/shard_map/ppermute | solution.py:382
  65.3 2.7 %collective-permute-start.6 = (f32[4,64,288]{2,1,0:T(8,128)S(1)}, f32[4,64,288]{2,1,0:T(8,128)S(1)}, u32[]{:S(2)}, u32[]{:S(2)}) collective-permute-start(f32[4,64,288]{2,1,0:T(8,128)S(1)} %get-tuple-element.22), channel_id=1, source_target_pairs={{0,1},{1,0},{2,3},{3,2},{4,5},{5,4},{6,7},{7,6},{8,9},{9,8},{10,11... | collective-permute-start | bytes 884744 | tf_op jit(solution)/shard_map/ppermute | solution.py:395
  96.7 2.6 %collective-permute-start.7 = (bf16[32,40,128]{2,1,0:T(8,128)(2,1)S(1)}, bf16[32,40,128]{2,1,0:T(8,128)(2,1)S(1)}, u32[]{:S(2)}, u32[]{:S(2)}) collective-permute-start(bf16[32,40,128]{2,1,0:T(8,128)(2,1)S(1)} %all_to_all.33.refs_2_), channel_id=1, source_target_pairs={{0,1},{1,0},{2,3},{3,2},{4,5},{5,4},{6,7},{7,6},{8,9},{9,8},{10,11... | collective-permute-start | bytes 983048 | tf_op jit(solution)/shard_map/ppermute | solution.py:382
  98.8 2.7 %collective-permute-start.8 = (f32[4,64,288]{2,1,0:T(8,128)S(1)}, f32[4,64,288]{2,1,0:T(8,128)S(1)}, u32[]{:S(2)}, u32[]{:S(2)}) collective-permute-start(f32[4,64,288]{2,1,0:T(8,128)S(1)} %get-tuple-element.26), channel_id=1, source_target_pairs={{0,1},{1,0},{2,3},{3,2},{4,5},{5,4},{6,7},{7,6},{8,9},{9,8},{10,11... | collective-permute-start | bytes 884744 | tf_op jit(solution)/shard_map/ppermute | solution.py:395

commit v2 on v1

v2 whole, which is shorter than its diff:
```python
import jax
import jax.numpy as jnp
from jax import lax
from jax.experimental import pallas as pl
from jax.experimental.pallas import tpu as pltpu
from jax.sharding import PartitionSpec as P

PRODUCTS = 3
LANES = 128
SMALLEST = 2.0**-100
VMEM_BYTES = 8 * 1024 * 1024
BF = jnp.bfloat16
F32 = jnp.float32


def from_root(array, axis, root):
    mine = lax.axis_index(axis) == root
    return lax.psum(jnp.where(mine, array, jnp.zeros_like(array)), axis)


def complex_scale(field_now, contrast_re, contrast_im):
    real_part = field_now[0]
    imag_part = field_now[1]
    scaled = jnp.stack(
        [
            contrast_re * real_part - contrast_im * imag_part,
            contrast_re * imag_part + contrast_im * real_part,
        ]
    )
    return scaled.astype(BF)


def combine(products):
    return jnp.stack([products[0, 0] - products[1, 1], products[0, 1] + products[1, 0]])


def local_general(green_blocks, slot_rows, slot_cols, slot_count, cell_class, class_contrast, background):
    row_index = lax.axis_index("row")
    col_index = lax.axis_index("col")
    stride = lax.axis_size("col")
    green_tiles = green_blocks[0, 0]
    slot_total = green_tiles.shape[0]
    entries = green_tiles.shape[-1]
    sources = background.shape[1]
    col_blocks = background.shape[2]
    row_blocks = 2 * col_blocks
    local_rows = slot_rows[0, 0]
    local_cols = slot_cols[0, 0]
    global_rows = local_rows // 2 * stride + 2 * row_index + local_rows % 2
    global_cols = local_cols * stride + col_index
    off_diagonal = (global_rows != global_cols).astype(F32)
    living = (jnp.arange(slot_total) < slot_count[0, 0]).astype(F32)
    row_pick = (local_rows[:, None] == jnp.arange(row_blocks)[None, :]).astype(F32) * living[:, None]
    col_pick = (local_cols[:, None] == jnp.arange(col_blocks)[None, :]).astype(F32) * (
        living * off_diagonal
    )[:, None]
    classes = class_contrast.shape[0]
    lookup = (cell_class[:, 0, :, None] == jnp.arange(classes)[None, None, :]).astype(F32)
    values = jnp.einsum("bte,ec->btc", lookup, class_contrast, precision=lax.Precision.HIGHEST)
    contrast_re = jnp.tile(values[:, :, 0], (1, 3))
    contrast_im = jnp.tile(values[:, :, 1], (1, 3))
    start_field = background[:, :, :, 0, :]
    field_now = start_field
    current = complex_scale(field_now, contrast_re, contrast_im)
    for step_index in range(PRODUCTS):
        final_step = step_index + 1 == PRODUCTS
        halves = [from_root(current, "col", 2 * row_index + parity) for parity in range(2)]
        row_current = jnp.stack(halves, axis=3).reshape(2, sources, row_blocks, entries)
        direct_in = jnp.take(current, local_cols, axis=2)
        mirror_in = jnp.take(row_current, local_rows, axis=2)
        direct_terms = combine(
            jnp.einsum("sqoi,pksi->qpkso", green_tiles, direct_in, preferred_element_type=F32)
        )
        mirror_terms = combine(
            jnp.einsum("sqoi,pkso->qpksi", green_tiles, mirror_in, preferred_element_type=F32)
        )
        direct_part = jnp.einsum(
            "pkse,sb->pkbe", direct_terms, row_pick, precision=lax.Precision.HIGHEST
        )
        mirror_part = jnp.einsum(
            "pkse,sb->pkbe", mirror_terms, col_pick, precision=lax.Precision.HIGHEST
        )
        row_total = lax.psum(direct_part, "col")
        owned_part = lax.dynamic_index_in_dim(
            row_total.reshape(2, sources, col_blocks, 2, entries),
            col_index % 2,
            axis=3,
            keepdims=False,
        )
        direct_here = from_root(owned_part, "row", col_index // 2)
        column_total = lax.psum(mirror_part, "row")
        field_now = start_field + column_total + direct_here
        if not final_step:
            current = complex_scale(field_now, contrast_re, contrast_im)
    return field_now[:, :, :, None, :]


def turned(value):
    shape = value.shape
    tiles = value.reshape(shape[0] // 8, 8, shape[1])
    return jnp.concatenate([-tiles[:, 4:], tiles[:, :4]], axis=1).reshape(shape)


def put_block(xs_ref, at, value):
    entries = value.shape[1]
    xs_ref[at, :, :entries] = value.astype(BF)
    xs_ref[at, :, entries:] = turned(value).astype(BF)


def unpack_half(msg_ref, q, half, xs_ref, at):
    groups = xs_ref.shape[1] // 8
    tail = xs_ref.shape[2] // 2 - 2 * LANES
    pieces = []
    for piece in range(2):
        both = msg_ref[q * groups : (q + 1) * groups, piece * 16 : piece * 16 + 16, :].astype(F32)
        pieces.append(both[:, half * 8 : half * 8 + 8, :].reshape(groups * 8, LANES))
    ends = msg_ref[q * groups : (q + 1) * groups, 32:40, :].astype(F32).reshape(groups * 8, LANES)
    if half:
        ends = pltpu.roll(ends, LANES - tail, 1)
    put_block(xs_ref, at, jnp.concatenate(pieces + [ends[:, :tail]], axis=1))


def copy_in(x_ref, xs_ref, offset):
    for q in range(x_ref.shape[0]):
        put_block(xs_ref, offset + q, x_ref[q].astype(F32))


def slot_products(table_ref, g_ref, xs_ref, acc_ref, mirror, cols):
    acc_ref[...] = jnp.zeros_like(acc_ref)
    slots, _, depth, entries = g_ref.shape
    r = table_ref[3, 0]
    c = table_ref[4, 0]
    blocks = (acc_ref.shape[0] - 1) // (1 if mirror else 2)
    for s in range(slots):
        local_row = table_ref[0, s]
        local_col = table_ref[1, s]
        living = s < table_ref[2, 0]
        half = local_row // 2
        place = (local_row % 2 ^ c % 2) * blocks + half
        if mirror:
            off_diagonal = half * cols + 2 * r + local_row % 2 != local_col * cols + c
            both = g_ref[s].reshape(2 * depth, entries)
            value = jnp.dot(xs_ref[place], both, preferred_element_type=F32)
            acc_ref[jnp.where(living & off_diagonal, local_col, blocks)] += value
        else:
            over = (((1,), (1,)), ((), ()))
            left = xs_ref[local_col, :, :entries]
            value = lax.dot_general(left, g_ref[s, 0], over, preferred_element_type=F32)
            left = xs_ref[local_col, :, entries:]
            value += lax.dot_general(left, g_ref[s, 1], over, preferred_element_type=F32)
            acc_ref[jnp.where(living, place, 2 * blocks)] += value


def start_kernel(classes, small_ref, back_ref, out_ref, contrast_ref):
    blocks = out_ref.shape[0]
    cells = contrast_ref.shape[2]
    kinds = small_ref[0:blocks, :cells]
    tables = small_ref[blocks : blocks + 2, :]
    contrast = []
    for part in range(2):
        value = jnp.zeros(kinds.shape, F32)
        for k in range(classes):
            value = jnp.where(kinds == float(k), tables[part : part + 1, k : k + 1], value)
        contrast_ref[part] = value
        contrast.append(jnp.concatenate([value] * 3, axis=1))
    real, imag = contrast
    for q in range(blocks):
        back = back_ref[q]
        out_ref[q] = (real[q : q + 1] * back + imag[q : q + 1] * turned(back)).astype(BF)


def share_kernel(table_ref, contrast_ref, back_ref, extra_ref):
    r = table_ref[3, 0]
    blocks, rows, entries = back_ref.shape
    half = LANES // 2
    cells = contrast_ref.shape[2]
    lane = lax.broadcasted_iota(jnp.int32, (8, LANES), 1)
    for q in range(blocks):
        marks = []
        for part in range(2):
            value = contrast_ref[part, q : q + 1]
            for _ in range(3):
                piece = value.astype(BF).astype(F32)
                marks.append(piece)
                value = value - piece
        marks = jnp.concatenate(marks + [jnp.zeros((2, cells), F32)], axis=0)
        marks = jnp.concatenate([marks, jnp.zeros((8, LANES - cells), F32)], axis=1)
        marks = jnp.where(r == 1, pltpu.roll(marks, half, 1), marks)
        for g in range(rows // 8):
            at = slice(g * 8, g * 8 + 8)
            value = jnp.where(r % 2 == 0, back_ref[q, at, :LANES], back_ref[q, at, LANES : 2 * LANES])
            high = value.astype(BF).astype(F32)
            value = jnp.where(r < 2, high, value - high)
            last = back_ref[q, at, 2 * LANES :]
            high = last.astype(BF).astype(F32)
            ends = jnp.concatenate([jnp.zeros((8, half), F32), high, last - high], axis=1)
            beside = jnp.where(r == 0, ends, jnp.where(r == 3, jnp.zeros_like(ends), marks))
            beside = jnp.where(lane < half, 0.0, beside)
            extra_ref[q * rows // 8 + g] = jnp.concatenate([beside, value], axis=0).astype(BF)


def direct_kernel(first, table_ref, g_ref, x_ref, own_ref, other_ref, xs_ref, acc_ref):
    blocks = own_ref.shape[0]
    if first:
        copy_in(x_ref, xs_ref, 0)
    else:
        for q in range(blocks):
            unpack_half(x_ref, q, 0, xs_ref, q)
    slot_products(table_ref, g_ref, xs_ref, acc_ref, False, 0)
    for q in range(blocks):
        own_ref[q] = acc_ref[q]
        other_ref[q] = acc_ref[blocks + q]


def mirror_kernel(first, cols, table_ref, g_ref, x_ref, x_other_ref, out_ref, xs_ref, acc_ref):
    blocks = out_ref.shape[0]
    if first:
        copy_in(x_ref, xs_ref, 0)
        copy_in(x_other_ref, xs_ref, blocks)
    else:
        for q in range(blocks):
            unpack_half(x_ref, q, 1, xs_ref, q)
            unpack_half(x_other_ref, q, 1, xs_ref, blocks + q)
    slot_products(table_ref, g_ref, xs_ref, acc_ref, True, cols)
    for q in range(blocks):
        out_ref[q] = acc_ref[q]


def pack_kernel(mirror_ref, own_ref, got_ref, *rest):
    msg_ref = rest[-1]
    blocks, rows, entries = own_ref.shape
    groups = rows // 8
    tail = entries - 2 * LANES
    for q in range(blocks):
        at = slice(q * groups, (q + 1) * groups)
        for piece in range(2):
            lanes = slice(piece * LANES, (piece + 1) * LANES)
            direct = (own_ref[q, :, lanes] + got_ref[q, :, lanes]).reshape(groups, 8, LANES)
            mirror = mirror_ref[q, :, lanes].reshape(groups, 8, LANES)
            start = piece * 16
            msg_ref[at, start : start + 16, :] = jnp.concatenate([direct, mirror], axis=1).astype(BF)
        lanes = slice(2 * LANES, entries)
        direct = own_ref[q, :, lanes] + got_ref[q, :, lanes]
        mirror = mirror_ref[q, :, lanes]
        filler = jnp.zeros((rows, LANES - 2 * tail), F32)
        ends = jnp.concatenate([direct, mirror, filler], axis=1).reshape(groups, 8, LANES)
        if len(rest) == 2:
            extra = rest[0][at].astype(F32)
            ends = jnp.concatenate([ends + extra[:, :8], extra[:, 8:]], axis=1)
        msg_ref[at, 32 : 32 + ends.shape[1], :] = ends.astype(BF)


def update_kernel(first, rows, cols, tail, msg_ref, *refs):
    back_ref, contrast_ref, out_ref = refs[1:] + refs[:1] if first else refs
    lane = lax.broadcasted_iota(jnp.int32, (8, LANES), 1)
    sign = jnp.where(lax.broadcasted_iota(jnp.int32, (8, LANES), 0) < 4, -1.0, 1.0)
    sums, ends = partial_sums(msg_ref, rows, cols, tail)
    half = LANES // 2
    cells = (2 * LANES + tail) // 3
    current = {}
    for j in range(cols):
        if first:
            parts = [msg_ref[r * cols + j, 40:48, :].astype(F32) for r in range(4)]
            beside = [ends[r * cols + j] for r in range(3)]
            last = pltpu.roll(beside[0], half, 1) + pltpu.roll(beside[0], half - tail, 1)
            background = [parts[0] + parts[2], parts[1] + parts[3], last]
            marks = jnp.where(lane < half, pltpu.roll(beside[1], half, 1), beside[2])
            contrast = []
            for start in (0, 3):
                value = marks[start : start + 1] + marks[start + 1 : start + 2] + marks[start + 2 : start + 3]
                value = jnp.broadcast_to(value, (8, LANES))
                contrast.append(
                    [
                        jnp.where(lane < cells, value, pltpu.roll(value, cells, 1)),
                        jnp.where(lane < half, pltpu.roll(value, cells, 1), pltpu.roll(value, half, 1)),
                        pltpu.roll(value, half, 1),
                    ]
                )
        for piece in range(3):
            if first:
                back, real, imag = background[piece], contrast[0][piece], contrast[1][piece] * sign
                back_ref[j, piece] = back
                contrast_ref[j, 0, piece] = real
                contrast_ref[j, 1, piece] = imag
            else:
                back, real, imag = back_ref[j, piece], contrast_ref[j, 0, piece], contrast_ref[j, 1, piece]
            total = sums[j, piece] + back
            current[j, piece] = real * total + imag * pltpu.roll(total, 4, 0)
    for r in range(rows):
        for c in range(cols):
            d = r * cols + c
            k = 2 * r + c % 2
            for piece in range(2):
                out_ref[d, piece * 16 : piece * 16 + 16, :] = jnp.concatenate(
                    [current[c, piece], current[k, piece]], axis=0
                ).astype(BF)
            ends = jnp.where(lane < tail, current[c, 2], pltpu.roll(current[k, 2], tail, 1))
            out_ref[d, 32:40, :] = ends.astype(BF)


def partial_sums(msg_ref, rows, cols, tail):
    direct = {}
    mirror = {}
    tails = []

    def add(store, key, value):
        store[key] = store[key] + value if key in store else value

    for r in range(rows):
        for c in range(cols):
            d = r * cols + c
            j = 2 * r + c % 2
            for piece in range(2):
                both = msg_ref[d, piece * 16 : piece * 16 + 16, :].astype(F32)
                add(direct, (j, piece), both[:8])
                add(mirror, (c, piece), both[8:])
            ends = msg_ref[d, 32:40, :].astype(F32)
            tails.append(ends)
            add(direct, (j, 2), ends)
            add(mirror, (c, 2), ends)
    for j in range(cols):
        mirror[j, 2] = pltpu.roll(mirror[j, 2], LANES - tail, 1)
    return {key: direct[key] + mirror[key] for key in direct}, tails


def last_kernel(rows, cols, tail, msg_ref, out_ref):
    lane = lax.broadcasted_iota(jnp.int32, (8, LANES), 1)
    sums, _ = partial_sums(msg_ref, rows, cols, tail)
    for j in range(cols):
        pieces = [sums[j, 0], sums[j, 1], jnp.where(lane < tail, sums[j, 2], 0.0)]
        most = jnp.maximum(jnp.maximum(jnp.abs(pieces[0]), jnp.abs(pieces[1])), jnp.abs(pieces[2]))
        most = jnp.max(most, axis=1, keepdims=True)
        power = jnp.floor(jnp.log2(jnp.maximum(most, SMALLEST)))
        scale = jnp.exp2(14.0 - power)
        coded = [jnp.clip(jnp.round(piece * scale), -32767.0, 32767.0) for piece in pieces]
        coded[2] = jnp.where(lane == tail, power, coded[2])
        coded = [piece.astype(jnp.int32) for piece in coded]
        main = jnp.concatenate(coded[:2], axis=0).astype(jnp.int16)
        last = coded[2].astype(jnp.int16)
        for r in range(rows):
            out_ref[r * cols + j, 0:16, :] = main
            out_ref[r * cols + j, 16:24, :] = last


def finish_kernel(msg_ref, back_ref, out_ref):
    blocks, rows, entries = out_ref.shape
    groups = rows // 8
    tail = entries - 2 * LANES
    for q in range(blocks):
        at = slice(q * groups, (q + 1) * groups)
        main = msg_ref[at, 0:16, :].astype(jnp.int32).astype(F32)
        last = msg_ref[at, 16:24, :].astype(jnp.int32).astype(F32).reshape(rows, LANES)
        scale = jnp.exp2(last[:, tail : tail + 1] - 14.0)
        for piece in range(2):
            lanes = slice(piece * LANES, (piece + 1) * LANES)
            value = main[:, piece * 8 : piece * 8 + 8, :].reshape(rows, LANES)
            out_ref[q, :, lanes] = back_ref[q, :, lanes] + value * scale
        lanes = slice(2 * LANES, entries)
        out_ref[q, :, lanes] = back_ref[q, :, lanes] + last[:, :tail] * scale


def whole_call(kernel, out_shape, spaces, operands, scratch, name):
    spaces = list(spaces) + [pltpu.VMEM] * (len(operands) - len(spaces))
    return pl.pallas_call(
        kernel,
        out_shape=out_shape,
        in_specs=[pl.BlockSpec(memory_space=space) for space in spaces],
        out_specs=jax.tree.map(lambda _: pl.BlockSpec(memory_space=pltpu.VMEM), out_shape),
        scratch_shapes=scratch,
        compiler_params=pltpu.CompilerParams(vmem_limit_bytes=VMEM_BYTES),
        name=name,
    )(*operands)


def stacked(arrays, dtype):
    rows = sum(array.shape[0] for array in arrays)
    total = 0
    at = 0
    for array in arrays:
        height, width = array.shape
        total += lax.pad(
            array,
            jnp.zeros((), array.dtype),
            ((at, rows - at - height, 0), (0, LANES - width, 0)),
        ).astype(dtype)
        at += height
    return total


def local_owners(green_blocks, slot_rows, slot_cols, slot_count, cell_class, class_contrast, background):
    r = lax.axis_index("row")
    c = lax.axis_index("col")
    rows = lax.axis_size("row")
    cols = lax.axis_size("col")
    green = green_blocks[0, 0]
    slots, _, entries, _ = green.shape
    sources, blocks = background.shape[1:3]
    groups = sources // 4
    tail = entries - 2 * LANES
    both = ("row", "col")

    floats = stacked([cell_class[:, 0, :], class_contrast.T], F32)
    here = jnp.stack([r, c]).astype(jnp.int32)[:, None]
    table = stacked([slot_rows[0], slot_cols[0], slot_count, here], jnp.int32)

    block = (groups * 8, entries)
    back = background[:, :, :, 0, :].reshape(2, groups, 4, blocks, entries)
    back = back.transpose(3, 1, 0, 2, 4).reshape((blocks,) + block)
    start, contrast = whole_call(
        lambda *refs: start_kernel(class_contrast.shape[0], *refs),
        (
            jax.ShapeDtypeStruct((blocks,) + block, BF),
            jax.ShapeDtypeStruct((2, blocks, entries // 3), F32),
        ),
        [],
        (floats, back),
        [],
        "start",
    )

    core_pairs = [(i, i ^ 1) for i in range(cols)]
    arrived = []
    for hop in range(1, cols // 2):
        pairs = [
            (a * cols + 2 * a + p, a * cols + 2 * ((a + hop) % (cols // 2)) + p)
            for a in range(rows)
            for p in range(2)
        ]
        arrived.append(lax.ppermute(start, both, pairs))
    row_mine = jnp.where(c // 2 == r, start, sum(arrived))
    row_other = lax.ppermute(row_mine, "col", core_pairs)

    extra = whole_call(
        share_kernel,
        jax.ShapeDtypeStruct((rows * cols, 16, LANES), BF),
        [pltpu.SMEM],
        (table, contrast, back),
        [],
        "share",
    )
    part = jax.ShapeDtypeStruct((blocks,) + block, F32)
    message = jax.ShapeDtypeStruct((rows * cols, 40, LANES), BF)
    for step in range(PRODUCTS):
        first = step == 0
        final = step + 1 == PRODUCTS
        if first:
            direct_in, mirror_in = start, (row_mine, row_other)
        else:
            direct_in, mirror_in = x_msg, (x_msg, lax.ppermute(x_msg, "col", core_pairs))
        own, other = whole_call(
            lambda *refs, first=first: direct_kernel(first, *refs),
            (part, part),
            [pltpu.SMEM],
            (table, green, direct_in),
            [
                pltpu.VMEM((blocks, groups * 8, 2 * entries), BF),
                pltpu.VMEM((2 * blocks + 1,) + block, F32),
            ],
            f"direct_{step}",
        )
        got = lax.ppermute(other, "col", core_pairs)
        mirror = whole_call(
            lambda *refs, first=first: mirror_kernel(first, cols, *refs),
            part,
            [pltpu.SMEM],
            (table, green) + mirror_in,
            [
                pltpu.VMEM((2 * blocks, groups * 8, 2 * entries), BF),
                pltpu.VMEM((blocks + 1,) + block, F32),
            ],
            f"mirror_{step}",
        )
        y_shape = jax.ShapeDtypeStruct((rows * cols, 48, LANES), BF) if first else message
        operands = (mirror, own, got) + ((extra,) if first else ())
        y_msg = whole_call(pack_kernel, y_shape, [], operands, [], f"pack_{step}")
        y_msg = lax.all_to_all(y_msg, both, 0, 0, tiled=True)
        run = lambda *refs, first=first: update_kernel(first, rows, cols, tail, *refs)
        if first:
            x_msg, owner_back, owner_contrast = whole_call(
                run,
                (
                    message,
                    jax.ShapeDtypeStruct((cols, 3, 8, LANES), F32),
                    jax.ShapeDtypeStruct((cols, 2, 3, 8, LANES), F32),
                ),
                [],
                (y_msg,),
                [],
                f"update_{step}",
            )
        elif not final:
            operands = (y_msg, owner_back, owner_contrast)
            x_msg = whole_call(run, message, [], operands, [], f"update_{step}")
        else:
            run = lambda *refs: last_kernel(rows, cols, tail, *refs)
            x_shape = jax.ShapeDtypeStruct((rows * cols, 24, LANES), jnp.int16)
            x_msg = whole_call(run, x_shape, [], (y_msg,), [], "last")
        x_msg = lax.all_to_all(x_msg, both, 0, 0, tiled=True)
    field = whole_call(finish_kernel, part, [], (x_msg, back), [], "finish")
    field = field.reshape(blocks, groups, 2, 4, entries).transpose(2, 1, 3, 0, 4)
    return field.reshape(2, sources, blocks, 1, entries)


def solution(mesh):
    in_specs = (
        P("row", "col", None, None, None, None),
        P("row", "col", None),
        P("row", "col", None),
        P("row", "col"),
        P(None, "col", None),
        P(),
        P(None, None, None, "col", None),
    )
    out_specs = P(None, None, None, "col", None)
    rows, cols = mesh.shape["row"], mesh.shape["col"]

    def local(*args):
        sources, blocks = args[6].shape[1:3]
        entries = args[6].shape[4]
        owners = (
            rows == blocks == 4
            and cols == 2 * rows
            and sources == 4 * cols
            and max(args[5].shape[0], args[1].shape[2]) <= LANES
            and entries == 2 * LANES + LANES // 4 == 3 * args[4].shape[2]
        )
        return (local_owners if owners else local_general)(*args)

    return jax.shard_map(local, mesh=mesh, in_specs=in_specs, out_specs=out_specs, check_vma=False)
```

time: 133 us -> 123 us (0.925)
  blocking collectives: 90.8 us -> 85.1 us
  local copies, waits for them, and re-layouts: 12.3 us -> 8.01 us
    all_to_all x3, blocking collectives: 44.3 us -> 39.8 us  [local_owners(): x_msg = lax.all_to_all(x_msg, both, 0, 0, tiled=True)]
    unnamed x18 -> x7, local copies, waits for them, and re-layouts: 9.89 us -> 6.11 us
    add x0 -> x2, other arithmetic: none -> 1.39 us  [stacked(): total += lax.pad(array, jnp.zeros((), array.dtype), ((at, rows - at - hei...]
    select_n x2 -> x0, other arithmetic: 1.36 us -> none  [the longest x1 0.69 us: local_owners(): jnp.where(living & off_diagonal, local_cols, blocks)]
    pallas_call x14 -> x15, Pallas kernels: 15.9 us -> 16 us  [whole_call(): pl.pallas_call(kernel, out_shape=out_shape, in_specs=[pl.BlockSpec(memory...]
  transfers between devices with their start and end apart: 9 -> 9, of which waited for: 1 -> 1; matrix products, arithmetic and copies ran while one was open for 0% -> 1% of each run, Pallas kernels for 11% -> 12%
where the time goes in v2:
time: 123 us; the launch traced here: 122 us
  blocking collectives  85.1 us (69%)
  Pallas kernels  16 us (13%)
  starting transfers between devices  10.2 us (8%)
  local copies, waits for them, and re-layouts  8.01 us (7%)
  other arithmetic  1.52 us (1%)
    all_to_all x3, blocking collectives, local_owners(): y_msg = lax.all_to_all(y_msg, both, 0, 0, tiled=True)  45.3 us
    all_to_all x3, blocking collectives, local_owners(): x_msg = lax.all_to_all(x_msg, both, 0, 0, tiled=True)  39.8 us
    pallas_call x15, Pallas kernels, whole_call(): pl.pallas_call(kernel, out_shape=out_shape, in_specs=[pl.BlockSpec(memory...  16 us
    ppermute x3, starting transfers between devices, local_owners(): arrived.append(lax.ppermute(start, both, pairs))  8.41 us
    unnamed x7, local copies, waits for them, and re-layouts  6.11 us
  transfers between devices with their start and end apart: 9, of which 1 were waited for; matrix products, arithmetic and copies ran while one was open for 1% of the time, Pallas kernels for 12%

profile of v2, /device:TPU:0, one launch (start us, length us, event | category | flops | bytes accessed | tf_op | source)
XLA Modules:
  0.0 122.4 jit_solution(9904037768493622905)
XLA Ops:
  0.0 1.1 copy.11
  1.1 0.1 copy.13
  1.2 0.1 reshape.9.refs_1_.back_ref
  1.4 0.7 pad_add_fusion.refs_0_
  2.1 0.3 start.1
  2.3 5.8 %collective-permute-start.2 = (bf16[4,64,288]{2,1,0:T(8,128)(2,1)S(1)}, bf16[4,64,288]{2,1,0:T(8,128)(2,1)S(1)}, u32[]{:S(2)}, u32[]{:S(2)}) collective-permute-start(bf16[4,64,288]{2,1,0:T(8,128)(2,1)S(1)} %get-tuple-element.16.refs_2_), channel_id=1, source_target_pairs={{0,6},{1,7},{10,8},{11,9},{20,18},{21,19},{30,28},{31,29}} | collective-permute-start | bytes 442376 | tf_op jit(solution)/shard_map/ppermute | solution.py:429
  8.2 1.3 %collective-permute-start.1 = (bf16[4,64,288]{2,1,0:T(8,128)(2,1)S(1)}, bf16[4,64,288]{2,1,0:T(8,128)(2,1)S(1)}, u32[]{:S(2)}, u32[]{:S(2)}) collective-permute-start(bf16[4,64,288]{2,1,0:T(8,128)(2,1)S(1)} %get-tuple-element.16.refs_2_), channel_id=1, source_target_pairs={{0,4},{1,5},{10,14},{11,15},{20,16},{21,17},{30,26},{31,27}} | collective-permute-start | bytes 442376 | tf_op jit(solution)/shard_map/ppermute | solution.py:429
  9.5 1.3 %collective-permute-start = (bf16[4,64,288]{2,1,0:T(8,128)(2,1)S(1)}, bf16[4,64,288]{2,1,0:T(8,128)(2,1)S(1)}, u32[]{:S(2)}, u32[]{:S(2)}) collective-permute-start(bf16[4,64,288]{2,1,0:T(8,128)(2,1)S(1)} %get-tuple-element.16.refs_2_), channel_id=1, source_target_pairs={{0,2},{1,3},{10,12},{11,13},{20,22},{21,23},{30,24},{31,25}} | collective-permute-start | bytes 442376 | tf_op jit(solution)/shard_map/ppermute | solution.py:429
  10.8 0.1 add_bitcast_fusion
  11.5 0.1 copy.8
  11.6 0.7 pad_add_fusion.1.refs_0_.table_ref
  12.3 2.5 %copy-done = bf16[1,1,12,2,288,288]{5,4,3,2,1,0:T(8,128)(2,1)S(1)} copy-done((bf16[1,1,12,2,288,288]{5,4,3,2,1,0:T(8,128)(2,1)S(1)}, bf16[1,1,12,2,288,288]{5,4,3,2,1,0:T(8,128)(2,1)}, u32[]{:S(2)}) %copy-start) | copy-done | bytes 3981336
  14.8 2.8 %direct_0.1 = (f32[4,64,288]{2,1,0:T(8,128)S(1)}, f32[4,64,288]{2,1,0:T(8,128)S(1)}) custom-call(s32[5,128]{1,0:T(8,128)S(1)} %pad_add_fusion.1.refs_0_.table_ref, bf16[12,2,288,288]{3,2,1,0:T(8,128)(2,1)S(1)} %bitcast.14, bf16[4,64,288]{2,1,0:T(8,128)(2,1)S(1)} %get-tuple-element.16.refs_2_), custom_call_target="tpu_custom_call" | custom-call | tf_op jit(solution)/shard_map/direct_0/pallas_call | solution.py:364
  17.6 0.1 collective-permute-start.4
  17.6 0.0 collective-permute-done.2
  17.7 0.0 collective-permute-done.1
  17.7 0.1 add_select_fusion.refs_2_
  17.7 0.5 collective-permute-start.3
  18.3 0.7 share.1.rest_0_
  19.0 0.6 collective-permute-done.3.refs_3_
  19.6 2.5 %copy-done.1 = bf16[1,1,12,2,288,288]{5,4,3,2,1,0:T(8,128)(2,1)S(1)} copy-done((bf16[1,1,12,2,288,288]{5,4,3,2,1,0:T(8,128)(2,1)S(1)}, bf16[1,1,12,2,288,288]{5,4,3,2,1,0:T(8,128)(2,1)}, u32[]{:S(2)}) %copy-start.1) | copy-done | bytes 3981336
  22.1 1.9 %mirror_0.1.mirror_ref = f32[4,64,288]{2,1,0:T(8,128)S(1)} custom-call(s32[5,128]{1,0:T(8,128)S(1)} %pad_add_fusion.1.refs_0_.table_ref, bf16[12,2,288,288]{3,2,1,0:T(8,128)(2,1)S(1)} %bitcast.15, bf16[4,64,288]{2,1,0:T(8,128)(2,1)S(1)} %add_select_fusion.refs_2_, bf16[4,64,288]{2,1,0:T(8,128)(2,1)S(1)} %collective-permute-done.3.refs_3_), custom_call_target="tpu_custom_call" | custom-call | tf_op jit(solution)/shard_map/mirror_0/pallas_call | solution.py:364
  24.0 0.0 collective-permute-done.4.got_ref
  24.0 0.1 pack_0.1
  24.2 16.9 %all_to_all.30.refs_0_ = bf16[32,48,128]{2,1,0:T(8,128)(2,1)S(1)} all-to-all(bf16[32,48,128]{2,1,0:T(8,128)(2,1)S(1)} %pack_0.1), channel_id=1, replica_groups=mesh['row'=4,'col'=8] {'row','col'}, dimensions={0} | all-to-all | bytes 786432 | tf_op jit(solution)/shard_map/all_to_all | solution.py:476
  41.1 0.2 update_0.1
  41.3 14.4 %all_to_all.31.refs_2_ = bf16[32,40,128]{2,1,0:T(8,128)(2,1)S(1)} all-to-all(bf16[32,40,128]{2,1,0:T(8,128)(2,1)S(1)} %get-tuple-element.20), channel_id=1, replica_groups=mesh['row'=4,'col'=8] {'row','col'}, dimensions={0} | all-to-all | bytes 655360 | tf_op jit(solution)/shard_map/all_to_all | solution.py:498
  55.8 2.8 %direct_1.1 = (f32[4,64,288]{2,1,0:T(8,128)S(1)}, f32[4,64,288]{2,1,0:T(8,128)S(1)}) custom-call(s32[5,128]{1,0:T(8,128)S(1)} %pad_add_fusion.1.refs_0_.table_ref, bf16[12,2,288,288]{3,2,1,0:T(8,128)(2,1)S(1)} %bitcast.16, bf16[32,40,128]{2,1,0:T(8,128)(2,1)S(1)} %all_to_all.31.refs_2_), custom_call_target="tpu_custom_call" | custom-call | tf_op jit(solution)/shard_map/direct_1/pallas_call | solution.py:364
  58.5 0.6 collective-permute-start.6
  59.1 0.0 collective-permute-done.5.refs_3_
  59.1 1.9 %mirror_1.1.mirror_ref = f32[4,64,288]{2,1,0:T(8,128)S(1)} custom-call(s32[5,128]{1,0:T(8,128)S(1)} %pad_add_fusion.1.refs_0_.table_ref, bf16[12,2,288,288]{3,2,1,0:T(8,128)(2,1)S(1)} %bitcast.17, bf16[32,40,128]{2,1,0:T(8,128)(2,1)S(1)} %all_to_all.31.refs_2_, bf16[32,40,128]{2,1,0:T(8,128)(2,1)S(1)} %collective-permute-done.5.refs_3_), custom_call_target="tpu_custom_call" | custom-call | tf_op jit(solution)/shard_map/mirror_1/pallas_call | solution.py:364
  61.1 0.0 collective-permute-done.6.got_ref
  61.1 0.1 pack_1.1
  61.2 14.2 %all_to_all.32.refs_0_ = bf16[32,40,128]{2,1,0:T(8,128)(2,1)S(1)} all-to-all(bf16[32,40,128]{2,1,0:T(8,128)(2,1)S(1)} %pack_1.1), channel_id=1, replica_groups=mesh['row'=4,'col'=8] {'row','col'}, dimensions={0} | all-to-all | bytes 655360 | tf_op jit(solution)/shard_map/all_to_all | solution.py:476
  75.4 0.2 update_1.1
  75.5 14.2 %all_to_all.33.refs_2_ = bf16[32,40,128]{2,1,0:T(8,128)(2,1)S(1)} all-to-all(bf16[32,40,128]{2,1,0:T(8,128)(2,1)S(1)} %update_1.1), channel_id=1, replica_groups=mesh['row'=4,'col'=8] {'row','col'}, dimensions={0} | all-to-all | bytes 655360 | tf_op jit(solution)/shard_map/all_to_all | solution.py:498
  89.8 2.8 %direct_2.1 = (f32[4,64,288]{2,1,0:T(8,128)S(1)}, f32[4,64,288]{2,1,0:T(8,128)S(1)}) custom-call(s32[5,128]{1,0:T(8,128)S(1)} %pad_add_fusion.1.refs_0_.table_ref, bf16[12,2,288,288]{3,2,1,0:T(8,128)(2,1)S(1)} %bitcast.18, bf16[32,40,128]{2,1,0:T(8,128)(2,1)S(1)} %all_to_all.33.refs_2_), custom_call_target="tpu_custom_call" | custom-call | tf_op jit(solution)/shard_map/direct_2/pallas_call | solution.py:364
  92.5 0.6 collective-permute-start.8
  93.1 0.0 collective-permute-done.7.refs_3_
  93.1 1.9 %mirror_2.1.mirror_ref = f32[4,64,288]{2,1,0:T(8,128)S(1)} custom-call(s32[5,128]{1,0:T(8,128)S(1)} %pad_add_fusion.1.refs_0_.table_ref, bf16[12,2,288,288]{3,2,1,0:T(8,128)(2,1)S(1)} %bitcast.19, bf16[32,40,128]{2,1,0:T(8,128)(2,1)S(1)} %all_to_all.33.refs_2_, bf16[32,40,128]{2,1,0:T(8,128)(2,1)S(1)} %collective-permute-done.7.refs_3_), custom_call_target="tpu_custom_call" | custom-call | tf_op jit(solution)/shard_map/mirror_2/pallas_call | solution.py:364
  95.1 0.1 pack_2.1
  95.2 14.2 %all_to_all.34.refs_0_ = bf16[32,40,128]{2,1,0:T(8,128)(2,1)S(1)} all-to-all(bf16[32,40,128]{2,1,0:T(8,128)(2,1)S(1)} %pack_2.1), channel_id=1, replica_groups=mesh['row'=4,'col'=8] {'row','col'}, dimensions={0} | all-to-all | bytes 655360 | tf_op jit(solution)/shard_map/all_to_all | solution.py:476
  109.4 0.2 last.1
  109.6 11.1 %all_to_all.35.msg_ref = s16[32,24,128]{2,1,0:T(8,128)(2,1)S(1)} all-to-all(s16[32,24,128]{2,1,0:T(8,128)(2,1)S(1)} %last.1), channel_id=1, replica_groups=mesh['row'=4,'col'=8] {'row','col'}, dimensions={0} | all-to-all | bytes 393216 | tf_op jit(solution)/shard_map/all_to_all | solution.py:498
  120.7 0.1 finish.1
  120.8 0.1 reshape.10
  120.9 0.3 copy.10
  121.2 1.2 reshape.11
  (8 shorter events, 0.0 us)
Async XLA Ops:
  2.3 15.3 %collective-permute-start.2 = (bf16[4,64,288]{2,1,0:T(8,128)(2,1)S(1)}, bf16[4,64,288]{2,1,0:T(8,128)(2,1)S(1)}, u32[]{:S(2)}, u32[]{:S(2)}) collective-permute-start(bf16[4,64,288]{2,1,0:T(8,128)(2,1)S(1)} %get-tuple-element.16.refs_2_), channel_id=1, source_target_pairs={{0,6},{1,7},{10,8},{11,9},{20,18},{21,19},{30,28},{31,29}} | collective-permute-start | bytes 442376 | tf_op jit(solution)/shard_map/ppermute | solution.py:429
  8.2 9.5 %collective-permute-start.1 = (bf16[4,64,288]{2,1,0:T(8,128)(2,1)S(1)}, bf16[4,64,288]{2,1,0:T(8,128)(2,1)S(1)}, u32[]{:S(2)}, u32[]{:S(2)}) collective-permute-start(bf16[4,64,288]{2,1,0:T(8,128)(2,1)S(1)} %get-tuple-element.16.refs_2_), channel_id=1, source_target_pairs={{0,4},{1,5},{10,14},{11,15},{20,16},{21,17},{30,26},{31,27}} | collective-permute-start | bytes 442376 | tf_op jit(solution)/shard_map/ppermute | solution.py:429
  9.5 8.2 %collective-permute-start = (bf16[4,64,288]{2,1,0:T(8,128)(2,1)S(1)}, bf16[4,64,288]{2,1,0:T(8,128)(2,1)S(1)}, u32[]{:S(2)}, u32[]{:S(2)}) collective-permute-start(bf16[4,64,288]{2,1,0:T(8,128)(2,1)S(1)} %get-tuple-element.16.refs_2_), channel_id=1, source_target_pairs={{0,2},{1,3},{10,12},{11,13},{20,22},{21,23},{30,24},{31,25}} | collective-permute-start | bytes 442376 | tf_op jit(solution)/shard_map/ppermute | solution.py:429
  12.3 2.5 %copy-start = (bf16[1,1,12,2,288,288]{5,4,3,2,1,0:T(8,128)(2,1)S(1)}, bf16[1,1,12,2,288,288]{5,4,3,2,1,0:T(8,128)(2,1)}, u32[]{:S(2)}) copy-start(bf16[1,1,12,2,288,288]{5,4,3,2,1,0:T(8,128)(2,1)} %param.7) | copy-start | bytes 11943940
  17.6 6.5 %collective-permute-start.4 = (f32[4,64,288]{2,1,0:T(8,128)S(1)}, f32[4,64,288]{2,1,0:T(8,128)S(1)}, u32[]{:S(2)}, u32[]{:S(2)}) collective-permute-start(f32[4,64,288]{2,1,0:T(8,128)S(1)} %get-tuple-element.18), channel_id=1, source_target_pairs={{0,1},{1,0},{2,3},{3,2},{4,5},{5,4},{6,7},{7,6},{8,9},{9,8},{10,11... | collective-permute-start | bytes 884744 | tf_op jit(solution)/shard_map/ppermute | solution.py:461
  17.7 1.9 %collective-permute-start.3 = (bf16[4,64,288]{2,1,0:T(8,128)(2,1)S(1)}, bf16[4,64,288]{2,1,0:T(8,128)(2,1)S(1)}, u32[]{:S(2)}, u32[]{:S(2)}) collective-permute-start(bf16[4,64,288]{2,1,0:T(8,128)(2,1)S(1)} %add_select_fusion.refs_2_), channel_id=1, source_target_pairs={{0,1},{1,0},{2,3},{3,2},{4,5},{5,4},{6,7},{7,6},{8,9},{9,8},{10,11... | collective-permute-start | bytes 442376 | tf_op jit(solution)/shard_map/ppermute | solution.py:431
  19.6 2.5 %copy-start.1 = (bf16[1,1,12,2,288,288]{5,4,3,2,1,0:T(8,128)(2,1)S(1)}, bf16[1,1,12,2,288,288]{5,4,3,2,1,0:T(8,128)(2,1)}, u32[]{:S(2)}) copy-start(bf16[1,1,12,2,288,288]{5,4,3,2,1,0:T(8,128)(2,1)} %param.7) | copy-start | bytes 11943940
  22.1 33.6 %copy-start.2 = (bf16[1,1,12,2,288,288]{5,4,3,2,1,0:T(8,128)(2,1)S(1)}, bf16[1,1,12,2,288,288]{5,4,3,2,1,0:T(8,128)(2,1)}, u32[]{:S(2)}) copy-start(bf16[1,1,12,2,288,288]{5,4,3,2,1,0:T(8,128)(2,1)} %param.7) | copy-start | bytes 11943940
  55.8 3.4 %collective-permute-start.5 = (bf16[32,40,128]{2,1,0:T(8,128)(2,1)S(1)}, bf16[32,40,128]{2,1,0:T(8,128)(2,1)S(1)}, u32[]{:S(2)}, u32[]{:S(2)}) collective-permute-start(bf16[32,40,128]{2,1,0:T(8,128)(2,1)S(1)} %all_to_all.31.refs_2_), channel_id=1, source_target_pairs={{0,1},{1,0},{2,3},{3,2},{4,5},{5,4},{6,7},{7,6},{8,9},{9,8},{10,11... | collective-permute-start | bytes 983048 | tf_op jit(solution)/shard_map/ppermute | solution.py:449
  58.5 2.5 %collective-permute-start.6 = (f32[4,64,288]{2,1,0:T(8,128)S(1)}, f32[4,64,288]{2,1,0:T(8,128)S(1)}, u32[]{:S(2)}, u32[]{:S(2)}) collective-permute-start(f32[4,64,288]{2,1,0:T(8,128)S(1)} %get-tuple-element.22), channel_id=1, source_target_pairs={{0,1},{1,0},{2,3},{3,2},{4,5},{5,4},{6,7},{7,6},{8,9},{9,8},{10,11... | collective-permute-start | bytes 884744 | tf_op jit(solution)/shard_map/ppermute | solution.py:461
  89.8 3.4 %collective-permute-start.7 = (bf16[32,40,128]{2,1,0:T(8,128)(2,1)S(1)}, bf16[32,40,128]{2,1,0:T(8,128)(2,1)S(1)}, u32[]{:S(2)}, u32[]{:S(2)}) collective-permute-start(bf16[32,40,128]{2,1,0:T(8,128)(2,1)S(1)} %all_to_all.33.refs_2_), channel_id=1, source_target_pairs={{0,1},{1,0},{2,3},{3,2},{4,5},{5,4},{6,7},{7,6},{8,9},{9,8},{10,11... | collective-permute-start | bytes 983048 | tf_op jit(solution)/shard_map/ppermute | solution.py:449
  92.5 2.5 %collective-permute-start.8 = (f32[4,64,288]{2,1,0:T(8,128)S(1)}, f32[4,64,288]{2,1,0:T(8,128)S(1)}, u32[]{:S(2)}, u32[]{:S(2)}) collective-permute-start(f32[4,64,288]{2,1,0:T(8,128)S(1)} %get-tuple-element.26), channel_id=1, source_target_pairs={{0,1},{1,0},{2,3},{3,2},{4,5},{5,4},{6,7},{7,6},{8,9},{9,8},{10,11... | collective-permute-start | bytes 884744 | tf_op jit(solution)/shard_map/ppermute | solution.py:461

commit v3 on v2

--- a/solution.py
+++ b/solution.py
@@ -101,10 +101,17 @@
     return jnp.concatenate([-tiles[:, 4:], tiles[:, :4]], axis=1).reshape(shape)
 
 
-def put_block(xs_ref, at, value):
+def put_block(xs_ref, at, value, mirror):
     entries = value.shape[1]
-    xs_ref[at, :, :entries] = value.astype(BF)
-    xs_ref[at, :, entries:] = turned(value).astype(BF)
+    main = 2 * LANES
+    both = [value.astype(BF), turned(value).astype(BF)]
+    if mirror:
+        xs_ref[at, :, :entries] = both[0]
+        xs_ref[at, :, entries:] = both[1]
+    else:
+        xs_ref[at, :, :main] = both[0][:, :main]
+        xs_ref[at, :, main : 2 * main] = both[1][:, :main]
+        xs_ref[at, :, 2 * main :] = jnp.concatenate([part[:, main:] for part in both], axis=1)
 
 
 def unpack_half(msg_ref, q, half, xs_ref, at):
@@ -117,24 +124,28 @@
     ends = msg_ref[q * groups : (q + 1) * groups, 32:40, :].astype(F32).reshape(groups * 8, LANES)
     if half:
         ends = pltpu.roll(ends, LANES - tail, 1)
-    put_block(xs_ref, at, jnp.concatenate(pieces + [ends[:, :tail]], axis=1))
-
-
-def copy_in(x_ref, xs_ref, offset):
+    put_block(xs_ref, at, jnp.concatenate(pieces + [ends[:, :tail]], axis=1), half)
+
+
+def copy_in(x_ref, xs_ref, offset, mirror):
     for q in range(x_ref.shape[0]):
-        put_block(xs_ref, offset + q, x_ref[q].astype(F32))
-
-
-def slot_products(table_ref, g_ref, xs_ref, acc_ref, mirror, cols):
+        put_block(xs_ref, offset + q, x_ref[q].astype(F32), mirror)
+
+
+def across(left, right):
+    return lax.dot_general(left, right, (((1,), (1,)), ((), ())), preferred_element_type=F32)
+
+
+def slot_products(count_ref, table_ref, g_ref, xs_ref, acc_ref, mirror, cols):
     acc_ref[...] = jnp.zeros_like(acc_ref)
     slots, _, depth, entries = g_ref.shape
-    r = table_ref[3, 0]
-    c = table_ref[4, 0]
+    r, c = [table_ref[row, 0].astype(jnp.int32) for row in (2, 3)]
+    count = count_ref[0, 0]
     blocks = (acc_ref.shape[0] - 1) // (1 if mirror else 2)
     for s in range(slots):
-        local_row = table_ref[0, s]
-        local_col = table_ref[1, s]
-        living = s < table_ref[2, 0]
+        local_row = table_ref[0, s].astype(jnp.int32)
+        local_col = table_ref[1, s].astype(jnp.int32)
+        living = s < count
         half = local_row // 2
         place = (local_row % 2 ^ c % 2) * blocks + half
         if mirror:
@@ -143,19 +154,20 @@
             value = jnp.dot(xs_ref[place], both, preferred_element_type=F32)
             acc_ref[jnp.where(living & off_diagonal, local_col, blocks)] += value
         else:
-            over = (((1,), (1,)), ((), ()))
-            left = xs_ref[local_col, :, :entries]
-            value = lax.dot_general(left, g_ref[s, 0], over, preferred_element_type=F32)
-            left = xs_ref[local_col, :, entries:]
-            value += lax.dot_general(left, g_ref[s, 1], over, preferred_element_type=F32)
+            main = 2 * LANES
+            left = xs_ref[local_col]
+            ends = jnp.concatenate([g_ref[s, 0, :, main:], g_ref[s, 1, :, main:]], axis=1)
+            value = across(left[:, :main], g_ref[s, 0, :, :main])
+            value += across(left[:, main : 2 * main], g_ref[s, 1, :, :main])
+            value += across(left[:, 2 * main :], ends)
             acc_ref[jnp.where(living, place, 2 * blocks)] += value
 
 
 def start_kernel(classes, small_ref, back_ref, out_ref, contrast_ref):
     blocks = out_ref.shape[0]
     cells = contrast_ref.shape[2]
-    kinds = small_ref[0:blocks, :cells]
-    tables = small_ref[blocks : blocks + 2, :]
+    kinds = small_ref[4 : 4 + blocks, :cells]
+    tables = small_ref[4 + blocks : 6 + blocks, :]
     contrast = []
     for part in range(2):
         value = jnp.zeros(kinds.shape, F32)
@@ -169,8 +181,8 @@
         out_ref[q] = (real[q : q + 1] * back + imag[q : q + 1] * turned(back)).astype(BF)
 
 
-def share_kernel(table_ref, contrast_ref, back_ref, extra_ref):
-    r = table_ref[3, 0]
+def share_kernel(table_ref, contrast_ref, back_ref, _, extra_ref):
+    r = table_ref[2, 0].astype(jnp.int32)
     blocks, rows, entries = back_ref.shape
     half = LANES // 2
     cells = contrast_ref.shape[2]
@@ -199,29 +211,29 @@
             extra_ref[q * rows // 8 + g] = jnp.concatenate([beside, value], axis=0).astype(BF)
 
 
-def direct_kernel(first, table_ref, g_ref, x_ref, own_ref, other_ref, xs_ref, acc_ref):
+def direct_kernel(first, count_ref, table_ref, g_ref, x_ref, own_ref, other_ref, xs_ref, acc_ref):
     blocks = own_ref.shape[0]
     if first:
-        copy_in(x_ref, xs_ref, 0)
+        copy_in(x_ref, xs_ref, 0, False)
     else:
         for q in range(blocks):
             unpack_half(x_ref, q, 0, xs_ref, q)
-    slot_products(table_ref, g_ref, xs_ref, acc_ref, False, 0)
+    slot_products(count_ref, table_ref, g_ref, xs_ref, acc_ref, False, 0)
     for q in range(blocks):
         own_ref[q] = acc_ref[q]
         other_ref[q] = acc_ref[blocks + q]
 
 
-def mirror_kernel(first, cols, table_ref, g_ref, x_ref, x_other_ref, out_ref, xs_ref, acc_ref):
+def mirror_kernel(first, cols, count_ref, table_ref, g_ref, x_ref, x_other_ref, out_ref, xs_ref, acc_ref):
     blocks = out_ref.shape[0]
     if first:
-        copy_in(x_ref, xs_ref, 0)
-        copy_in(x_other_ref, xs_ref, blocks)
+        copy_in(x_ref, xs_ref, 0, True)
+        copy_in(x_other_ref, xs_ref, blocks, True)
     else:
         for q in range(blocks):
             unpack_half(x_ref, q, 1, xs_ref, q)
             unpack_half(x_other_ref, q, 1, xs_ref, blocks + q)
-    slot_products(table_ref, g_ref, xs_ref, acc_ref, True, cols)
+    slot_products(count_ref, table_ref, g_ref, xs_ref, acc_ref, True, cols)
     for q in range(blocks):
         out_ref[q] = acc_ref[q]
 
@@ -372,17 +384,14 @@
     )(*operands)
 
 
-def stacked(arrays, dtype):
-    rows = sum(array.shape[0] for array in arrays)
+def stacked(arrays):
+    heights = [1 if array is None else array.shape[0] for array in arrays]
     total = 0
     at = 0
-    for array in arrays:
-        height, width = array.shape
-        total += lax.pad(
-            array,
-            jnp.zeros((), array.dtype),
-            ((at, rows - at - height, 0), (0, LANES - width, 0)),
-        ).astype(dtype)
+    for array, height in zip(arrays, heights):
+        if array is not None:
+            edges = ((at, sum(heights) - at - height, 0), (0, LANES - array.shape[1], 0))
+            total += lax.pad(array, jnp.zeros((), array.dtype), edges).astype(F32)
         at += height
     return total
 
@@ -399,9 +408,9 @@
     tail = entries - 2 * LANES
     both = ("row", "col")
 
-    floats = stacked([cell_class[:, 0, :], class_contrast.T], F32)
-    here = jnp.stack([r, c]).astype(jnp.int32)[:, None]
-    table = stacked([slot_rows[0], slot_cols[0], slot_count, here], jnp.int32)
+    small = stacked([slot_rows[0], slot_cols[0], None, None, cell_class[:, 0, :], class_contrast.T])
+    line = lax.broadcasted_iota(jnp.int32, small.shape, 0)
+    small = jnp.where(line == 2, r.astype(F32), jnp.where(line == 3, c.astype(F32), small))
 
     block = (groups * 8, entries)
     back = background[:, :, :, 0, :].reshape(2, groups, 4, blocks, entries)
@@ -413,31 +422,37 @@
             jax.ShapeDtypeStruct((2, blocks, entries // 3), F32),
         ),
         [],
-        (floats, back),
+        (small, back),
         [],
         "start",
     )
 
     core_pairs = [(i, i ^ 1) for i in range(cols)]
+    chips = cols // 2
     arrived = []
-    for hop in range(1, cols // 2):
-        pairs = [
-            (a * cols + 2 * a + p, a * cols + 2 * ((a + hop) % (cols // 2)) + p)
-            for a in range(rows)
-            for p in range(2)
-        ]
+    for hop in range(1, chips):
+        pairs = []
+        for a in range(rows):
+            far = (a + hop) % chips
+            for k in range(chips):
+                for p in range(2):
+                    to = {a: 2 * far + p, far: 2 * a + p}.get(k, 2 * k + 1 - p)
+                    pairs.append((a * cols + 2 * k + p, a * cols + to))
         arrived.append(lax.ppermute(start, both, pairs))
-    row_mine = jnp.where(c // 2 == r, start, sum(arrived))
-    row_other = lax.ppermute(row_mine, "col", core_pairs)
-
     extra = whole_call(
         share_kernel,
         jax.ShapeDtypeStruct((rows * cols, 16, LANES), BF),
         [pltpu.SMEM],
-        (table, contrast, back),
+        (small, contrast, back, green),
         [],
         "share",
     )
+    extra, *arrived = lax.optimization_barrier((extra, *arrived))
+    row_mine = start
+    for hop in range(1, chips):
+        row_mine = jnp.where(c // 2 == (r + hop) % chips, arrived[hop - 1], row_mine)
+    row_other = lax.ppermute(row_mine, "col", core_pairs)
+
     part = jax.ShapeDtypeStruct((blocks,) + block, F32)
     message = jax.ShapeDtypeStruct((rows * cols, 40, LANES), BF)
     for step in range(PRODUCTS):
@@ -450,8 +465,8 @@
         own, other = whole_call(
             lambda *refs, first=first: direct_kernel(first, *refs),
             (part, part),
-            [pltpu.SMEM],
-            (table, green, direct_in),
+            [pltpu.SMEM] * 2,
+            (slot_count, small, green, direct_in),
             [
                 pltpu.VMEM((blocks, groups * 8, 2 * entries), BF),
                 pltpu.VMEM((2 * blocks + 1,) + block, F32),
@@ -462,8 +477,8 @@
         mirror = whole_call(
             lambda *refs, first=first: mirror_kernel(first, cols, *refs),
             part,
-            [pltpu.SMEM],
-            (table, green) + mirror_in,
+            [pltpu.SMEM] * 2,
+            (slot_count, small, green) + mirror_in,
             [
                 pltpu.VMEM((2 * blocks, groups * 8, 2 * entries), BF),
                 pltpu.VMEM((blocks + 1,) + block, F32),

time: 123 us -> 119 us (0.967)
  starting transfers between devices: 10.2 us -> 5.61 us
  blocking collectives: 85.1 us -> 86.5 us
    ppermute x3, starting transfers between devices: 8.41 us -> 3.96 us  [local_owners(): arrived.append(lax.ppermute(start, both, pairs))]
    all_to_all x3, blocking collectives: 45.3 us -> 46.8 us  [local_owners(): y_msg = lax.all_to_all(y_msg, both, 0, 0, tiled=True)]
    add x2 -> x0, other arithmetic: 1.39 us -> none  [stacked(): total += lax.pad(array, jnp.zeros((), array.dtype), ((at, rows - at - hei...]
  transfers between devices with their start and end apart: 9 -> 9, of which waited for: 1 -> 2; matrix products, arithmetic and copies ran while one was open for 1% -> 0% of each run, Pallas kernels for 12% -> 12%
where the time goes in v3:
time: 119 us; the launch traced here: 118 us
  blocking collectives  86.5 us (73%)
  Pallas kernels  15.2 us (13%)
  local copies, waits for them, and re-layouts  7.95 us (7%)
  starting transfers between devices  5.61 us (5%)
  waiting for transfers between devices  1.19 us (1%)
    all_to_all x3, blocking collectives, local_owners(): y_msg = lax.all_to_all(y_msg, both, 0, 0, tiled=True)  46.8 us
    all_to_all x3, blocking collectives, local_owners(): x_msg = lax.all_to_all(x_msg, both, 0, 0, tiled=True)  39.8 us
    pallas_call x15, Pallas kernels, whole_call(): pl.pallas_call(kernel, out_shape=out_shape, in_specs=[pl.BlockSpec(memory...  15.2 us
    unnamed x7, local copies, waits for them, and re-layouts  6.14 us
    ppermute x3, starting transfers between devices, local_owners(): arrived.append(lax.ppermute(start, both, pairs))  3.96 us
  transfers between devices with their start and end apart: 9, of which 2 were waited for; matrix products, arithmetic and copies ran while one was open for 0% of the time, Pallas kernels for 12%

profile of v3, /device:TPU:0, one launch (start us, length us, event | category | flops | bytes accessed | tf_op | source)
XLA Modules:
  0.0 118.3 jit_solution(2610820911964636610)
XLA Ops:
  0.0 1.1 copy.10
  1.1 0.1 copy.12
  1.2 0.1 reshape.9.refs_1_.back_ref
  1.4 0.8 select_select_fusion.1.refs_0_.table_ref.refs_1_
  2.1 0.3 start.1
  2.4 4.0 %collective-permute-start.2 = (bf16[4,64,288]{2,1,0:T(8,128)(2,1)S(1)}, bf16[4,64,288]{2,1,0:T(8,128)(2,1)S(1)}, u32[]{:S(2)}, u32[]{:S(2)}) collective-permute-start(bf16[4,64,288]{2,1,0:T(8,128)(2,1)S(1)} %get-tuple-element.21.refs_3_), channel_id=1, source_target_pairs={{0,6},{1,7},{2,3},{3,2},{4,5},{5,4},{6,0},{7,1},{8,10},{9,11},{10,... | collective-permute-start | bytes 442376 | tf_op jit(solution)/shard_map/ppermute | solution.py:441
  6.4 0.0 collective-permute-start.1
  6.4 0.0 collective-permute-start
  7.0 0.0 copy-start
  7.0 2.5 %copy-done = bf16[1,1,12,2,288,288]{5,4,3,2,1,0:T(8,128)(2,1)S(1)} copy-done((bf16[1,1,12,2,288,288]{5,4,3,2,1,0:T(8,128)(2,1)S(1)}, bf16[1,1,12,2,288,288]{5,4,3,2,1,0:T(8,128)(2,1)}, u32[]{:S(2)}) %copy-start) | copy-done | bytes 3981336
  9.5 2.4 %direct_0.1 = (f32[4,64,288]{2,1,0:T(8,128)S(1)}, f32[4,64,288]{2,1,0:T(8,128)S(1)}) custom-call(s32[1,1]{1,0:T(1,128)S(6)} %copy.13.refs_0_, f32[10,128]{1,0:T(8,128)S(1)} %select_select_fusion.1.refs_0_.table_ref.refs_1_, bf16[12,2,288,288]{3,2,1,0:T(8,128)(2,1)S(1)} %bitcast.10, bf16[4,64,288]{2,1,0:T(8,128)(2,1)S(1)} %get-tuple-element.21.refs_3_), custom_call_target="tpu_custom_call" | custom-call | tf_op jit(solution)/shard_map/direct_0/pallas_call | solution.py:376
  12.0 0.1 collective-permute-start.4
  12.1 0.0 copy-start.1
  12.1 2.5 %copy-done.1 = bf16[1,1,12,2,288,288]{5,4,3,2,1,0:T(8,128)(2,1)S(1)} copy-done((bf16[1,1,12,2,288,288]{5,4,3,2,1,0:T(8,128)(2,1)S(1)}, bf16[1,1,12,2,288,288]{5,4,3,2,1,0:T(8,128)(2,1)}, u32[]{:S(2)}) %copy-start.1) | copy-done | bytes 3981336
  14.6 0.8 share.1.rest_0_
  15.4 0.0 collective-permute-done.2
  15.4 0.1 collective-permute-done.1
  15.5 0.1 select_select_fusion.refs_3_
  15.5 0.4 collective-permute-start.3
  16.0 1.1 collective-permute-done.3.refs_4_
  17.1 0.0 copy-done.2
  17.1 2.0 %mirror_0.1.mirror_ref = f32[4,64,288]{2,1,0:T(8,128)S(1)} custom-call(s32[1,1]{1,0:T(1,128)S(6)} %copy.13.refs_0_, f32[10,128]{1,0:T(8,128)S(1)} %select_select_fusion.1.refs_0_.table_ref.refs_1_, bf16[12,2,288,288]{3,2,1,0:T(8,128)(2,1)S(1)} %bitcast.12, bf16[4,64,288]{2,1,0:T(8,128)(2,1)S(1)} %select_select_fusion.refs_3_, ...), custom_call_target="tpu_custom_call" | custom-call | tf_op jit(solution)/shard_map/mirror_0/pallas_call | solution.py:376
  19.1 0.0 collective-permute-done.4.got_ref
  19.1 0.1 pack_0.1
  19.2 18.3 %all_to_all.30.refs_0_ = bf16[32,48,128]{2,1,0:T(8,128)(2,1)S(1)} all-to-all(bf16[32,48,128]{2,1,0:T(8,128)(2,1)S(1)} %pack_0.1), channel_id=1, replica_groups=mesh['row'=4,'col'=8] {'row','col'}, dimensions={0} | all-to-all | bytes 786432 | tf_op jit(solution)/shard_map/all_to_all | solution.py:491
  37.5 0.2 update_0.1
  37.8 14.4 %all_to_all.31.refs_3_ = bf16[32,40,128]{2,1,0:T(8,128)(2,1)S(1)} all-to-all(bf16[32,40,128]{2,1,0:T(8,128)(2,1)S(1)} %get-tuple-element.28), channel_id=1, replica_groups=mesh['row'=4,'col'=8] {'row','col'}, dimensions={0} | all-to-all | bytes 655360 | tf_op jit(solution)/shard_map/all_to_all | solution.py:513
  52.2 2.4 %direct_1.1 = (f32[4,64,288]{2,1,0:T(8,128)S(1)}, f32[4,64,288]{2,1,0:T(8,128)S(1)}) custom-call(s32[1,1]{1,0:T(1,128)S(6)} %copy.13.refs_0_, f32[10,128]{1,0:T(8,128)S(1)} %select_select_fusion.1.refs_0_.table_ref.refs_1_, bf16[12,2,288,288]{3,2,1,0:T(8,128)(2,1)S(1)} %bitcast.13, bf16[32,40,128]{2,1,0:T(8,128)(2,1)S(1)} %all_to_all.31.refs_3_), custom_call_target="tpu_custom_call" | custom-call | tf_op jit(solution)/shard_map/direct_1/pallas_call | solution.py:376
  54.6 0.6 collective-permute-start.6
  55.2 0.0 collective-permute-done.5.refs_4_
  55.2 2.0 %mirror_1.1.mirror_ref = f32[4,64,288]{2,1,0:T(8,128)S(1)} custom-call(s32[1,1]{1,0:T(1,128)S(6)} %copy.13.refs_0_, f32[10,128]{1,0:T(8,128)S(1)} %select_select_fusion.1.refs_0_.table_ref.refs_1_, bf16[12,2,288,288]{3,2,1,0:T(8,128)(2,1)S(1)} %bitcast.14, bf16[32,40,128]{2,1,0:T(8,128)(2,1)S(1)} %all_to_all.31.refs_3_, ...), custom_call_target="tpu_custom_call" | custom-call | tf_op jit(solution)/shard_map/mirror_1/pallas_call | solution.py:376
  57.2 0.0 collective-permute-done.6.got_ref
  57.2 0.1 pack_1.1
  57.3 14.2 %all_to_all.32.refs_0_ = bf16[32,40,128]{2,1,0:T(8,128)(2,1)S(1)} all-to-all(bf16[32,40,128]{2,1,0:T(8,128)(2,1)S(1)} %pack_1.1), channel_id=1, replica_groups=mesh['row'=4,'col'=8] {'row','col'}, dimensions={0} | all-to-all | bytes 655360 | tf_op jit(solution)/shard_map/all_to_all | solution.py:491
  71.5 0.2 update_1.1
  71.7 14.2 %all_to_all.33.refs_3_ = bf16[32,40,128]{2,1,0:T(8,128)(2,1)S(1)} all-to-all(bf16[32,40,128]{2,1,0:T(8,128)(2,1)S(1)} %update_1.1), channel_id=1, replica_groups=mesh['row'=4,'col'=8] {'row','col'}, dimensions={0} | all-to-all | bytes 655360 | tf_op jit(solution)/shard_map/all_to_all | solution.py:513
  85.9 2.4 %direct_2.1 = (f32[4,64,288]{2,1,0:T(8,128)S(1)}, f32[4,64,288]{2,1,0:T(8,128)S(1)}) custom-call(s32[1,1]{1,0:T(1,128)S(6)} %copy.13.refs_0_, f32[10,128]{1,0:T(8,128)S(1)} %select_select_fusion.1.refs_0_.table_ref.refs_1_, bf16[12,2,288,288]{3,2,1,0:T(8,128)(2,1)S(1)} %bitcast.15, bf16[32,40,128]{2,1,0:T(8,128)(2,1)S(1)} %all_to_all.33.refs_3_), custom_call_target="tpu_custom_call" | custom-call | tf_op jit(solution)/shard_map/direct_2/pallas_call | solution.py:376
  88.3 0.6 collective-permute-start.8
  88.9 2.0 %mirror_2.1.mirror_ref = f32[4,64,288]{2,1,0:T(8,128)S(1)} custom-call(s32[1,1]{1,0:T(1,128)S(6)} %copy.13.refs_0_, f32[10,128]{1,0:T(8,128)S(1)} %select_select_fusion.1.refs_0_.table_ref.refs_1_, bf16[12,2,288,288]{3,2,1,0:T(8,128)(2,1)S(1)} %bitcast.16, bf16[32,40,128]{2,1,0:T(8,128)(2,1)S(1)} %all_to_all.33.refs_3_, ...), custom_call_target="tpu_custom_call" | custom-call | tf_op jit(solution)/shard_map/mirror_2/pallas_call | solution.py:376
  90.9 0.0 collective-permute-done.8.got_ref
  90.9 0.1 pack_2.1
  91.0 14.2 %all_to_all.34.refs_0_ = bf16[32,40,128]{2,1,0:T(8,128)(2,1)S(1)} all-to-all(bf16[32,40,128]{2,1,0:T(8,128)(2,1)S(1)} %pack_2.1), channel_id=1, replica_groups=mesh['row'=4,'col'=8] {'row','col'}, dimensions={0} | all-to-all | bytes 655360 | tf_op jit(solution)/shard_map/all_to_all | solution.py:491
  105.3 0.2 last.1
  105.5 11.1 %all_to_all.35.msg_ref = s16[32,24,128]{2,1,0:T(8,128)(2,1)S(1)} all-to-all(s16[32,24,128]{2,1,0:T(8,128)(2,1)S(1)} %last.1), channel_id=1, replica_groups=mesh['row'=4,'col'=8] {'row','col'}, dimensions={0} | all-to-all | bytes 393216 | tf_op jit(solution)/shard_map/all_to_all | solution.py:513
  116.6 0.1 finish.1
  116.7 0.1 reshape.10
  116.8 0.3 copy.9
  117.1 1.2 %reshape.11 = f32[2,32,4,1,288]{4,3,2,1,0:T(1,128)} reshape(f32[2,8,4,4,288]{4,3,2,1,0:T(4,128)S(1)} %copy.9) | data formatting | bytes 589824 | tf_op jit(solution)/shard_map/reshape | solution.py:516
  (6 shorter events, 0.0 us)
Async XLA Ops:
  2.4 13.0 %collective-permute-start.2 = (bf16[4,64,288]{2,1,0:T(8,128)(2,1)S(1)}, bf16[4,64,288]{2,1,0:T(8,128)(2,1)S(1)}, u32[]{:S(2)}, u32[]{:S(2)}) collective-permute-start(bf16[4,64,288]{2,1,0:T(8,128)(2,1)S(1)} %get-tuple-element.21.refs_3_), channel_id=1, source_target_pairs={{0,6},{1,7},{2,3},{3,2},{4,5},{5,4},{6,0},{7,1},{8,10},{9,11},{10,... | collective-permute-start | bytes 442376 | tf_op jit(solution)/shard_map/ppermute | solution.py:441
  6.4 9.1 %collective-permute-start.1 = (bf16[4,64,288]{2,1,0:T(8,128)(2,1)S(1)}, bf16[4,64,288]{2,1,0:T(8,128)(2,1)S(1)}, u32[]{:S(2)}, u32[]{:S(2)}) collective-permute-start(bf16[4,64,288]{2,1,0:T(8,128)(2,1)S(1)} %get-tuple-element.21.refs_3_), channel_id=1, source_target_pairs={{0,4},{1,5},{2,3},{3,2},{4,0},{5,1},{6,7},{7,6},{8,9},{9,8},{10,14... | collective-permute-start | bytes 442376 | tf_op jit(solution)/shard_map/ppermute | solution.py:441
  6.4 9.1 %collective-permute-start = (bf16[4,64,288]{2,1,0:T(8,128)(2,1)S(1)}, bf16[4,64,288]{2,1,0:T(8,128)(2,1)S(1)}, u32[]{:S(2)}, u32[]{:S(2)}) collective-permute-start(bf16[4,64,288]{2,1,0:T(8,128)(2,1)S(1)} %get-tuple-element.21.refs_3_), channel_id=1, source_target_pairs={{0,2},{1,3},{2,0},{3,1},{4,5},{5,4},{6,7},{7,6},{8,9},{9,8},{10,12... | collective-permute-start | bytes 442376 | tf_op jit(solution)/shard_map/ppermute | solution.py:441
  7.0 2.5 %copy-start = (bf16[1,1,12,2,288,288]{5,4,3,2,1,0:T(8,128)(2,1)S(1)}, bf16[1,1,12,2,288,288]{5,4,3,2,1,0:T(8,128)(2,1)}, u32[]{:S(2)}) copy-start(bf16[1,1,12,2,288,288]{5,4,3,2,1,0:T(8,128)(2,1)} %param.7) | copy-start | bytes 11943940
  12.0 7.1 %collective-permute-start.4 = (f32[4,64,288]{2,1,0:T(8,128)S(1)}, f32[4,64,288]{2,1,0:T(8,128)S(1)}, u32[]{:S(2)}, u32[]{:S(2)}) collective-permute-start(f32[4,64,288]{2,1,0:T(8,128)S(1)} %get-tuple-element.26), channel_id=1, source_target_pairs={{0,1},{1,0},{2,3},{3,2},{4,5},{5,4},{6,7},{7,6},{8,9},{9,8},{10,11... | collective-permute-start | bytes 884744 | tf_op jit(solution)/shard_map/ppermute | solution.py:476
  12.1 2.5 %copy-start.1 = (bf16[1,1,12,2,288,288]{5,4,3,2,1,0:T(8,128)(2,1)S(1)}, bf16[1,1,12,2,288,288]{5,4,3,2,1,0:T(8,128)(2,1)}, u32[]{:S(2)}) copy-start(bf16[1,1,12,2,288,288]{5,4,3,2,1,0:T(8,128)(2,1)} %param.7) | copy-start | bytes 11943940
  14.6 2.5 %copy-start.2 = (bf16[1,1,12,2,288,288]{5,4,3,2,1,0:T(8,128)(2,1)S(1)}, bf16[1,1,12,2,288,288]{5,4,3,2,1,0:T(8,128)(2,1)}, u32[]{:S(2)}) copy-start(bf16[1,1,12,2,288,288]{5,4,3,2,1,0:T(8,128)(2,1)} %param.7) | copy-start | bytes 11943940
  15.5 1.5 %collective-permute-start.3 = (bf16[4,64,288]{2,1,0:T(8,128)(2,1)S(1)}, bf16[4,64,288]{2,1,0:T(8,128)(2,1)S(1)}, u32[]{:S(2)}, u32[]{:S(2)}) collective-permute-start(bf16[4,64,288]{2,1,0:T(8,128)(2,1)S(1)} %select_select_fusion.refs_3_), channel_id=1, source_target_pairs={{0,1},{1,0},{2,3},{3,2},{4,5},{5,4},{6,7},{7,6},{8,9},{9,8},{10,11... | collective-permute-start | bytes 442376 | tf_op jit(solution)/shard_map/ppermute | solution.py:454
  52.2 3.0 %collective-permute-start.5 = (bf16[32,40,128]{2,1,0:T(8,128)(2,1)S(1)}, bf16[32,40,128]{2,1,0:T(8,128)(2,1)S(1)}, u32[]{:S(2)}, u32[]{:S(2)}) collective-permute-start(bf16[32,40,128]{2,1,0:T(8,128)(2,1)S(1)} %all_to_all.31.refs_3_), channel_id=1, source_target_pairs={{0,1},{1,0},{2,3},{3,2},{4,5},{5,4},{6,7},{7,6},{8,9},{9,8},{10,11... | collective-permute-start | bytes 983048 | tf_op jit(solution)/shard_map/ppermute | solution.py:464
  54.6 2.6 %collective-permute-start.6 = (f32[4,64,288]{2,1,0:T(8,128)S(1)}, f32[4,64,288]{2,1,0:T(8,128)S(1)}, u32[]{:S(2)}, u32[]{:S(2)}) collective-permute-start(f32[4,64,288]{2,1,0:T(8,128)S(1)} %get-tuple-element.30), channel_id=1, source_target_pairs={{0,1},{1,0},{2,3},{3,2},{4,5},{5,4},{6,7},{7,6},{8,9},{9,8},{10,11... | collective-permute-start | bytes 884744 | tf_op jit(solution)/shard_map/ppermute | solution.py:476
  85.9 3.0 %collective-permute-start.7 = (bf16[32,40,128]{2,1,0:T(8,128)(2,1)S(1)}, bf16[32,40,128]{2,1,0:T(8,128)(2,1)S(1)}, u32[]{:S(2)}, u32[]{:S(2)}) collective-permute-start(bf16[32,40,128]{2,1,0:T(8,128)(2,1)S(1)} %all_to_all.33.refs_3_), channel_id=1, source_target_pairs={{0,1},{1,0},{2,3},{3,2},{4,5},{5,4},{6,7},{7,6},{8,9},{9,8},{10,11... | collective-permute-start | bytes 983048 | tf_op jit(solution)/shard_map/ppermute | solution.py:464
  88.3 2.6 %collective-permute-start.8 = (f32[4,64,288]{2,1,0:T(8,128)S(1)}, f32[4,64,288]{2,1,0:T(8,128)S(1)}, u32[]{:S(2)}, u32[]{:S(2)}) collective-permute-start(f32[4,64,288]{2,1,0:T(8,128)S(1)} %get-tuple-element.34), channel_id=1, source_target_pairs={{0,1},{1,0},{2,3},{3,2},{4,5},{5,4},{6,7},{7,6},{8,9},{9,8},{10,11... | collective-permute-start | bytes 884744 | tf_op jit(solution)/shard_map/ppermute | solution.py:476

commit v4 on v3

v4 whole, which is shorter than its diff:
```python
import jax
import jax.numpy as jnp
from jax import lax
from jax.experimental import pallas as pl
from jax.experimental.pallas import tpu as pltpu
from jax.sharding import PartitionSpec as P

PRODUCTS = 3
LANES = 128
SMALLEST = 2.0**-100
VMEM_BYTES = 8 * 1024 * 1024
BF = jnp.bfloat16
F32 = jnp.float32


def from_root(array, axis, root):
    mine = lax.axis_index(axis) == root
    return lax.psum(jnp.where(mine, array, jnp.zeros_like(array)), axis)


def complex_scale(field_now, contrast_re, contrast_im):
    real_part = field_now[0]
    imag_part = field_now[1]
    scaled = jnp.stack(
        [
            contrast_re * real_part - contrast_im * imag_part,
            contrast_re * imag_part + contrast_im * real_part,
        ]
    )
    return scaled.astype(BF)


def combine(products):
    return jnp.stack([products[0, 0] - products[1, 1], products[0, 1] + products[1, 0]])


def local_general(green_blocks, slot_rows, slot_cols, slot_count, cell_class, class_contrast, background):
    row_index = lax.axis_index("row")
    col_index = lax.axis_index("col")
    stride = lax.axis_size("col")
    green_tiles = green_blocks[0, 0]
    slot_total = green_tiles.shape[0]
    entries = green_tiles.shape[-1]
    sources = background.shape[1]
    col_blocks = background.shape[2]
    row_blocks = 2 * col_blocks
    local_rows = slot_rows[0, 0]
    local_cols = slot_cols[0, 0]
    global_rows = local_rows // 2 * stride + 2 * row_index + local_rows % 2
    global_cols = local_cols * stride + col_index
    off_diagonal = (global_rows != global_cols).astype(F32)
    living = (jnp.arange(slot_total) < slot_count[0, 0]).astype(F32)
    row_pick = (local_rows[:, None] == jnp.arange(row_blocks)[None, :]).astype(F32) * living[:, None]
    col_pick = (local_cols[:, None] == jnp.arange(col_blocks)[None, :]).astype(F32) * (
        living * off_diagonal
    )[:, None]
    classes = class_contrast.shape[0]
    lookup = (cell_class[:, 0, :, None] == jnp.arange(classes)[None, None, :]).astype(F32)
    values = jnp.einsum("bte,ec->btc", lookup, class_contrast, precision=lax.Precision.HIGHEST)
    contrast_re = jnp.tile(values[:, :, 0], (1, 3))
    contrast_im = jnp.tile(values[:, :, 1], (1, 3))
    start_field = background[:, :, :, 0, :]
    field_now = start_field
    current = complex_scale(field_now, contrast_re, contrast_im)
    for step_index in range(PRODUCTS):
        final_step = step_index + 1 == PRODUCTS
        halves = [from_root(current, "col", 2 * row_index + parity) for parity in range(2)]
        row_current = jnp.stack(halves, axis=3).reshape(2, sources, row_blocks, entries)
        direct_in = jnp.take(current, local_cols, axis=2)
        mirror_in = jnp.take(row_current, local_rows, axis=2)
        direct_terms = combine(
            jnp.einsum("sqoi,pksi->qpkso", green_tiles, direct_in, preferred_element_type=F32)
        )
        mirror_terms = combine(
            jnp.einsum("sqoi,pkso->qpksi", green_tiles, mirror_in, preferred_element_type=F32)
        )
        direct_part = jnp.einsum(
            "pkse,sb->pkbe", direct_terms, row_pick, precision=lax.Precision.HIGHEST
        )
        mirror_part = jnp.einsum(
            "pkse,sb->pkbe", mirror_terms, col_pick, precision=lax.Precision.HIGHEST
        )
        row_total = lax.psum(direct_part, "col")
        owned_part = lax.dynamic_index_in_dim(
            row_total.reshape(2, sources, col_blocks, 2, entries),
            col_index % 2,
            axis=3,
            keepdims=False,
        )
        direct_here = from_root(owned_part, "row", col_index // 2)
        column_total = lax.psum(mirror_part, "row")
        field_now = start_field + column_total + direct_here
        if not final_step:
            current = complex_scale(field_now, contrast_re, contrast_im)
    return field_now[:, :, :, None, :]


MAIN = 2 * LANES
TAIL = LANES // 4
ENDS = 4 * MAIN
WIDTH = ENDS + LANES


def turned(value):
    half = value.shape[0] // 2
    return jnp.concatenate([-value[half:], value[:half]], axis=0)


def shifted(value, lanes):
    return pltpu.roll(value, LANES - lanes, 1) if lanes else value


def put_block(xs_ref, at, value, mirror):
    entries = value.shape[1]
    both = [value.astype(BF), turned(value).astype(BF)]
    if mirror:
        xs_ref[at, :, :entries] = both[0]
        xs_ref[at, :, entries:] = both[1]
    else:
        xs_ref[at, :, :MAIN] = both[0][:, :MAIN]
        xs_ref[at, :, MAIN : 2 * MAIN] = both[1][:, :MAIN]
        xs_ref[at, :, 2 * MAIN :] = jnp.concatenate([part[:, MAIN:] for part in both], axis=1)


def gathered_rows(msg_ref, q, lanes):
    groups = msg_ref.shape[0] // 4
    return jnp.concatenate([msg_ref[q * groups + g, :, lanes].astype(F32) for g in range(groups)], axis=0)


def unpack_half(msg_ref, q, half, xs_ref, at):
    ends = gathered_rows(msg_ref, q, slice(ENDS, WIDTH))
    parts = []
    for k in (2 * half, 2 * half + 1):
        main = gathered_rows(msg_ref, q, slice(k * MAIN, (k + 1) * MAIN))
        parts.append(jnp.concatenate([main, shifted(ends, k * TAIL)[:, :TAIL]], axis=1))
    put_block(xs_ref, at, jnp.concatenate(parts, axis=0), half)


def copy_in(x_ref, xs_ref, offset, mirror):
    for q in range(x_ref.shape[0]):
        put_block(xs_ref, offset + q, x_ref[q].astype(F32), mirror)


def across(left, right):
    return lax.dot_general(left, right, (((1,), (1,)), ((), ())), preferred_element_type=F32)


def slot_products(count_ref, table_ref, g_ref, xs_ref, acc_ref, mirror, cols):
    acc_ref[...] = jnp.zeros_like(acc_ref)
    slots, _, depth, entries = g_ref.shape
    r, c = [table_ref[row, 0].astype(jnp.int32) for row in (2, 3)]
    count = count_ref[0, 0]
    blocks = (acc_ref.shape[0] - 1) // (1 if mirror else 2)
    for s in range(slots):
        local_row = table_ref[0, s].astype(jnp.int32)
        local_col = table_ref[1, s].astype(jnp.int32)
        living = s < count
        half = local_row // 2
        place = (local_row % 2 ^ c % 2) * blocks + half
        if mirror:
            off_diagonal = half * cols + 2 * r + local_row % 2 != local_col * cols + c
            both = g_ref[s].reshape(2 * depth, entries)
            value = jnp.dot(xs_ref[place], both, preferred_element_type=F32)
            acc_ref[jnp.where(living & off_diagonal, local_col, blocks)] += value
        else:
            left = xs_ref[local_col]
            ends = jnp.concatenate([g_ref[s, 0, :, MAIN:], g_ref[s, 1, :, MAIN:]], axis=1)
            value = across(left[:, :MAIN], g_ref[s, 0, :, :MAIN])
            value += across(left[:, MAIN : 2 * MAIN], g_ref[s, 1, :, :MAIN])
            value += across(left[:, 2 * MAIN :], ends)
            acc_ref[jnp.where(living, place, 2 * blocks)] += value


def start_kernel(classes, small_ref, back_ref, out_ref, contrast_ref):
    blocks = out_ref.shape[0]
    cells = contrast_ref.shape[2]
    kinds = small_ref[4 : 4 + blocks, :cells]
    tables = small_ref[4 + blocks : 6 + blocks, :]
    contrast = []
    for part in range(2):
        value = jnp.zeros(kinds.shape, F32)
        for k in range(classes):
            value = jnp.where(kinds == float(k), tables[part : part + 1, k : k + 1], value)
        contrast_ref[part] = value
        contrast.append(jnp.concatenate([value] * 3, axis=1))
    real, imag = contrast
    for q in range(blocks):
        back = back_ref[q]
        out_ref[q] = (real[q : q + 1] * back + imag[q : q + 1] * turned(back)).astype(BF)


def share_kernel(table_ref, contrast_ref, back_ref, _, extra_ref):
    r = table_ref[2, 0].astype(jnp.int32)
    blocks, rows, _ = back_ref.shape
    half = rows // 2
    cells = contrast_ref.shape[2]
    for q in range(blocks):
        rest = jnp.where(r == 2, contrast_ref[1, q : q + 1], contrast_ref[0, q : q + 1])
        marks = []
        for _ in range(3):
            piece = rest.astype(BF).astype(F32)
            marks.append(piece)
            rest = rest - piece
        marks = jnp.concatenate(marks + [jnp.zeros((1, cells), F32)], axis=0)
        marks = jnp.concatenate([marks, jnp.zeros((4, LANES - cells), F32)], axis=1)
        value = jnp.where(r % 2 == 0, back_ref[q, :half, :MAIN], back_ref[q, half:, :MAIN])
        high = value.astype(BF).astype(F32)
        value = jnp.where(r < 2, high, value - high)
        ends = jnp.concatenate([back_ref[q, :half, MAIN:], back_ref[q, half:, MAIN:]], axis=1)
        high = ends.astype(BF).astype(F32)
        ends = jnp.concatenate([high, ends - high], axis=1)
        for g in range(half // 4):
            at = slice(4 * g, 4 * g + 4)
            d = q * (half // 4) + g
            extra_ref[d, :, :MAIN] = value[at].astype(BF)
            extra_ref[d, :, MAIN:] = jnp.where(r == 0, ends[at], marks).astype(BF)


def direct_kernel(first, count_ref, table_ref, g_ref, x_ref, own_ref, other_ref, xs_ref, acc_ref):
    blocks = own_ref.shape[0]
    if first:
        copy_in(x_ref, xs_ref, 0, False)
    else:
        for q in range(blocks):
            unpack_half(x_ref, q, 0, xs_ref, q)
    slot_products(count_ref, table_ref, g_ref, xs_ref, acc_ref, False, 0)
    for q in range(blocks):
        own_ref[q] = acc_ref[q]
        other_ref[q] = acc_ref[blocks + q]


def mirror_kernel(first, cols, count_ref, table_ref, g_ref, x_ref, x_other_ref, out_ref, xs_ref, acc_ref):
    blocks = out_ref.shape[0]
    if first:
        copy_in(x_ref, xs_ref, 0, True)
        copy_in(x_other_ref, xs_ref, blocks, True)
    else:
        for q in range(blocks):
            unpack_half(x_ref, q, 1, xs_ref, q)
            unpack_half(x_other_ref, q, 1, xs_ref, blocks + q)
    slot_products(count_ref, table_ref, g_ref, xs_ref, acc_ref, True, cols)
    for q in range(blocks):
        out_ref[q] = acc_ref[q]


def pack_kernel(mirror_ref, own_ref, got_ref, *rest):
    msg_ref = rest[-1]
    blocks, rows, _ = own_ref.shape
    half = rows // 2
    for q in range(blocks):
        halves = [own_ref[q] + got_ref[q], mirror_ref[q]]
        parts = [value[p * half : (p + 1) * half] for value in halves for p in range(2)]
        ends = jnp.concatenate([part[:, MAIN:] for part in parts], axis=1)
        for g in range(half // 4):
            at = slice(4 * g, 4 * g + 4)
            d = q * (half // 4) + g
            for k, part in enumerate(parts):
                msg_ref[d, :, k * MAIN : (k + 1) * MAIN] = part[at, :MAIN].astype(BF)
            msg_ref[d, :, ENDS:WIDTH] = ends[at].astype(BF)
    if len(rest) == 2:
        msg_ref[:, :, WIDTH:] = rest[0][...]


def partial_sums(msg_ref, rows, cols):
    direct = {}
    mirror = {}

    def add(store, key, value):
        store[key] = store[key] + value if key in store else value

    for r in range(rows):
        for c in range(cols):
            d = r * cols + c
            j = 2 * r + c % 2
            for k in range(9):
                value = msg_ref[d, :, k * LANES : (k + 1) * LANES].astype(F32)
                if k < 4 or k == 8:
                    add(direct, (j, min(k, 4)), value)
                if k >= 4:
                    add(mirror, (c, k - 4), value)
    for j in range(cols):
        mirror[j, 4] = shifted(mirror[j, 4], 2 * TAIL)
    return {key: direct[key] + mirror[key] for key in direct}


def update_kernel(first, rows, cols, msg_ref, *refs):
    back_ref, contrast_ref, out_ref = refs[1:] + refs[:1] if first else refs
    lane = lax.broadcasted_iota(jnp.int32, (4, LANES), 1)
    cells = (MAIN + TAIL) // 3
    sums = partial_sums(msg_ref, rows, cols)
    current = {}
    for j in range(cols):
        if first:
            extra = [
                [msg_ref[r * cols + j, :, WIDTH + k * LANES : WIDTH + (k + 1) * LANES].astype(F32) for k in range(3)]
                for r in range(4)
            ]
            back = [extra[p][k] + extra[p + 2][k] for p in range(2) for k in range(2)]
            back.append(extra[0][2] + shifted(extra[0][2], 2 * TAIL))
            contrast = []
            for r in (1, 2):
                value = extra[r][2]
                value = jnp.broadcast_to(value[0:1] + value[1:2] + value[2:3], (4, LANES))
                moved = [value, shifted(value, TAIL), shifted(value, 2 * TAIL)]
                contrast.append(
                    [
                        jnp.where(lane < cells, moved[0], shifted(value, TAIL)),
                        jnp.where(lane < 2 * TAIL, moved[1], moved[2]),
                        jnp.where(lane < TAIL, moved[2], moved[1]),
                    ]
                )
            for k in range(5):
                back_ref[j, k] = back[k]
            for part in range(2):
                for k in range(3):
                    contrast_ref[j, part, k] = contrast[part][k]
        else:
            back = [back_ref[j, k] for k in range(5)]
            contrast = [[contrast_ref[j, part, k] for k in range(3)] for part in range(2)]
        total = [sums[j, k] + back[k] for k in range(5)]
        real, imag = contrast
        for k in range(2):
            current[j, k] = real[k] * total[k] - imag[k] * total[k + 2]
            current[j, k + 2] = real[k] * total[k + 2] + imag[k] * total[k]
        other = jnp.where(lane < TAIL, -shifted(total[4], TAIL), pltpu.roll(total[4], TAIL, 1))
        current[j, 4] = real[2] * total[4] + imag[2] * other
    for r in range(rows):
        for c in range(cols):
            d = r * cols + c
            j = 2 * r + c % 2
            for k in range(4):
                out_ref[d, :, k * LANES : (k + 1) * LANES] = current[c, k].astype(BF)
                out_ref[d, :, (k + 4) * LANES : (k + 5) * LANES] = current[j, k].astype(BF)
            ends = jnp.where(lane < 2 * TAIL, current[c, 4], shifted(current[j, 4], 2 * TAIL))
            out_ref[d, :, ENDS:WIDTH] = ends.astype(BF)


def last_kernel(rows, cols, msg_ref, out_ref):
    lane = lax.broadcasted_iota(jnp.int32, (4, LANES), 1)
    sums = partial_sums(msg_ref, rows, cols)
    for j in range(cols):
        ends = sums[j, 4]
        coded_ends = jnp.zeros((4, LANES), F32)
        for p in range(2):
            mine = (lane >= p * TAIL) & (lane < (p + 1) * TAIL)
            main = [sums[j, 2 * p], sums[j, 2 * p + 1]]
            most = jnp.maximum(jnp.maximum(jnp.abs(main[0]), jnp.abs(main[1])), jnp.where(mine, jnp.abs(ends), 0.0))
            most = jnp.max(most, axis=1, keepdims=True)
            power = jnp.floor(jnp.log2(jnp.maximum(most, SMALLEST)))
            scale = jnp.exp2(14.0 - power)
            for k in range(2):
                coded = as_integers(main[k] * scale)
                for r in range(rows):
                    out_ref[r * cols + j, :, (2 * p + k) * LANES : (2 * p + k + 1) * LANES] = coded
            coded_ends = jnp.where(mine, ends * scale, jnp.where(lane == 2 * TAIL + p, power, coded_ends))
        coded = as_integers(coded_ends)
        for r in range(rows):
            out_ref[r * cols + j, :, 2 * MAIN : 2 * MAIN + LANES] = coded


def as_integers(value):
    return jnp.clip(jnp.round(value), -32767.0, 32767.0).astype(jnp.int32).astype(jnp.int16)


def finish_kernel(msg_ref, back_ref, out_ref):
    blocks, rows, _ = out_ref.shape
    half = rows // 2
    groups = half // 4

    def rows_of(q, lanes):
        pieces = [msg_ref[q * groups + g, :, lanes].astype(jnp.int32).astype(F32) for g in range(groups)]
        return jnp.concatenate(pieces, axis=0)

    for q in range(blocks):
        ends = rows_of(q, slice(2 * MAIN, 2 * MAIN + LANES))
        for p in range(2):
            at = slice(p * half, (p + 1) * half)
            scale = jnp.exp2(ends[:, 2 * TAIL + p : 2 * TAIL + p + 1] - 14.0)
            main = rows_of(q, slice(p * MAIN, (p + 1) * MAIN))
            out_ref[q, at, :MAIN] = back_ref[q, at, :MAIN] + main * scale
            out_ref[q, at, MAIN:] = back_ref[q, at, MAIN:] + shifted(ends, p * TAIL)[:, :TAIL] * scale


def whole_call(kernel, out_shape, spaces, operands, scratch, name):
    spaces = list(spaces) + [pltpu.VMEM] * (len(operands) - len(spaces))
    return pl.pallas_call(
        kernel,
        out_shape=out_shape,
        in_specs=[pl.BlockSpec(memory_space=space) for space in spaces],
        out_specs=jax.tree.map(lambda _: pl.BlockSpec(memory_space=pltpu.VMEM), out_shape),
        scratch_shapes=scratch,
        compiler_params=pltpu.CompilerParams(vmem_limit_bytes=VMEM_BYTES),
        name=name,
    )(*operands)


def stacked(arrays):
    heights = [1 if array is None else array.shape[0] for array in arrays]
    total = 0
    at = 0
    for array, height in zip(arrays, heights):
        if array is not None:
            edges = ((at, sum(heights) - at - height, 0), (0, LANES - array.shape[1], 0))
            total += lax.pad(array, jnp.zeros((), array.dtype), edges).astype(F32)
        at += height
    return total


def local_owners(green_blocks, slot_rows, slot_cols, slot_count, cell_class, class_contrast, background):
    r = lax.axis_index("row")
    c = lax.axis_index("col")
    rows = lax.axis_size("row")
    cols = lax.axis_size("col")
    green = green_blocks[0, 0]
    slots, _, entries, _ = green.shape
    sources, blocks = background.shape[1:3]
    both = ("row", "col")

    small = stacked([slot_rows[0], slot_cols[0], None, None, cell_class[:, 0, :], class_contrast.T])
    line = lax.broadcasted_iota(jnp.int32, small.shape, 0)
    small = jnp.where(line == 2, r.astype(F32), jnp.where(line == 3, c.astype(F32), small))

    block = (2 * sources, entries)
    back = background[:, :, :, 0, :].transpose(2, 0, 1, 3).reshape((blocks,) + block)
    start, contrast = whole_call(
        lambda *refs: start_kernel(class_contrast.shape[0], *refs),
        (
            jax.ShapeDtypeStruct((blocks,) + block, BF),
            jax.ShapeDtypeStruct((2, blocks, entries // 3), F32),
        ),
        [],
        (small, back),
        [],
        "start",
    )

    core_pairs = [(i, i ^ 1) for i in range(cols)]
    chips = cols // 2
    arrived = []
    for hop in range(1, chips):
        pairs = []
        for a in range(rows):
            far = (a + hop) % chips
            for k in range(chips):
                for p in range(2):
                    to = {a: 2 * far + p, far: 2 * a + p}.get(k, 2 * k + 1 - p)
                    pairs.append((a * cols + 2 * k + p, a * cols + to))
        arrived.append(lax.ppermute(start, both, pairs))
    extra = whole_call(
        share_kernel,
        jax.ShapeDtypeStruct((rows * cols, 4, 3 * LANES), BF),
        [pltpu.SMEM],
        (small, contrast, back, green),
        [],
        "share",
    )
    extra, *arrived = lax.optimization_barrier((extra, *arrived))
    row_mine = start
    for hop in range(1, chips):
        row_mine = jnp.where(c // 2 == (r + hop) % chips, arrived[hop - 1], row_mine)
    row_other = lax.ppermute(row_mine, "col", core_pairs)

    part = jax.ShapeDtypeStruct((blocks,) + block, F32)
    message = jax.ShapeDtypeStruct((rows * cols, 4, WIDTH), BF)
    for step in range(PRODUCTS):
        first = step == 0
        final = step + 1 == PRODUCTS
        if first:
            direct_in, mirror_in = start, (row_mine, row_other)
        else:
            direct_in, mirror_in = x_msg, (x_msg, lax.ppermute(x_msg, "col", core_pairs))
        own, other = whole_call(
            lambda *refs, first=first: direct_kernel(first, *refs),
            (part, part),
            [pltpu.SMEM] * 2,
            (slot_count, small, green, direct_in),
            [
                pltpu.VMEM((blocks, 2 * sources, 2 * entries), BF),
                pltpu.VMEM((2 * blocks + 1,) + block, F32),
            ],
            f"direct_{step}",
        )
        got = lax.ppermute(other, "col", core_pairs)
        mirror = whole_call(
            lambda *refs, first=first: mirror_kernel(first, cols, *refs),
            part,
            [pltpu.SMEM] * 2,
            (slot_count, small, green) + mirror_in,
            [
                pltpu.VMEM((2 * blocks, 2 * sources, 2 * entries), BF),
                pltpu.VMEM((blocks + 1,) + block, F32),
            ],
            f"mirror_{step}",
        )
        y_shape = jax.ShapeDtypeStruct((rows * cols, 4, WIDTH + 3 * LANES), BF) if first else message
        operands = (mirror, own, got) + ((extra,) if first else ())
        y_msg = whole_call(pack_kernel, y_shape, [], operands, [], f"pack_{step}")
        y_msg = lax.all_to_all(y_msg, both, 0, 0, tiled=True)
        run = lambda *refs, first=first: update_kernel(first, rows, cols, *refs)
        if first:
            x_msg, owner_back, owner_contrast = whole_call(
                run,
                (
                    message,
                    jax.ShapeDtypeStruct((cols, 5, 4, LANES), F32),
                    jax.ShapeDtypeStruct((cols, 2, 3, 4, LANES), F32),
                ),
                [],
                (y_msg,),
                [],
                f"update_{step}",
            )
        elif not final:
            operands = (y_msg, owner_back, owner_contrast)
            x_msg = whole_call(run, message, [], operands, [], f"update_{step}")
        else:
            run = lambda *refs: last_kernel(rows, cols, *refs)
            x_shape = jax.ShapeDtypeStruct((rows * cols, 4, 2 * MAIN + LANES), jnp.int16)
            x_msg = whole_call(run, x_shape, [], (y_msg,), [], "last")
        x_msg = lax.all_to_all(x_msg, both, 0, 0, tiled=True)
    field = whole_call(finish_kernel, part, [], (x_msg, back), [], "finish")
    field = field.reshape(blocks, 2, sources, entries).transpose(1, 2, 0, 3)
    return field[:, :, :, None, :]


def solution(mesh):
    in_specs = (
        P("row", "col", None, None, None, None),
        P("row", "col", None),
        P("row", "col", None),
        P("row", "col"),
        P(None, "col", None),
        P(),
        P(None, None, None, "col", None),
    )
    out_specs = P(None, None, None, "col", None)
    rows, cols = mesh.shape["row"], mesh.shape["col"]

    def local(*args):
        sources, blocks = args[6].shape[1:3]
        entries = args[6].shape[4]
        owners = (
            rows == blocks == 4
            and cols == 2 * rows
            and sources == 4 * cols
            and max(args[5].shape[0], args[1].shape[2]) <= LANES
            and entries == 2 * LANES + LANES // 4 == 3 * args[4].shape[2]
        )
        return (local_owners if owners else local_general)(*args)

    return jax.shard_map(local, mesh=mesh, in_specs=in_specs, out_specs=out_specs, check_vma=False)
```

time: 119 us -> 115 us (0.966)
  blocking collectives: 86.5 us -> 83.4 us
    all_to_all x3, blocking collectives: 39.8 us -> 38 us  [local_owners(): x_msg = lax.all_to_all(x_msg, both, 0, 0, tiled=True)]
    all_to_all x3, blocking collectives: 46.8 us -> 45.4 us  [local_owners(): y_msg = lax.all_to_all(y_msg, both, 0, 0, tiled=True)]
    reshape x3 -> x1, local copies, waits for them, and re-layouts: 1.45 us -> 0.26 us  [local_owners(): field = field.reshape(blocks, 2, sources, entries).transpose(1, 2, 0, 3)]
where the time goes in v4:
time: 115 us
  blocking collectives  83.4 us (73%)
  Pallas kernels  15.5 us (13%)
  local copies, waits for them, and re-layouts  7.4 us (6%)
  starting transfers between devices  5.64 us (5%)
  waiting for transfers between devices  1.16 us (1%)
    all_to_all x3, blocking collectives, local_owners(): y_msg = lax.all_to_all(y_msg, both, 0, 0, tiled=True)  45.4 us
    all_to_all x3, blocking collectives, local_owners(): x_msg = lax.all_to_all(x_msg, both, 0, 0, tiled=True)  38 us
    pallas_call x15, Pallas kernels, whole_call(): pl.pallas_call(kernel, out_shape=out_shape, in_specs=[pl.BlockSpec(memory...  15.5 us
    unnamed x7, local copies, waits for them, and re-layouts  6.1 us
    ppermute x3, starting transfers between devices, local_owners(): arrived.append(lax.ppermute(start, both, pairs))  3.96 us
  transfers between devices with their start and end apart: 9, of which 2 were waited for; matrix products, arithmetic and copies ran while one was open for 0% of the time, Pallas kernels for 12%

profile of v4, /device:TPU:0, one launch (start us, length us, event | category | flops | bytes accessed | tf_op | source)
XLA Modules:
  0.0 114.9 jit_solution(7858674896323104843)
XLA Ops:
  0.0 1.1 copy.13
  1.1 0.8 select_select_fusion.1.refs_0_.table_ref.refs_1_
  1.9 0.3 start.1
  2.2 4.0 %collective-permute-start.2 = (bf16[4,64,288]{2,1,0:T(8,128)(2,1)S(1)}, bf16[4,64,288]{2,1,0:T(8,128)(2,1)S(1)}, u32[]{:S(2)}, u32[]{:S(2)}) collective-permute-start(bf16[4,64,288]{2,1,0:T(8,128)(2,1)S(1)} %get-tuple-element.21.refs_3_), channel_id=1, source_target_pairs={{0,6},{1,7},{2,3},{3,2},{4,5},{5,4},{6,0},{7,1},{8,10},{9,11},{10,... | collective-permute-start | bytes 442376 | tf_op jit(solution)/shard_map/ppermute | solution.py:448
  6.2 0.0 collective-permute-start.1
  6.2 0.0 collective-permute-start
  6.8 0.0 copy-start
  6.8 2.5 %copy-done = bf16[1,1,12,2,288,288]{5,4,3,2,1,0:T(8,128)(2,1)S(1)} copy-done((bf16[1,1,12,2,288,288]{5,4,3,2,1,0:T(8,128)(2,1)S(1)}, bf16[1,1,12,2,288,288]{5,4,3,2,1,0:T(8,128)(2,1)}, u32[]{:S(2)}) %copy-start) | copy-done | bytes 3981336
  9.3 2.4 %direct_0.1 = (f32[4,64,288]{2,1,0:T(8,128)S(1)}, f32[4,64,288]{2,1,0:T(8,128)S(1)}) custom-call(s32[1,1]{1,0:T(1,128)S(6)} %copy.15.refs_0_, f32[10,128]{1,0:T(8,128)S(1)} %select_select_fusion.1.refs_0_.table_ref.refs_1_, bf16[12,2,288,288]{3,2,1,0:T(8,128)(2,1)S(1)} %bitcast.15, bf16[4,64,288]{2,1,0:T(8,128)(2,1)S(1)} %get-tuple-element.21.refs_3_), custom_call_target="tpu_custom_call" | custom-call | tf_op jit(solution)/shard_map/direct_0/pallas_call | solution.py:386
  11.7 0.1 collective-permute-start.4
  11.8 0.0 copy-start.1
  11.9 2.5 %copy-done.1 = bf16[1,1,12,2,288,288]{5,4,3,2,1,0:T(8,128)(2,1)S(1)} copy-done((bf16[1,1,12,2,288,288]{5,4,3,2,1,0:T(8,128)(2,1)S(1)}, bf16[1,1,12,2,288,288]{5,4,3,2,1,0:T(8,128)(2,1)}, u32[]{:S(2)}) %copy-start.1) | copy-done | bytes 3981336
  14.4 0.8 share.1.rest_0_
  15.2 0.0 collective-permute-done.2
  15.2 0.1 collective-permute-done.1
  15.3 0.0 collective-permute-done
  15.3 0.1 select_select_fusion.refs_3_
  15.3 0.5 collective-permute-start.3
  15.8 1.1 collective-permute-done.3.refs_4_
  16.9 1.9 %mirror_0.1.mirror_ref = f32[4,64,288]{2,1,0:T(8,128)S(1)} custom-call(s32[1,1]{1,0:T(1,128)S(6)} %copy.15.refs_0_, f32[10,128]{1,0:T(8,128)S(1)} %select_select_fusion.1.refs_0_.table_ref.refs_1_, bf16[12,2,288,288]{3,2,1,0:T(8,128)(2,1)S(1)} %bitcast.17, bf16[4,64,288]{2,1,0:T(8,128)(2,1)S(1)} %select_select_fusion.refs_3_, ...), custom_call_target="tpu_custom_call" | custom-call | tf_op jit(solution)/shard_map/mirror_0/pallas_call | solution.py:386
  18.8 0.0 collective-permute-done.4.got_ref
  18.8 0.1 pack_0.1
  18.9 18.4 %all_to_all.30.refs_0_ = bf16[32,4,1536]{2,1,0:T(4,128)(2,1)S(1)} all-to-all(bf16[32,4,1536]{2,1,0:T(4,128)(2,1)S(1)} %pack_0.1), channel_id=1, replica_groups=mesh['row'=4,'col'=8] {'row','col'}, dimensions={0} | all-to-all | bytes 786432 | tf_op jit(solution)/shard_map/all_to_all | solution.py:498
  37.3 0.3 update_0.1
  37.5 13.8 %all_to_all.31.refs_3_ = bf16[32,4,1152]{2,1,0:T(4,128)(2,1)S(1)} all-to-all(bf16[32,4,1152]{2,1,0:T(4,128)(2,1)S(1)} %get-tuple-element.28), channel_id=1, replica_groups=mesh['row'=4,'col'=8] {'row','col'}, dimensions={0} | all-to-all | bytes 589824 | tf_op jit(solution)/shard_map/all_to_all | solution.py:520
  51.4 0.0 collective-permute-start.5
  51.4 2.5 %direct_1.1 = (f32[4,64,288]{2,1,0:T(8,128)S(1)}, f32[4,64,288]{2,1,0:T(8,128)S(1)}) custom-call(s32[1,1]{1,0:T(1,128)S(6)} %copy.15.refs_0_, f32[10,128]{1,0:T(8,128)S(1)} %select_select_fusion.1.refs_0_.table_ref.refs_1_, bf16[12,2,288,288]{3,2,1,0:T(8,128)(2,1)S(1)} %bitcast.18, bf16[32,4,1152]{2,1,0:T(4,128)(2,1)S(1)} %all_to_all.31.refs_3_), custom_call_target="tpu_custom_call" | custom-call | tf_op jit(solution)/shard_map/direct_1/pallas_call | solution.py:386
  53.9 0.6 collective-permute-start.6
  54.4 0.0 collective-permute-done.5.refs_4_
  54.4 2.0 %mirror_1.1.mirror_ref = f32[4,64,288]{2,1,0:T(8,128)S(1)} custom-call(s32[1,1]{1,0:T(1,128)S(6)} %copy.15.refs_0_, f32[10,128]{1,0:T(8,128)S(1)} %select_select_fusion.1.refs_0_.table_ref.refs_1_, bf16[12,2,288,288]{3,2,1,0:T(8,128)(2,1)S(1)} %bitcast.19, bf16[32,4,1152]{2,1,0:T(4,128)(2,1)S(1)} %all_to_all.31.refs_3_, ...), custom_call_target="tpu_custom_call" | custom-call | tf_op jit(solution)/shard_map/mirror_1/pallas_call | solution.py:386
  56.4 0.0 collective-permute-done.6.got_ref
  56.4 0.1 pack_1.1
  56.5 13.5 %all_to_all.32.refs_0_ = bf16[32,4,1152]{2,1,0:T(4,128)(2,1)S(1)} all-to-all(bf16[32,4,1152]{2,1,0:T(4,128)(2,1)S(1)} %pack_1.1), channel_id=1, replica_groups=mesh['row'=4,'col'=8] {'row','col'}, dimensions={0} | all-to-all | bytes 589824 | tf_op jit(solution)/shard_map/all_to_all | solution.py:498
  70.1 0.3 update_1.1
  70.4 13.5 %all_to_all.33.refs_3_ = bf16[32,4,1152]{2,1,0:T(4,128)(2,1)S(1)} all-to-all(bf16[32,4,1152]{2,1,0:T(4,128)(2,1)S(1)} %update_1.1), channel_id=1, replica_groups=mesh['row'=4,'col'=8] {'row','col'}, dimensions={0} | all-to-all | bytes 589824 | tf_op jit(solution)/shard_map/all_to_all | solution.py:520
  83.9 0.0 collective-permute-start.7
  83.9 2.5 %direct_2.1 = (f32[4,64,288]{2,1,0:T(8,128)S(1)}, f32[4,64,288]{2,1,0:T(8,128)S(1)}) custom-call(s32[1,1]{1,0:T(1,128)S(6)} %copy.15.refs_0_, f32[10,128]{1,0:T(8,128)S(1)} %select_select_fusion.1.refs_0_.table_ref.refs_1_, bf16[12,2,288,288]{3,2,1,0:T(8,128)(2,1)S(1)} %bitcast.20, bf16[32,4,1152]{2,1,0:T(4,128)(2,1)S(1)} %all_to_all.33.refs_3_), custom_call_target="tpu_custom_call" | custom-call | tf_op jit(solution)/shard_map/direct_2/pallas_call | solution.py:386
  86.4 0.6 collective-permute-start.8
  86.9 0.0 collective-permute-done.7.refs_4_
  86.9 2.0 %mirror_2.1.mirror_ref = f32[4,64,288]{2,1,0:T(8,128)S(1)} custom-call(s32[1,1]{1,0:T(1,128)S(6)} %copy.15.refs_0_, f32[10,128]{1,0:T(8,128)S(1)} %select_select_fusion.1.refs_0_.table_ref.refs_1_, bf16[12,2,288,288]{3,2,1,0:T(8,128)(2,1)S(1)} %bitcast.21, bf16[32,4,1152]{2,1,0:T(4,128)(2,1)S(1)} %all_to_all.33.refs_3_, ...), custom_call_target="tpu_custom_call" | custom-call | tf_op jit(solution)/shard_map/mirror_2/pallas_call | solution.py:386
  88.9 0.0 collective-permute-done.8.got_ref
  88.9 0.1 pack_2.1
  89.1 13.5 %all_to_all.34.refs_0_ = bf16[32,4,1152]{2,1,0:T(4,128)(2,1)S(1)} all-to-all(bf16[32,4,1152]{2,1,0:T(4,128)(2,1)S(1)} %pack_2.1), channel_id=1, replica_groups=mesh['row'=4,'col'=8] {'row','col'}, dimensions={0} | all-to-all | bytes 589824 | tf_op jit(solution)/shard_map/all_to_all | solution.py:498
  102.6 0.2 last.1
  102.8 10.7 %all_to_all.35.msg_ref = s16[32,4,640]{2,1,0:T(4,128)(2,1)S(1)} all-to-all(s16[32,4,640]{2,1,0:T(4,128)(2,1)S(1)} %last.1), channel_id=1, replica_groups=mesh['row'=4,'col'=8] {'row','col'}, dimensions={0} | all-to-all | bytes 327680 | tf_op jit(solution)/shard_map/all_to_all | solution.py:520
  113.5 0.1 finish.1
  113.6 0.3 copy.14
  113.9 1.0 broadcast_in_dim.12
  (4 shorter events, 0.0 us)
Async XLA Ops:
  2.2 13.0 %collective-permute-start.2 = (bf16[4,64,288]{2,1,0:T(8,128)(2,1)S(1)}, bf16[4,64,288]{2,1,0:T(8,128)(2,1)S(1)}, u32[]{:S(2)}, u32[]{:S(2)}) collective-permute-start(bf16[4,64,288]{2,1,0:T(8,128)(2,1)S(1)} %get-tuple-element.21.refs_3_), channel_id=1, source_target_pairs={{0,6},{1,7},{2,3},{3,2},{4,5},{5,4},{6,0},{7,1},{8,10},{9,11},{10,... | collective-permute-start | bytes 442376 | tf_op jit(solution)/shard_map/ppermute | solution.py:448
  6.2 9.1 %collective-permute-start.1 = (bf16[4,64,288]{2,1,0:T(8,128)(2,1)S(1)}, bf16[4,64,288]{2,1,0:T(8,128)(2,1)S(1)}, u32[]{:S(2)}, u32[]{:S(2)}) collective-permute-start(bf16[4,64,288]{2,1,0:T(8,128)(2,1)S(1)} %get-tuple-element.21.refs_3_), channel_id=1, source_target_pairs={{0,4},{1,5},{2,3},{3,2},{4,0},{5,1},{6,7},{7,6},{8,9},{9,8},{10,14... | collective-permute-start | bytes 442376 | tf_op jit(solution)/shard_map/ppermute | solution.py:448
  6.2 9.1 %collective-permute-start = (bf16[4,64,288]{2,1,0:T(8,128)(2,1)S(1)}, bf16[4,64,288]{2,1,0:T(8,128)(2,1)S(1)}, u32[]{:S(2)}, u32[]{:S(2)}) collective-permute-start(bf16[4,64,288]{2,1,0:T(8,128)(2,1)S(1)} %get-tuple-element.21.refs_3_), channel_id=1, source_target_pairs={{0,2},{1,3},{2,0},{3,1},{4,5},{5,4},{6,7},{7,6},{8,9},{9,8},{10,12... | collective-permute-start | bytes 442376 | tf_op jit(solution)/shard_map/ppermute | solution.py:448
  6.8 2.5 %copy-start = (bf16[1,1,12,2,288,288]{5,4,3,2,1,0:T(8,128)(2,1)S(1)}, bf16[1,1,12,2,288,288]{5,4,3,2,1,0:T(8,128)(2,1)}, u32[]{:S(2)}) copy-start(bf16[1,1,12,2,288,288]{5,4,3,2,1,0:T(8,128)(2,1)} %param.7) | copy-start | bytes 11943940
  11.7 7.1 %collective-permute-start.4 = (f32[4,64,288]{2,1,0:T(8,128)S(1)}, f32[4,64,288]{2,1,0:T(8,128)S(1)}, u32[]{:S(2)}, u32[]{:S(2)}) collective-permute-start(f32[4,64,288]{2,1,0:T(8,128)S(1)} %get-tuple-element.26), channel_id=1, source_target_pairs={{0,1},{1,0},{2,3},{3,2},{4,5},{5,4},{6,7},{7,6},{8,9},{9,8},{10,11... | collective-permute-start | bytes 884744 | tf_op jit(solution)/shard_map/ppermute | solution.py:483
  11.8 2.5 %copy-start.1 = (bf16[1,1,12,2,288,288]{5,4,3,2,1,0:T(8,128)(2,1)S(1)}, bf16[1,1,12,2,288,288]{5,4,3,2,1,0:T(8,128)(2,1)}, u32[]{:S(2)}) copy-start(bf16[1,1,12,2,288,288]{5,4,3,2,1,0:T(8,128)(2,1)} %param.7) | copy-start | bytes 11943940
  14.4 2.5 %copy-start.2 = (bf16[1,1,12,2,288,288]{5,4,3,2,1,0:T(8,128)(2,1)S(1)}, bf16[1,1,12,2,288,288]{5,4,3,2,1,0:T(8,128)(2,1)}, u32[]{:S(2)}) copy-start(bf16[1,1,12,2,288,288]{5,4,3,2,1,0:T(8,128)(2,1)} %param.7) | copy-start | bytes 11943940
  15.3 1.5 %collective-permute-start.3 = (bf16[4,64,288]{2,1,0:T(8,128)(2,1)S(1)}, bf16[4,64,288]{2,1,0:T(8,128)(2,1)S(1)}, u32[]{:S(2)}, u32[]{:S(2)}) collective-permute-start(bf16[4,64,288]{2,1,0:T(8,128)(2,1)S(1)} %select_select_fusion.refs_3_), channel_id=1, source_target_pairs={{0,1},{1,0},{2,3},{3,2},{4,5},{5,4},{6,7},{7,6},{8,9},{9,8},{10,11... | collective-permute-start | bytes 442376 | tf_op jit(solution)/shard_map/ppermute | solution.py:461
  51.4 3.0 %collective-permute-start.5 = (bf16[32,4,1152]{2,1,0:T(4,128)(2,1)S(1)}, bf16[32,4,1152]{2,1,0:T(4,128)(2,1)S(1)}, u32[]{:S(2)}, u32[]{:S(2)}) collective-permute-start(bf16[32,4,1152]{2,1,0:T(4,128)(2,1)S(1)} %all_to_all.31.refs_3_), channel_id=1, source_target_pairs={{0,1},{1,0},{2,3},{3,2},{4,5},{5,4},{6,7},{7,6},{8,9},{9,8},{10,11... | collective-permute-start | bytes 884744 | tf_op jit(solution)/shard_map/ppermute | solution.py:471
  53.9 2.6 %collective-permute-start.6 = (f32[4,64,288]{2,1,0:T(8,128)S(1)}, f32[4,64,288]{2,1,0:T(8,128)S(1)}, u32[]{:S(2)}, u32[]{:S(2)}) collective-permute-start(f32[4,64,288]{2,1,0:T(8,128)S(1)} %get-tuple-element.30), channel_id=1, source_target_pairs={{0,1},{1,0},{2,3},{3,2},{4,5},{5,4},{6,7},{7,6},{8,9},{9,8},{10,11... | collective-permute-start | bytes 884744 | tf_op jit(solution)/shard_map/ppermute | solution.py:483
  83.9 3.0 %collective-permute-start.7 = (bf16[32,4,1152]{2,1,0:T(4,128)(2,1)S(1)}, bf16[32,4,1152]{2,1,0:T(4,128)(2,1)S(1)}, u32[]{:S(2)}, u32[]{:S(2)}) collective-permute-start(bf16[32,4,1152]{2,1,0:T(4,128)(2,1)S(1)} %all_to_all.33.refs_3_), channel_id=1, source_target_pairs={{0,1},{1,0},{2,3},{3,2},{4,5},{5,4},{6,7},{7,6},{8,9},{9,8},{10,11... | collective-permute-start | bytes 884744 | tf_op jit(solution)/shard_map/ppermute | solution.py:471
  86.4 2.6 %collective-permute-start.8 = (f32[4,64,288]{2,1,0:T(8,128)S(1)}, f32[4,64,288]{2,1,0:T(8,128)S(1)}, u32[]{:S(2)}, u32[]{:S(2)}) collective-permute-start(f32[4,64,288]{2,1,0:T(8,128)S(1)} %get-tuple-element.34), channel_id=1, source_target_pairs={{0,1},{1,0},{2,3},{3,2},{4,5},{5,4},{6,7},{7,6},{8,9},{9,8},{10,11... | collective-permute-start | bytes 884744 | tf_op jit(solution)/shard_map/ppermute | solution.py:483

commit v5 on v4

--- a/solution.py
+++ b/solution.py
@@ -145,30 +145,21 @@
     return lax.dot_general(left, right, (((1,), (1,)), ((), ())), preferred_element_type=F32)
 
 
-def slot_products(count_ref, table_ref, g_ref, xs_ref, acc_ref, mirror, cols):
+def slot_products(table_ref, g_ref, xs_ref, acc_ref, mirror):
     acc_ref[...] = jnp.zeros_like(acc_ref)
     slots, _, depth, entries = g_ref.shape
-    r, c = [table_ref[row, 0].astype(jnp.int32) for row in (2, 3)]
-    count = count_ref[0, 0]
-    blocks = (acc_ref.shape[0] - 1) // (1 if mirror else 2)
+    table = table_ref[...]
+    first = 2 if mirror else 0
     for s in range(slots):
-        local_row = table_ref[0, s].astype(jnp.int32)
-        local_col = table_ref[1, s].astype(jnp.int32)
-        living = s < count
-        half = local_row // 2
-        place = (local_row % 2 ^ c % 2) * blocks + half
+        left = xs_ref[table[first, s]]
         if mirror:
-            off_diagonal = half * cols + 2 * r + local_row % 2 != local_col * cols + c
-            both = g_ref[s].reshape(2 * depth, entries)
-            value = jnp.dot(xs_ref[place], both, preferred_element_type=F32)
-            acc_ref[jnp.where(living & off_diagonal, local_col, blocks)] += value
+            value = jnp.dot(left, g_ref[s].reshape(2 * depth, entries), preferred_element_type=F32)
         else:
-            left = xs_ref[local_col]
             ends = jnp.concatenate([g_ref[s, 0, :, MAIN:], g_ref[s, 1, :, MAIN:]], axis=1)
             value = across(left[:, :MAIN], g_ref[s, 0, :, :MAIN])
             value += across(left[:, MAIN : 2 * MAIN], g_ref[s, 1, :, :MAIN])
             value += across(left[:, 2 * MAIN :], ends)
-            acc_ref[jnp.where(living, place, 2 * blocks)] += value
+        acc_ref[table[first + 1, s]] += value
 
 
 def start_kernel(classes, small_ref, back_ref, out_ref, contrast_ref):
@@ -189,8 +180,8 @@
         out_ref[q] = (real[q : q + 1] * back + imag[q : q + 1] * turned(back)).astype(BF)
 
 
-def share_kernel(table_ref, contrast_ref, back_ref, _, extra_ref):
-    r = table_ref[2, 0].astype(jnp.int32)
+def share_kernel(small_ref, contrast_ref, back_ref, _, extra_ref):
+    r = small_ref[2:3, 0:1].astype(jnp.int32)
     blocks, rows, _ = back_ref.shape
     half = rows // 2
     cells = contrast_ref.shape[2]
@@ -216,20 +207,20 @@
             extra_ref[d, :, MAIN:] = jnp.where(r == 0, ends[at], marks).astype(BF)
 
 
-def direct_kernel(first, count_ref, table_ref, g_ref, x_ref, own_ref, other_ref, xs_ref, acc_ref):
+def direct_kernel(first, table_ref, g_ref, x_ref, own_ref, other_ref, xs_ref, acc_ref):
     blocks = own_ref.shape[0]
     if first:
         copy_in(x_ref, xs_ref, 0, False)
     else:
         for q in range(blocks):
             unpack_half(x_ref, q, 0, xs_ref, q)
-    slot_products(count_ref, table_ref, g_ref, xs_ref, acc_ref, False, 0)
+    slot_products(table_ref, g_ref, xs_ref, acc_ref, False)
     for q in range(blocks):
         own_ref[q] = acc_ref[q]
         other_ref[q] = acc_ref[blocks + q]
 
 
-def mirror_kernel(first, cols, count_ref, table_ref, g_ref, x_ref, x_other_ref, out_ref, xs_ref, acc_ref):
+def mirror_kernel(first, table_ref, g_ref, x_ref, x_other_ref, out_ref, xs_ref, acc_ref):
     blocks = out_ref.shape[0]
     if first:
         copy_in(x_ref, xs_ref, 0, True)
@@ -238,7 +229,7 @@
         for q in range(blocks):
             unpack_half(x_ref, q, 1, xs_ref, q)
             unpack_half(x_other_ref, q, 1, xs_ref, blocks + q)
-    slot_products(count_ref, table_ref, g_ref, xs_ref, acc_ref, True, cols)
+    slot_products(table_ref, g_ref, xs_ref, acc_ref, True)
     for q in range(blocks):
         out_ref[q] = acc_ref[q]
 
@@ -381,13 +372,13 @@
             out_ref[q, at, MAIN:] = back_ref[q, at, MAIN:] + shifted(ends, p * TAIL)[:, :TAIL] * scale
 
 
-def whole_call(kernel, out_shape, spaces, operands, scratch, name):
-    spaces = list(spaces) + [pltpu.VMEM] * (len(operands) - len(spaces))
+def whole_call(kernel, out_shape, operands, scratch, name):
+    vmem = pl.BlockSpec(memory_space=pltpu.VMEM)
     return pl.pallas_call(
         kernel,
         out_shape=out_shape,
-        in_specs=[pl.BlockSpec(memory_space=space) for space in spaces],
-        out_specs=jax.tree.map(lambda _: pl.BlockSpec(memory_space=pltpu.VMEM), out_shape),
+        in_specs=[vmem] * len(operands),
+        out_specs=jax.tree.map(lambda _: vmem, out_shape),
         scratch_shapes=scratch,
         compiler_params=pltpu.CompilerParams(vmem_limit_bytes=VMEM_BYTES),
         name=name,
@@ -420,6 +411,22 @@
     line = lax.broadcasted_iota(jnp.int32, small.shape, 0)
     small = jnp.where(line == 2, r.astype(F32), jnp.where(line == 3, c.astype(F32), small))
 
+    local_rows = small[0:1, :].astype(jnp.int32)
+    local_cols = small[1:2, :].astype(jnp.int32)
+    living = lax.broadcasted_iota(jnp.int32, (1, LANES), 1) < slot_count
+    off_diagonal = (local_rows // 2 * cols + 2 * r + local_rows % 2) != (local_cols * cols + c)
+    place = (local_rows % 2 ^ c % 2) * blocks + local_rows // 2
+    spare = jnp.full_like(place, 2 * blocks)
+    table = jnp.concatenate(
+        [
+            local_cols,
+            jnp.where(living, place, spare),
+            place,
+            jnp.where(living & off_diagonal, local_cols, spare // 2),
+        ],
+        axis=0,
+    )
+
     block = (2 * sources, entries)
     back = background[:, :, :, 0, :].transpose(2, 0, 1, 3).reshape((blocks,) + block)
     start, contrast = whole_call(
@@ -428,7 +435,6 @@
             jax.ShapeDtypeStruct((blocks,) + block, BF),
             jax.ShapeDtypeStruct((2, blocks, entries // 3), F32),
         ),
-        [],
         (small, back),
         [],
         "start",
@@ -449,7 +455,6 @@
     extra = whole_call(
         share_kernel,
         jax.ShapeDtypeStruct((rows * cols, 4, 3 * LANES), BF),
-        [pltpu.SMEM],
         (small, contrast, back, green),
         [],
         "share",
@@ -472,8 +477,7 @@
         own, other = whole_call(
             lambda *refs, first=first: direct_kernel(first, *refs),
             (part, part),
-            [pltpu.SMEM] * 2,
-            (slot_count, small, green, direct_in),
+            (table, green, direct_in),
             [
                 pltpu.VMEM((blocks, 2 * sources, 2 * entries), BF),
                 pltpu.VMEM((2 * blocks + 1,) + block, F32),
@@ -482,10 +486,9 @@
         )
         got = lax.ppermute(other, "col", core_pairs)
         mirror = whole_call(
-            lambda *refs, first=first: mirror_kernel(first, cols, *refs),
+            lambda *refs, first=first: mirror_kernel(first, *refs),
             part,
-            [pltpu.SMEM] * 2,
-            (slot_count, small, green) + mirror_in,
+            (table, green) + mirror_in,
             [
                 pltpu.VMEM((2 * blocks, 2 * sources, 2 * entries), BF),
                 pltpu.VMEM((blocks + 1,) + block, F32),
@@ -494,7 +497,7 @@
         )
         y_shape = jax.ShapeDtypeStruct((rows * cols, 4, WIDTH + 3 * LANES), BF) if first else message
         operands = (mirror, own, got) + ((extra,) if first else ())
-        y_msg = whole_call(pack_kernel, y_shape, [], operands, [], f"pack_{step}")
+        y_msg = whole_call(pack_kernel, y_shape, operands, [], f"pack_{step}")
         y_msg = lax.all_to_all(y_msg, both, 0, 0, tiled=True)
         run = lambda *refs, first=first: update_kernel(first, rows, cols, *refs)
         if first:
@@ -505,20 +508,19 @@
                     jax.ShapeDtypeStruct((cols, 5, 4, LANES), F32),
                     jax.ShapeDtypeStruct((cols, 2, 3, 4, LANES), F32),
                 ),
-                [],
                 (y_msg,),
                 [],
                 f"update_{step}",
             )
         elif not final:
             operands = (y_msg, owner_back, owner_contrast)
-            x_msg = whole_call(run, message, [], operands, [], f"update_{step}")
+            x_msg = whole_call(run, message, operands, [], f"update_{step}")
         else:
             run = lambda *refs: last_kernel(rows, cols, *refs)
             x_shape = jax.ShapeDtypeStruct((rows * cols, 4, 2 * MAIN + LANES), jnp.int16)
-            x_msg = whole_call(run, x_shape, [], (y_msg,), [], "last")
+            x_msg = whole_call(run, x_shape, (y_msg,), [], "last")
         x_msg = lax.all_to_all(x_msg, both, 0, 0, tiled=True)
-    field = whole_call(finish_kernel, part, [], (x_msg, back), [], "finish")
+    field = whole_call(finish_kernel, part, (x_msg, back), [], "finish")
     field = field.reshape(blocks, 2, sources, entries).transpose(1, 2, 0, 3)
     return field[:, :, :, None, :]
 

time: 115 us -> 112 us (0.974)
  Pallas kernels: 15.5 us -> 11.2 us
  waiting for transfers between devices: 1.16 us -> 2.7 us
    pallas_call x15, Pallas kernels: 15.5 us -> 11.2 us  [whole_call(): pl.pallas_call(kernel, out_shape=out_shape, in_specs=[vmem] * len(operand...]
    ppermute x3, waiting for transfers between devices: 0.08 us -> 1.23 us  [local_owners(): arrived.append(lax.ppermute(start, both, pairs))]
  transfers between devices with their start and end apart: 9 -> 9, of which waited for: 2 -> 2; matrix products, arithmetic and copies ran while one was open for 0% -> 0% of each run, Pallas kernels for 12% -> 9%
where the time goes in v5:
time: 112 us
  blocking collectives  83.5 us (75%)
  Pallas kernels  11.2 us (10%)
  local copies, waits for them, and re-layouts  7.4 us (7%)
  starting transfers between devices  5.26 us (5%)
  waiting for transfers between devices  2.7 us (2%)
    all_to_all x3, blocking collectives, local_owners(): y_msg = lax.all_to_all(y_msg, both, 0, 0, tiled=True)  45.4 us
    all_to_all x3, blocking collectives, local_owners(): x_msg = lax.all_to_all(x_msg, both, 0, 0, tiled=True)  38 us
    pallas_call x15, Pallas kernels, whole_call(): pl.pallas_call(kernel, out_shape=out_shape, in_specs=[vmem] * len(operand...  11.2 us
    unnamed x7, local copies, waits for them, and re-layouts  6.1 us
    ppermute x3, starting transfers between devices, local_owners(): arrived.append(lax.ppermute(start, both, pairs))  3.96 us
  transfers between devices with their start and end apart: 9, of which 2 were waited for; matrix products, arithmetic and copies ran while one was open for 0% of the time, Pallas kernels for 9%

profile of v5, /device:TPU:0, one launch (start us, length us, event | category | flops | bytes accessed | tf_op | source)
XLA Modules:
  0.0 111.8 jit_solution(14412133850061176226)
XLA Ops:
  0.0 1.1 copy.13
  1.1 0.8 select_select_fusion.1.refs_0_.small_ref
  1.9 0.3 start.1
  2.2 4.0 %collective-permute-start.2 = (bf16[4,64,288]{2,1,0:T(8,128)(2,1)S(1)}, bf16[4,64,288]{2,1,0:T(8,128)(2,1)S(1)}, u32[]{:S(2)}, u32[]{:S(2)}) collective-permute-start(bf16[4,64,288]{2,1,0:T(8,128)(2,1)S(1)} %get-tuple-element.21.refs_2_), channel_id=1, source_target_pairs={{0,6},{1,7},{2,3},{3,2},{4,5},{5,4},{6,0},{7,1},{8,10},{9,11},{10,... | collective-permute-start | bytes 442376 | tf_op jit(solution)/shard_map/ppermute | solution.py:454
  6.2 0.0 collective-permute-start.1
  6.2 0.0 collective-permute-start
  6.9 0.0 copy-start
  6.9 2.5 %copy-done = bf16[1,1,12,2,288,288]{5,4,3,2,1,0:T(8,128)(2,1)S(1)} copy-done((bf16[1,1,12,2,288,288]{5,4,3,2,1,0:T(8,128)(2,1)S(1)}, bf16[1,1,12,2,288,288]{5,4,3,2,1,0:T(8,128)(2,1)}, u32[]{:S(2)}) %copy-start) | copy-done | bytes 3981336
  9.4 1.8 %direct_0.1 = (f32[4,64,288]{2,1,0:T(8,128)S(1)}, f32[4,64,288]{2,1,0:T(8,128)S(1)}) custom-call(s32[4,128]{1,0:T(4,128)S(1)} %pad_add_fusion.refs_0_, bf16[12,2,288,288]{3,2,1,0:T(8,128)(2,1)S(1)} %bitcast.18, bf16[4,64,288]{2,1,0:T(8,128)(2,1)S(1)} %get-tuple-element.21.refs_2_), custom_call_target="tpu_custom_call" | custom-call | tf_op jit(solution)/shard_map/direct_0/pallas_call | solution.py:377
  11.2 0.1 collective-permute-start.4
  11.4 0.0 copy-start.1
  11.4 2.5 %copy-done.1 = bf16[1,1,12,2,288,288]{5,4,3,2,1,0:T(8,128)(2,1)S(1)} copy-done((bf16[1,1,12,2,288,288]{5,4,3,2,1,0:T(8,128)(2,1)S(1)}, bf16[1,1,12,2,288,288]{5,4,3,2,1,0:T(8,128)(2,1)}, u32[]{:S(2)}) %copy-start.1) | copy-done | bytes 3981336
  13.9 0.2 share.1.rest_0_
  14.0 0.0 collective-permute-done.2
  14.0 1.2 %collective-permute-done.1 = bf16[4,64,288]{2,1,0:T(8,128)(2,1)S(1)} collective-permute-done((bf16[4,64,288]{2,1,0:T(8,128)(2,1)S(1)}, bf16[4,64,288]{2,1,0:T(8,128)(2,1)S(1)}, u32[]{:S(2)}, u32[]{:S(2)}) %collective-permute-start.1) | collective-permute-done | bytes 147488 | tf_op jit(solution)/shard_map/ppermute | solution.py:454
  15.3 0.0 collective-permute-done
  15.3 0.1 collective-permute-start.3
  15.4 1.4 %collective-permute-done.3.refs_3_ = bf16[4,64,288]{2,1,0:T(8,128)(2,1)S(1)} collective-permute-done((bf16[4,64,288]{2,1,0:T(8,128)(2,1)S(1)}, bf16[4,64,288]{2,1,0:T(8,128)(2,1)S(1)}, u32[]{:S(2)}, u32[]{:S(2)}) %collective-permute-start.3) | collective-permute-done | bytes 147488 | tf_op jit(solution)/shard_map/ppermute | solution.py:466
  16.8 0.0 copy-done.2
  16.8 1.3 %mirror_0.1.mirror_ref = f32[4,64,288]{2,1,0:T(8,128)S(1)} custom-call(s32[4,128]{1,0:T(4,128)S(1)} %pad_add_fusion.refs_0_, bf16[12,2,288,288]{3,2,1,0:T(8,128)(2,1)S(1)} %bitcast.20, bf16[4,64,288]{2,1,0:T(8,128)(2,1)S(1)} %select_select_fusion.refs_2_, bf16[4,64,288]{2,1,0:T(8,128)(2,1)S(1)} %collective-permute-done.3.refs_3_), custom_call_target="tpu_custom_call" | custom-call | tf_op jit(solution)/shard_map/mirror_0/pallas_call | solution.py:377
  18.1 0.0 collective-permute-done.4.got_ref
  18.1 0.1 pack_0.1
  18.2 18.4 %all_to_all.30.refs_0_ = bf16[32,4,1536]{2,1,0:T(4,128)(2,1)S(1)} all-to-all(bf16[32,4,1536]{2,1,0:T(4,128)(2,1)S(1)} %pack_0.1), channel_id=1, replica_groups=mesh['row'=4,'col'=8] {'row','col'}, dimensions={0} | all-to-all | bytes 786432 | tf_op jit(solution)/shard_map/all_to_all | solution.py:501
  36.6 0.3 update_0.1
  36.9 13.8 %all_to_all.31.refs_2_ = bf16[32,4,1152]{2,1,0:T(4,128)(2,1)S(1)} all-to-all(bf16[32,4,1152]{2,1,0:T(4,128)(2,1)S(1)} %get-tuple-element.28), channel_id=1, replica_groups=mesh['row'=4,'col'=8] {'row','col'}, dimensions={0} | all-to-all | bytes 589824 | tf_op jit(solution)/shard_map/all_to_all | solution.py:522
  50.7 0.0 collective-permute-start.5
  50.7 1.9 %direct_1.1 = (f32[4,64,288]{2,1,0:T(8,128)S(1)}, f32[4,64,288]{2,1,0:T(8,128)S(1)}) custom-call(s32[4,128]{1,0:T(4,128)S(1)} %pad_add_fusion.refs_0_, bf16[12,2,288,288]{3,2,1,0:T(8,128)(2,1)S(1)} %bitcast.21, bf16[32,4,1152]{2,1,0:T(4,128)(2,1)S(1)} %all_to_all.31.refs_2_), custom_call_target="tpu_custom_call" | custom-call | tf_op jit(solution)/shard_map/direct_1/pallas_call | solution.py:377
  52.6 0.6 collective-permute-start.6
  53.2 0.0 collective-permute-done.5.refs_3_
  53.2 1.3 %mirror_1.1.mirror_ref = f32[4,64,288]{2,1,0:T(8,128)S(1)} custom-call(s32[4,128]{1,0:T(4,128)S(1)} %pad_add_fusion.refs_0_, bf16[12,2,288,288]{3,2,1,0:T(8,128)(2,1)S(1)} %bitcast.22, bf16[32,4,1152]{2,1,0:T(4,128)(2,1)S(1)} %all_to_all.31.refs_2_, bf16[32,4,1152]{2,1,0:T(4,128)(2,1)S(1)} %collective-permute-done.5.refs_3_), custom_call_target="tpu_custom_call" | custom-call | tf_op jit(solution)/shard_map/mirror_1/pallas_call | solution.py:377
  54.5 0.0 collective-permute-done.6.got_ref
  54.6 0.1 pack_1.1
  54.7 13.5 %all_to_all.32.refs_0_ = bf16[32,4,1152]{2,1,0:T(4,128)(2,1)S(1)} all-to-all(bf16[32,4,1152]{2,1,0:T(4,128)(2,1)S(1)} %pack_1.1), channel_id=1, replica_groups=mesh['row'=4,'col'=8] {'row','col'}, dimensions={0} | all-to-all | bytes 589824 | tf_op jit(solution)/shard_map/all_to_all | solution.py:501
  68.2 0.3 update_1.1
  68.5 13.5 %all_to_all.33.refs_2_ = bf16[32,4,1152]{2,1,0:T(4,128)(2,1)S(1)} all-to-all(bf16[32,4,1152]{2,1,0:T(4,128)(2,1)S(1)} %update_1.1), channel_id=1, replica_groups=mesh['row'=4,'col'=8] {'row','col'}, dimensions={0} | all-to-all | bytes 589824 | tf_op jit(solution)/shard_map/all_to_all | solution.py:522
  82.0 0.0 collective-permute-start.7
  82.0 1.9 %direct_2.1 = (f32[4,64,288]{2,1,0:T(8,128)S(1)}, f32[4,64,288]{2,1,0:T(8,128)S(1)}) custom-call(s32[4,128]{1,0:T(4,128)S(1)} %pad_add_fusion.refs_0_, bf16[12,2,288,288]{3,2,1,0:T(8,128)(2,1)S(1)} %bitcast.23, bf16[32,4,1152]{2,1,0:T(4,128)(2,1)S(1)} %all_to_all.33.refs_2_), custom_call_target="tpu_custom_call" | custom-call | tf_op jit(solution)/shard_map/direct_2/pallas_call | solution.py:377
  83.9 0.6 collective-permute-start.8
  84.5 0.0 collective-permute-done.7.refs_3_
  84.5 1.3 %mirror_2.1.mirror_ref = f32[4,64,288]{2,1,0:T(8,128)S(1)} custom-call(s32[4,128]{1,0:T(4,128)S(1)} %pad_add_fusion.refs_0_, bf16[12,2,288,288]{3,2,1,0:T(8,128)(2,1)S(1)} %bitcast.24, bf16[32,4,1152]{2,1,0:T(4,128)(2,1)S(1)} %all_to_all.33.refs_2_, bf16[32,4,1152]{2,1,0:T(4,128)(2,1)S(1)} %collective-permute-done.7.refs_3_), custom_call_target="tpu_custom_call" | custom-call | tf_op jit(solution)/shard_map/mirror_2/pallas_call | solution.py:377
  85.8 0.0 collective-permute-done.8.got_ref
  85.9 0.1 pack_2.1
  86.0 13.5 %all_to_all.34.refs_0_ = bf16[32,4,1152]{2,1,0:T(4,128)(2,1)S(1)} all-to-all(bf16[32,4,1152]{2,1,0:T(4,128)(2,1)S(1)} %pack_2.1), channel_id=1, replica_groups=mesh['row'=4,'col'=8] {'row','col'}, dimensions={0} | all-to-all | bytes 589824 | tf_op jit(solution)/shard_map/all_to_all | solution.py:501
  99.5 0.2 last.1
  99.7 10.7 %all_to_all.35.msg_ref = s16[32,4,640]{2,1,0:T(4,128)(2,1)S(1)} all-to-all(s16[32,4,640]{2,1,0:T(4,128)(2,1)S(1)} %last.1), channel_id=1, replica_groups=mesh['row'=4,'col'=8] {'row','col'}, dimensions={0} | all-to-all | bytes 327680 | tf_op jit(solution)/shard_map/all_to_all | solution.py:522
  110.4 0.1 finish.1
  110.5 0.3 copy.14
  110.8 1.0 broadcast_in_dim.12
  (8 shorter events, 0.1 us)
Async XLA Ops:
  2.2 11.8 %collective-permute-start.2 = (bf16[4,64,288]{2,1,0:T(8,128)(2,1)S(1)}, bf16[4,64,288]{2,1,0:T(8,128)(2,1)S(1)}, u32[]{:S(2)}, u32[]{:S(2)}) collective-permute-start(bf16[4,64,288]{2,1,0:T(8,128)(2,1)S(1)} %get-tuple-element.21.refs_2_), channel_id=1, source_target_pairs={{0,6},{1,7},{2,3},{3,2},{4,5},{5,4},{6,0},{7,1},{8,10},{9,11},{10,... | collective-permute-start | bytes 442376 | tf_op jit(solution)/shard_map/ppermute | solution.py:454
  6.2 9.1 %collective-permute-start.1 = (bf16[4,64,288]{2,1,0:T(8,128)(2,1)S(1)}, bf16[4,64,288]{2,1,0:T(8,128)(2,1)S(1)}, u32[]{:S(2)}, u32[]{:S(2)}) collective-permute-start(bf16[4,64,288]{2,1,0:T(8,128)(2,1)S(1)} %get-tuple-element.21.refs_2_), channel_id=1, source_target_pairs={{0,4},{1,5},{2,3},{3,2},{4,0},{5,1},{6,7},{7,6},{8,9},{9,8},{10,14... | collective-permute-start | bytes 442376 | tf_op jit(solution)/shard_map/ppermute | solution.py:454
  6.2 9.1 %collective-permute-start = (bf16[4,64,288]{2,1,0:T(8,128)(2,1)S(1)}, bf16[4,64,288]{2,1,0:T(8,128)(2,1)S(1)}, u32[]{:S(2)}, u32[]{:S(2)}) collective-permute-start(bf16[4,64,288]{2,1,0:T(8,128)(2,1)S(1)} %get-tuple-element.21.refs_2_), channel_id=1, source_target_pairs={{0,2},{1,3},{2,0},{3,1},{4,5},{5,4},{6,7},{7,6},{8,9},{9,8},{10,12... | collective-permute-start | bytes 442376 | tf_op jit(solution)/shard_map/ppermute | solution.py:454
  6.9 2.5 %copy-start = (bf16[1,1,12,2,288,288]{5,4,3,2,1,0:T(8,128)(2,1)S(1)}, bf16[1,1,12,2,288,288]{5,4,3,2,1,0:T(8,128)(2,1)}, u32[]{:S(2)}) copy-start(bf16[1,1,12,2,288,288]{5,4,3,2,1,0:T(8,128)(2,1)} %param.7) | copy-start | bytes 11943940
  11.2 6.9 %collective-permute-start.4 = (f32[4,64,288]{2,1,0:T(8,128)S(1)}, f32[4,64,288]{2,1,0:T(8,128)S(1)}, u32[]{:S(2)}, u32[]{:S(2)}) collective-permute-start(f32[4,64,288]{2,1,0:T(8,128)S(1)} %get-tuple-element.26), channel_id=1, source_target_pairs={{0,1},{1,0},{2,3},{3,2},{4,5},{5,4},{6,7},{7,6},{8,9},{9,8},{10,11... | collective-permute-start | bytes 884744 | tf_op jit(solution)/shard_map/ppermute | solution.py:487
  11.4 2.5 %copy-start.1 = (bf16[1,1,12,2,288,288]{5,4,3,2,1,0:T(8,128)(2,1)S(1)}, bf16[1,1,12,2,288,288]{5,4,3,2,1,0:T(8,128)(2,1)}, u32[]{:S(2)}) copy-start(bf16[1,1,12,2,288,288]{5,4,3,2,1,0:T(8,128)(2,1)} %param.7) | copy-start | bytes 11943940
  13.9 3.0 %copy-start.2 = (bf16[1,1,12,2,288,288]{5,4,3,2,1,0:T(8,128)(2,1)S(1)}, bf16[1,1,12,2,288,288]{5,4,3,2,1,0:T(8,128)(2,1)}, u32[]{:S(2)}) copy-start(bf16[1,1,12,2,288,288]{5,4,3,2,1,0:T(8,128)(2,1)} %param.7) | copy-start | bytes 11943940
  15.3 1.5 %collective-permute-start.3 = (bf16[4,64,288]{2,1,0:T(8,128)(2,1)S(1)}, bf16[4,64,288]{2,1,0:T(8,128)(2,1)S(1)}, u32[]{:S(2)}, u32[]{:S(2)}) collective-permute-start(bf16[4,64,288]{2,1,0:T(8,128)(2,1)S(1)} %select_select_fusion.refs_2_), channel_id=1, source_target_pairs={{0,1},{1,0},{2,3},{3,2},{4,5},{5,4},{6,7},{7,6},{8,9},{9,8},{10,11... | collective-permute-start | bytes 442376 | tf_op jit(solution)/shard_map/ppermute | solution.py:466
  50.7 2.5 %collective-permute-start.5 = (bf16[32,4,1152]{2,1,0:T(4,128)(2,1)S(1)}, bf16[32,4,1152]{2,1,0:T(4,128)(2,1)S(1)}, u32[]{:S(2)}, u32[]{:S(2)}) collective-permute-start(bf16[32,4,1152]{2,1,0:T(4,128)(2,1)S(1)} %all_to_all.31.refs_2_), channel_id=1, source_target_pairs={{0,1},{1,0},{2,3},{3,2},{4,5},{5,4},{6,7},{7,6},{8,9},{9,8},{10,11... | collective-permute-start | bytes 884744 | tf_op jit(solution)/shard_map/ppermute | solution.py:476
  52.6 1.9 %collective-permute-start.6 = (f32[4,64,288]{2,1,0:T(8,128)S(1)}, f32[4,64,288]{2,1,0:T(8,128)S(1)}, u32[]{:S(2)}, u32[]{:S(2)}) collective-permute-start(f32[4,64,288]{2,1,0:T(8,128)S(1)} %get-tuple-element.30), channel_id=1, source_target_pairs={{0,1},{1,0},{2,3},{3,2},{4,5},{5,4},{6,7},{7,6},{8,9},{9,8},{10,11... | collective-permute-start | bytes 884744 | tf_op jit(solution)/shard_map/ppermute | solution.py:487
  82.0 2.5 %collective-permute-start.7 = (bf16[32,4,1152]{2,1,0:T(4,128)(2,1)S(1)}, bf16[32,4,1152]{2,1,0:T(4,128)(2,1)S(1)}, u32[]{:S(2)}, u32[]{:S(2)}) collective-permute-start(bf16[32,4,1152]{2,1,0:T(4,128)(2,1)S(1)} %all_to_all.33.refs_2_), channel_id=1, source_target_pairs={{0,1},{1,0},{2,3},{3,2},{4,5},{5,4},{6,7},{7,6},{8,9},{9,8},{10,11... | collective-permute-start | bytes 884744 | tf_op jit(solution)/shard_map/ppermute | solution.py:476
  83.9 1.9 %collective-permute-start.8 = (f32[4,64,288]{2,1,0:T(8,128)S(1)}, f32[4,64,288]{2,1,0:T(8,128)S(1)}, u32[]{:S(2)}, u32[]{:S(2)}) collective-permute-start(f32[4,64,288]{2,1,0:T(8,128)S(1)} %get-tuple-element.34), channel_id=1, source_target_pairs={{0,1},{1,0},{2,3},{3,2},{4,5},{5,4},{6,7},{7,6},{8,9},{9,8},{10,11... | collective-permute-start | bytes 884744 | tf_op jit(solution)/shard_map/ppermute | solution.py:487

commit v6 on v5

--- a/solution.py
+++ b/solution.py
@@ -136,9 +136,21 @@
     put_block(xs_ref, at, jnp.concatenate(parts, axis=0), half)
 
 
+def put_side_by_side(out_ref, values):
+    for q, value in enumerate(values):
+        out_ref[:, q * MAIN : (q + 1) * MAIN] = value[:, :MAIN].astype(out_ref.dtype)
+    out_ref[:, ENDS:] = jnp.concatenate([value[:, MAIN:] for value in values], axis=1).astype(out_ref.dtype)
+
+
+def side_by_side(ref):
+    ends = ref[:, ENDS:].astype(F32)
+    mains = [ref[:, q * MAIN : (q + 1) * MAIN].astype(F32) for q in range(4)]
+    return [jnp.concatenate([main, shifted(ends, q * TAIL)[:, :TAIL]], axis=1) for q, main in enumerate(mains)]
+
+
 def copy_in(x_ref, xs_ref, offset, mirror):
-    for q in range(x_ref.shape[0]):
-        put_block(xs_ref, offset + q, x_ref[q].astype(F32), mirror)
+    for q, value in enumerate(side_by_side(x_ref)):
+        put_block(xs_ref, offset + q, value, mirror)
 
 
 def across(left, right):
@@ -163,7 +175,7 @@
 
 
 def start_kernel(classes, small_ref, back_ref, out_ref, contrast_ref):
-    blocks = out_ref.shape[0]
+    blocks = back_ref.shape[0]
     cells = contrast_ref.shape[2]
     kinds = small_ref[4 : 4 + blocks, :cells]
     tables = small_ref[4 + blocks : 6 + blocks, :]
@@ -175,9 +187,11 @@
         contrast_ref[part] = value
         contrast.append(jnp.concatenate([value] * 3, axis=1))
     real, imag = contrast
+    values = []
     for q in range(blocks):
         back = back_ref[q]
-        out_ref[q] = (real[q : q + 1] * back + imag[q : q + 1] * turned(back)).astype(BF)
+        values.append(real[q : q + 1] * back + imag[q : q + 1] * turned(back))
+    put_side_by_side(out_ref, values)
 
 
 def share_kernel(small_ref, contrast_ref, back_ref, _, extra_ref):
@@ -217,7 +231,7 @@
     slot_products(table_ref, g_ref, xs_ref, acc_ref, False)
     for q in range(blocks):
         own_ref[q] = acc_ref[q]
-        other_ref[q] = acc_ref[blocks + q]
+    put_side_by_side(other_ref, [acc_ref[blocks + q] for q in range(blocks)])
 
 
 def mirror_kernel(first, table_ref, g_ref, x_ref, x_other_ref, out_ref, xs_ref, acc_ref):
@@ -238,8 +252,9 @@
     msg_ref = rest[-1]
     blocks, rows, _ = own_ref.shape
     half = rows // 2
+    got = side_by_side(got_ref)
     for q in range(blocks):
-        halves = [own_ref[q] + got_ref[q], mirror_ref[q]]
+        halves = [own_ref[q] + got[q], mirror_ref[q]]
         parts = [value[p * half : (p + 1) * half] for value in halves for p in range(2)]
         ends = jnp.concatenate([part[:, MAIN:] for part in parts], axis=1)
         for g in range(half // 4):
@@ -432,7 +447,7 @@
     start, contrast = whole_call(
         lambda *refs: start_kernel(class_contrast.shape[0], *refs),
         (
-            jax.ShapeDtypeStruct((blocks,) + block, BF),
+            jax.ShapeDtypeStruct((2 * sources, WIDTH), BF),
             jax.ShapeDtypeStruct((2, blocks, entries // 3), F32),
         ),
         (small, back),
@@ -476,7 +491,7 @@
             direct_in, mirror_in = x_msg, (x_msg, lax.ppermute(x_msg, "col", core_pairs))
         own, other = whole_call(
             lambda *refs, first=first: direct_kernel(first, *refs),
-            (part, part),
+            (part, jax.ShapeDtypeStruct((2 * sources, WIDTH), F32)),
             (table, green, direct_in),
             [
                 pltpu.VMEM((blocks, 2 * sources, 2 * entries), BF),

time: 112 us -> 112 us (level)
  waiting for transfers between devices: 2.7 us -> 1.03 us
    ppermute x3, waiting for transfers between devices: 1.23 us -> 0.01 us  [local_owners(): arrived.append(lax.ppermute(start, both, pairs))]
  transfers between devices with their start and end apart: 9 -> 9, of which waited for: 2 -> 1; matrix products, arithmetic and copies ran while one was open for 0% -> 0% of each run, Pallas kernels for 9% -> 9%
where the time goes in v6:
time: 112 us; the launch traced here: 111 us
  blocking collectives  83 us (74%)
  Pallas kernels  11.8 us (11%)
  local copies, waits for them, and re-layouts  8.14 us (7%)
  starting transfers between devices  5.68 us (5%)
    all_to_all x3, blocking collectives, local_owners(): y_msg = lax.all_to_all(y_msg, both, 0, 0, tiled=True)  45 us
    all_to_all x3, blocking collectives, local_owners(): x_msg = lax.all_to_all(x_msg, both, 0, 0, tiled=True)  38 us
    pallas_call x15, Pallas kernels, whole_call(): pl.pallas_call(kernel, out_shape=out_shape, in_specs=[vmem] * len(operand...  11.8 us
    unnamed x7, local copies, waits for them, and re-layouts  6.84 us
    ppermute x3, starting transfers between devices, local_owners(): arrived.append(lax.ppermute(start, both, pairs))  3.96 us
  transfers between devices with their start and end apart: 9, of which 1 were waited for; matrix products, arithmetic and copies ran while one was open for 0% of the time, Pallas kernels for 9%

profile of v6, /device:TPU:0, one launch (start us, length us, event | category | flops | bytes accessed | tf_op | source)
XLA Modules:
  0.0 111.4 jit_solution(17837514229383760553)
XLA Ops:
  0.0 1.1 copy.13
  1.1 0.8 select_select_fusion.1.refs_0_.small_ref
  1.9 0.3 start.1
  2.3 4.0 %collective-permute-start.2 = (bf16[64,1152]{1,0:T(8,128)(2,1)S(1)}, bf16[64,1152]{1,0:T(8,128)(2,1)S(1)}, u32[]{:S(2)}, u32[]{:S(2)}) collective-permute-start(bf16[64,1152]{1,0:T(8,128)(2,1)S(1)} %get-tuple-element.21.refs_2_), channel_id=1, source_target_pairs={{0,6},{1,7},{2,3},{3,2},{4,5},{5,4},{6,0},{7,1},{8,10},{9,11},{10,... | collective-permute-start | bytes 442376 | tf_op jit(solution)/shard_map/ppermute | solution.py:469
  6.2 0.0 collective-permute-start.1
  6.2 0.0 collective-permute-start
  7.0 0.0 copy-start
  7.0 2.5 %copy-done = bf16[1,1,12,2,288,288]{5,4,3,2,1,0:T(8,128)(2,1)S(1)} copy-done((bf16[1,1,12,2,288,288]{5,4,3,2,1,0:T(8,128)(2,1)S(1)}, bf16[1,1,12,2,288,288]{5,4,3,2,1,0:T(8,128)(2,1)}, u32[]{:S(2)}) %copy-start) | copy-done | bytes 3981336
  9.5 1.9 %direct_0.1 = (f32[4,64,288]{2,1,0:T(8,128)S(1)}, f32[64,1152]{1,0:T(8,128)S(1)}) custom-call(s32[4,128]{1,0:T(4,128)S(1)} %pad_add_fusion.refs_0_, bf16[12,2,288,288]{3,2,1,0:T(8,128)(2,1)S(1)} %bitcast.18, bf16[64,1152]{1,0:T(8,128)(2,1)S(1)} %get-tuple-element.21.refs_2_), custom_call_target="tpu_custom_call" | custom-call | tf_op jit(solution)/shard_map/direct_0/pallas_call | solution.py:392
  11.4 0.1 collective-permute-start.4
  11.5 0.0 copy-start.1
  11.6 2.5 %copy-done.1 = bf16[1,1,12,2,288,288]{5,4,3,2,1,0:T(8,128)(2,1)S(1)} copy-done((bf16[1,1,12,2,288,288]{5,4,3,2,1,0:T(8,128)(2,1)S(1)}, bf16[1,1,12,2,288,288]{5,4,3,2,1,0:T(8,128)(2,1)}, u32[]{:S(2)}) %copy-start.1) | copy-done | bytes 3981336
  14.1 0.2 share.1.rest_0_
  14.2 0.0 collective-permute-done.2
  14.2 0.0 collective-permute-done.1
  14.2 0.0 collective-permute-done
  14.3 0.5 collective-permute-start.3
  14.8 1.0 collective-permute-done.3.refs_3_
  15.8 0.7 copy-done.2
  16.6 1.3 %mirror_0.1.mirror_ref = f32[4,64,288]{2,1,0:T(8,128)S(1)} custom-call(s32[4,128]{1,0:T(4,128)S(1)} %pad_add_fusion.refs_0_, bf16[12,2,288,288]{3,2,1,0:T(8,128)(2,1)S(1)} %bitcast.20, bf16[64,1152]{1,0:T(8,128)(2,1)S(1)} %select_select_fusion.refs_2_, bf16[64,1152]{1,0:T(8,128)(2,1)S(1)} %collective-permute-done.3.refs_3_), custom_call_target="tpu_custom_call" | custom-call | tf_op jit(solution)/shard_map/mirror_0/pallas_call | solution.py:392
  17.9 0.0 collective-permute-done.4.got_ref
  17.9 0.2 pack_0.1
  18.1 17.9 %all_to_all.30.refs_0_ = bf16[32,4,1536]{2,1,0:T(4,128)(2,1)S(1)} all-to-all(bf16[32,4,1536]{2,1,0:T(4,128)(2,1)S(1)} %pack_0.1), channel_id=1, replica_groups=mesh['row'=4,'col'=8] {'row','col'}, dimensions={0} | all-to-all | bytes 786432 | tf_op jit(solution)/shard_map/all_to_all | solution.py:516
  36.0 0.3 update_0.1
  36.3 13.8 %all_to_all.31.refs_2_ = bf16[32,4,1152]{2,1,0:T(4,128)(2,1)S(1)} all-to-all(bf16[32,4,1152]{2,1,0:T(4,128)(2,1)S(1)} %get-tuple-element.28), channel_id=1, replica_groups=mesh['row'=4,'col'=8] {'row','col'}, dimensions={0} | all-to-all | bytes 589824 | tf_op jit(solution)/shard_map/all_to_all | solution.py:537
  50.1 0.0 collective-permute-start.5
  50.1 1.9 %direct_1.1 = (f32[4,64,288]{2,1,0:T(8,128)S(1)}, f32[64,1152]{1,0:T(8,128)S(1)}) custom-call(s32[4,128]{1,0:T(4,128)S(1)} %pad_add_fusion.refs_0_, bf16[12,2,288,288]{3,2,1,0:T(8,128)(2,1)S(1)} %bitcast.21, bf16[32,4,1152]{2,1,0:T(4,128)(2,1)S(1)} %all_to_all.31.refs_2_), custom_call_target="tpu_custom_call" | custom-call | tf_op jit(solution)/shard_map/direct_1/pallas_call | solution.py:392
  52.1 0.6 collective-permute-start.6
  52.6 0.0 collective-permute-done.5.refs_3_
  52.6 1.3 %mirror_1.1.mirror_ref = f32[4,64,288]{2,1,0:T(8,128)S(1)} custom-call(s32[4,128]{1,0:T(4,128)S(1)} %pad_add_fusion.refs_0_, bf16[12,2,288,288]{3,2,1,0:T(8,128)(2,1)S(1)} %bitcast.22, bf16[32,4,1152]{2,1,0:T(4,128)(2,1)S(1)} %all_to_all.31.refs_2_, bf16[32,4,1152]{2,1,0:T(4,128)(2,1)S(1)} %collective-permute-done.5.refs_3_), custom_call_target="tpu_custom_call" | custom-call | tf_op jit(solution)/shard_map/mirror_1/pallas_call | solution.py:392
  54.0 0.0 collective-permute-done.6.got_ref
  54.0 0.2 pack_1.1
  54.2 13.5 %all_to_all.32.refs_0_ = bf16[32,4,1152]{2,1,0:T(4,128)(2,1)S(1)} all-to-all(bf16[32,4,1152]{2,1,0:T(4,128)(2,1)S(1)} %pack_1.1), channel_id=1, replica_groups=mesh['row'=4,'col'=8] {'row','col'}, dimensions={0} | all-to-all | bytes 589824 | tf_op jit(solution)/shard_map/all_to_all | solution.py:516
  67.7 0.3 update_1.1
  68.0 13.5 %all_to_all.33.refs_2_ = bf16[32,4,1152]{2,1,0:T(4,128)(2,1)S(1)} all-to-all(bf16[32,4,1152]{2,1,0:T(4,128)(2,1)S(1)} %update_1.1), channel_id=1, replica_groups=mesh['row'=4,'col'=8] {'row','col'}, dimensions={0} | all-to-all | bytes 589824 | tf_op jit(solution)/shard_map/all_to_all | solution.py:537
  81.5 0.0 collective-permute-start.7
  81.5 1.9 %direct_2.1 = (f32[4,64,288]{2,1,0:T(8,128)S(1)}, f32[64,1152]{1,0:T(8,128)S(1)}) custom-call(s32[4,128]{1,0:T(4,128)S(1)} %pad_add_fusion.refs_0_, bf16[12,2,288,288]{3,2,1,0:T(8,128)(2,1)S(1)} %bitcast.23, bf16[32,4,1152]{2,1,0:T(4,128)(2,1)S(1)} %all_to_all.33.refs_2_), custom_call_target="tpu_custom_call" | custom-call | tf_op jit(solution)/shard_map/direct_2/pallas_call | solution.py:392
  83.5 0.6 collective-permute-start.8
  84.0 0.0 collective-permute-done.7.refs_3_
  84.0 1.3 %mirror_2.1.mirror_ref = f32[4,64,288]{2,1,0:T(8,128)S(1)} custom-call(s32[4,128]{1,0:T(4,128)S(1)} %pad_add_fusion.refs_0_, bf16[12,2,288,288]{3,2,1,0:T(8,128)(2,1)S(1)} %bitcast.24, bf16[32,4,1152]{2,1,0:T(4,128)(2,1)S(1)} %all_to_all.33.refs_2_, bf16[32,4,1152]{2,1,0:T(4,128)(2,1)S(1)} %collective-permute-done.7.refs_3_), custom_call_target="tpu_custom_call" | custom-call | tf_op jit(solution)/shard_map/mirror_2/pallas_call | solution.py:392
  85.4 0.0 collective-permute-done.8.got_ref
  85.4 0.2 pack_2.1
  85.6 13.5 %all_to_all.34.refs_0_ = bf16[32,4,1152]{2,1,0:T(4,128)(2,1)S(1)} all-to-all(bf16[32,4,1152]{2,1,0:T(4,128)(2,1)S(1)} %pack_2.1), channel_id=1, replica_groups=mesh['row'=4,'col'=8] {'row','col'}, dimensions={0} | all-to-all | bytes 589824 | tf_op jit(solution)/shard_map/all_to_all | solution.py:516
  99.1 0.2 last.1
  99.3 10.7 %all_to_all.35.msg_ref = s16[32,4,640]{2,1,0:T(4,128)(2,1)S(1)} all-to-all(s16[32,4,640]{2,1,0:T(4,128)(2,1)S(1)} %last.1), channel_id=1, replica_groups=mesh['row'=4,'col'=8] {'row','col'}, dimensions={0} | all-to-all | bytes 327680 | tf_op jit(solution)/shard_map/all_to_all | solution.py:537
  110.0 0.1 finish.1
  110.1 0.3 copy.14
  110.4 1.0 broadcast_in_dim.12
  (8 shorter events, 0.1 us)
Async XLA Ops:
  2.3 12.0 %collective-permute-start.2 = (bf16[64,1152]{1,0:T(8,128)(2,1)S(1)}, bf16[64,1152]{1,0:T(8,128)(2,1)S(1)}, u32[]{:S(2)}, u32[]{:S(2)}) collective-permute-start(bf16[64,1152]{1,0:T(8,128)(2,1)S(1)} %get-tuple-element.21.refs_2_), channel_id=1, source_target_pairs={{0,6},{1,7},{2,3},{3,2},{4,5},{5,4},{6,0},{7,1},{8,10},{9,11},{10,... | collective-permute-start | bytes 442376 | tf_op jit(solution)/shard_map/ppermute | solution.py:469
  6.2 8.0 %collective-permute-start.1 = (bf16[64,1152]{1,0:T(8,128)(2,1)S(1)}, bf16[64,1152]{1,0:T(8,128)(2,1)S(1)}, u32[]{:S(2)}, u32[]{:S(2)}) collective-permute-start(bf16[64,1152]{1,0:T(8,128)(2,1)S(1)} %get-tuple-element.21.refs_2_), channel_id=1, source_target_pairs={{0,4},{1,5},{2,3},{3,2},{4,0},{5,1},{6,7},{7,6},{8,9},{9,8},{10,14... | collective-permute-start | bytes 442376 | tf_op jit(solution)/shard_map/ppermute | solution.py:469
  6.2 8.0 %collective-permute-start = (bf16[64,1152]{1,0:T(8,128)(2,1)S(1)}, bf16[64,1152]{1,0:T(8,128)(2,1)S(1)}, u32[]{:S(2)}, u32[]{:S(2)}) collective-permute-start(bf16[64,1152]{1,0:T(8,128)(2,1)S(1)} %get-tuple-element.21.refs_2_), channel_id=1, source_target_pairs={{0,2},{1,3},{2,0},{3,1},{4,5},{5,4},{6,7},{7,6},{8,9},{9,8},{10,12... | collective-permute-start | bytes 442376 | tf_op jit(solution)/shard_map/ppermute | solution.py:469
  7.0 2.5 %copy-start = (bf16[1,1,12,2,288,288]{5,4,3,2,1,0:T(8,128)(2,1)S(1)}, bf16[1,1,12,2,288,288]{5,4,3,2,1,0:T(8,128)(2,1)}, u32[]{:S(2)}) copy-start(bf16[1,1,12,2,288,288]{5,4,3,2,1,0:T(8,128)(2,1)} %param.7) | copy-start | bytes 11943940
  11.4 6.5 %collective-permute-start.4 = (f32[64,1152]{1,0:T(8,128)S(1)}, f32[64,1152]{1,0:T(8,128)S(1)}, u32[]{:S(2)}, u32[]{:S(2)}) collective-permute-start(f32[64,1152]{1,0:T(8,128)S(1)} %get-tuple-element.26), channel_id=1, source_target_pairs={{0,1},{1,0},{2,3},{3,2},{4,5},{5,4},{6,7},{7,6},{8,9},{9,8},{10,11... | collective-permute-start | bytes 884744 | tf_op jit(solution)/shard_map/ppermute | solution.py:502
  11.5 2.5 %copy-start.1 = (bf16[1,1,12,2,288,288]{5,4,3,2,1,0:T(8,128)(2,1)S(1)}, bf16[1,1,12,2,288,288]{5,4,3,2,1,0:T(8,128)(2,1)}, u32[]{:S(2)}) copy-start(bf16[1,1,12,2,288,288]{5,4,3,2,1,0:T(8,128)(2,1)} %param.7) | copy-start | bytes 11943940
  14.1 2.5 %copy-start.2 = (bf16[1,1,12,2,288,288]{5,4,3,2,1,0:T(8,128)(2,1)S(1)}, bf16[1,1,12,2,288,288]{5,4,3,2,1,0:T(8,128)(2,1)}, u32[]{:S(2)}) copy-start(bf16[1,1,12,2,288,288]{5,4,3,2,1,0:T(8,128)(2,1)} %param.7) | copy-start | bytes 11943940
  14.3 1.5 %collective-permute-start.3 = (bf16[64,1152]{1,0:T(8,128)(2,1)S(1)}, bf16[64,1152]{1,0:T(8,128)(2,1)S(1)}, u32[]{:S(2)}, u32[]{:S(2)}) collective-permute-start(bf16[64,1152]{1,0:T(8,128)(2,1)S(1)} %select_select_fusion.refs_2_), channel_id=1, source_target_pairs={{0,1},{1,0},{2,3},{3,2},{4,5},{5,4},{6,7},{7,6},{8,9},{9,8},{10,11... | collective-permute-start | bytes 442376 | tf_op jit(solution)/shard_map/ppermute | solution.py:481
  50.1 2.5 %collective-permute-start.5 = (bf16[32,4,1152]{2,1,0:T(4,128)(2,1)S(1)}, bf16[32,4,1152]{2,1,0:T(4,128)(2,1)S(1)}, u32[]{:S(2)}, u32[]{:S(2)}) collective-permute-start(bf16[32,4,1152]{2,1,0:T(4,128)(2,1)S(1)} %all_to_all.31.refs_2_), channel_id=1, source_target_pairs={{0,1},{1,0},{2,3},{3,2},{4,5},{5,4},{6,7},{7,6},{8,9},{9,8},{10,11... | collective-permute-start | bytes 884744 | tf_op jit(solution)/shard_map/ppermute | solution.py:491
  52.1 1.9 %collective-permute-start.6 = (f32[64,1152]{1,0:T(8,128)S(1)}, f32[64,1152]{1,0:T(8,128)S(1)}, u32[]{:S(2)}, u32[]{:S(2)}) collective-permute-start(f32[64,1152]{1,0:T(8,128)S(1)} %get-tuple-element.30), channel_id=1, source_target_pairs={{0,1},{1,0},{2,3},{3,2},{4,5},{5,4},{6,7},{7,6},{8,9},{9,8},{10,11... | collective-permute-start | bytes 884744 | tf_op jit(solution)/shard_map/ppermute | solution.py:502
  81.5 2.5 %collective-permute-start.7 = (bf16[32,4,1152]{2,1,0:T(4,128)(2,1)S(1)}, bf16[32,4,1152]{2,1,0:T(4,128)(2,1)S(1)}, u32[]{:S(2)}, u32[]{:S(2)}) collective-permute-start(bf16[32,4,1152]{2,1,0:T(4,128)(2,1)S(1)} %all_to_all.33.refs_2_), channel_id=1, source_target_pairs={{0,1},{1,0},{2,3},{3,2},{4,5},{5,4},{6,7},{7,6},{8,9},{9,8},{10,11... | collective-permute-start | bytes 884744 | tf_op jit(solution)/shard_map/ppermute | solution.py:491
  83.5 1.9 %collective-permute-start.8 = (f32[64,1152]{1,0:T(8,128)S(1)}, f32[64,1152]{1,0:T(8,128)S(1)}, u32[]{:S(2)}, u32[]{:S(2)}) collective-permute-start(f32[64,1152]{1,0:T(8,128)S(1)} %get-tuple-element.34), channel_id=1, source_target_pairs={{0,1},{1,0},{2,3},{3,2},{4,5},{5,4},{6,7},{7,6},{8,9},{9,8},{10,11... | collective-permute-start | bytes 884744 | tf_op jit(solution)/shard_map/ppermute | solution.py:502

commit v7 on v6

--- a/solution.py
+++ b/solution.py
@@ -99,6 +99,7 @@
 TAIL = LANES // 4
 ENDS = 4 * MAIN
 WIDTH = ENDS + LANES
+POWER = 3 * TAIL
 
 
 def turned(value):
@@ -157,8 +158,10 @@
     return lax.dot_general(left, right, (((1,), (1,)), ((), ())), preferred_element_type=F32)
 
 
-def slot_products(table_ref, g_ref, xs_ref, acc_ref, mirror):
+def slot_products(table_ref, g_ref, xs_ref, acc_ref, mirror, start_ref=None):
     acc_ref[...] = jnp.zeros_like(acc_ref)
+    if start_ref is not None:
+        acc_ref[: start_ref.shape[0]] = start_ref[...]
     slots, _, depth, entries = g_ref.shape
     table = table_ref[...]
     first = 2 if mirror else 0
@@ -194,31 +197,29 @@
     put_side_by_side(out_ref, values)
 
 
-def share_kernel(small_ref, contrast_ref, back_ref, _, extra_ref):
-    r = small_ref[2:3, 0:1].astype(jnp.int32)
-    blocks, rows, _ = back_ref.shape
-    half = rows // 2
+def share_kernel(small_ref, contrast_ref, back_ref, _, marks_ref, share_ref):
+    r = small_ref[2:3, 0:1]
     cells = contrast_ref.shape[2]
-    for q in range(blocks):
-        rest = jnp.where(r == 2, contrast_ref[1, q : q + 1], contrast_ref[0, q : q + 1])
+    for q in range(back_ref.shape[0]):
+        share_ref[q] = jnp.where(r == 0.0, back_ref[q], 0.0)
         marks = []
-        for _ in range(3):
-            piece = rest.astype(BF).astype(F32)
-            marks.append(piece)
-            rest = rest - piece
-        marks = jnp.concatenate(marks + [jnp.zeros((1, cells), F32)], axis=0)
-        marks = jnp.concatenate([marks, jnp.zeros((4, LANES - cells), F32)], axis=1)
-        value = jnp.where(r % 2 == 0, back_ref[q, :half, :MAIN], back_ref[q, half:, :MAIN])
-        high = value.astype(BF).astype(F32)
-        value = jnp.where(r < 2, high, value - high)
-        ends = jnp.concatenate([back_ref[q, :half, MAIN:], back_ref[q, half:, MAIN:]], axis=1)
-        high = ends.astype(BF).astype(F32)
-        ends = jnp.concatenate([high, ends - high], axis=1)
-        for g in range(half // 4):
-            at = slice(4 * g, 4 * g + 4)
-            d = q * (half // 4) + g
-            extra_ref[d, :, :MAIN] = value[at].astype(BF)
-            extra_ref[d, :, MAIN:] = jnp.where(r == 0, ends[at], marks).astype(BF)
+        for part in range(2):
+            value = contrast_ref[part, q : q + 1] * 2.0**15
+            marks += [jnp.round(value), (value - jnp.round(value)) * 2.0**16]
+        marks = jnp.concatenate([whole(part) for part in marks], axis=0)
+        marks_ref[q] = jnp.concatenate([marks, jnp.zeros((4, LANES - cells), F32)], axis=1)
+
+
+def whole(value):
+    return jnp.clip(jnp.round(value), -32767.0, 32767.0)
+
+
+def as_integers(value):
+    return value.astype(jnp.int32).astype(jnp.int16)
+
+
+def as_floats(value):
+    return value.astype(jnp.int32).astype(F32)
 
 
 def direct_kernel(first, table_ref, g_ref, x_ref, own_ref, other_ref, xs_ref, acc_ref):
@@ -234,7 +235,8 @@
     put_side_by_side(other_ref, [acc_ref[blocks + q] for q in range(blocks)])
 
 
-def mirror_kernel(first, table_ref, g_ref, x_ref, x_other_ref, out_ref, xs_ref, acc_ref):
+def mirror_kernel(first, table_ref, g_ref, x_ref, x_other_ref, *refs):
+    *start, out_ref, xs_ref, acc_ref = refs
     blocks = out_ref.shape[0]
     if first:
         copy_in(x_ref, xs_ref, 0, True)
@@ -243,7 +245,7 @@
         for q in range(blocks):
             unpack_half(x_ref, q, 1, xs_ref, q)
             unpack_half(x_other_ref, q, 1, xs_ref, blocks + q)
-    slot_products(table_ref, g_ref, xs_ref, acc_ref, True)
+    slot_products(table_ref, g_ref, xs_ref, acc_ref, True, *start)
     for q in range(blocks):
         out_ref[q] = acc_ref[q]
 
@@ -252,19 +254,31 @@
     msg_ref = rest[-1]
     blocks, rows, _ = own_ref.shape
     half = rows // 2
+    lane = lax.broadcasted_iota(jnp.int32, (4, LANES), 1)
     got = side_by_side(got_ref)
     for q in range(blocks):
         halves = [own_ref[q] + got[q], mirror_ref[q]]
         parts = [value[p * half : (p + 1) * half] for value in halves for p in range(2)]
+        power, scale = row_power(parts)
+        parts = [whole(part * scale) for part in parts]
         ends = jnp.concatenate([part[:, MAIN:] for part in parts], axis=1)
+        marks = rest[0][q] if len(rest) == 2 else jnp.zeros((4, LANES), F32)
         for g in range(half // 4):
             at = slice(4 * g, 4 * g + 4)
             d = q * (half // 4) + g
             for k, part in enumerate(parts):
-                msg_ref[d, :, k * MAIN : (k + 1) * MAIN] = part[at, :MAIN].astype(BF)
-            msg_ref[d, :, ENDS:WIDTH] = ends[at].astype(BF)
-    if len(rest) == 2:
-        msg_ref[:, :, WIDTH:] = rest[0][...]
+                msg_ref[d, :, k * MAIN : (k + 1) * MAIN] = as_integers(part[at, :MAIN])
+            msg_ref[d, :, ENDS:WIDTH] = as_integers(ends[at])
+            msg_ref[d, :, WIDTH:] = as_integers(jnp.where(lane == POWER, power[at], marks))
+
+
+def row_power(parts):
+    most = jnp.abs(parts[0])
+    for part in parts[1:]:
+        most = jnp.maximum(most, jnp.abs(part))
+    most = jnp.max(most, axis=1, keepdims=True)
+    power = jnp.floor(jnp.log2(jnp.maximum(most, SMALLEST)))
+    return power, jnp.exp2(14.0 - power)
 
 
 def partial_sums(msg_ref, rows, cols):
@@ -278,8 +292,9 @@
         for c in range(cols):
             d = r * cols + c
             j = 2 * r + c % 2
+            scale = jnp.exp2(as_floats(msg_ref[d, :, WIDTH : WIDTH + LANES])[:, POWER : POWER + 1] - 14.0)
             for k in range(9):
-                value = msg_ref[d, :, k * LANES : (k + 1) * LANES].astype(F32)
+                value = as_floats(msg_ref[d, :, k * LANES : (k + 1) * LANES]) * scale
                 if k < 4 or k == 8:
                     add(direct, (j, min(k, 4)), value)
                 if k >= 4:
@@ -290,40 +305,32 @@
 
 
 def update_kernel(first, rows, cols, msg_ref, *refs):
-    back_ref, contrast_ref, out_ref = refs[1:] + refs[:1] if first else refs
+    contrast_ref, out_ref = refs[::-1] if first else refs
     lane = lax.broadcasted_iota(jnp.int32, (4, LANES), 1)
     cells = (MAIN + TAIL) // 3
     sums = partial_sums(msg_ref, rows, cols)
     current = {}
     for j in range(cols):
         if first:
-            extra = [
-                [msg_ref[r * cols + j, :, WIDTH + k * LANES : WIDTH + (k + 1) * LANES].astype(F32) for k in range(3)]
-                for r in range(4)
-            ]
-            back = [extra[p][k] + extra[p + 2][k] for p in range(2) for k in range(2)]
-            back.append(extra[0][2] + shifted(extra[0][2], 2 * TAIL))
+            marks = as_floats(msg_ref[j, :, WIDTH : WIDTH + LANES])
             contrast = []
-            for r in (1, 2):
-                value = extra[r][2]
-                value = jnp.broadcast_to(value[0:1] + value[1:2] + value[2:3], (4, LANES))
-                moved = [value, shifted(value, TAIL), shifted(value, 2 * TAIL)]
+            for row in (0, 2):
+                value = marks[row : row + 1] * 2.0**-15 + marks[row + 1 : row + 2] * 2.0**-31
+                value = jnp.broadcast_to(value, (4, LANES))
+                near, far = shifted(value, TAIL), shifted(value, 2 * TAIL)
                 contrast.append(
                     [
-                        jnp.where(lane < cells, moved[0], shifted(value, TAIL)),
-                        jnp.where(lane < 2 * TAIL, moved[1], moved[2]),
-                        jnp.where(lane < TAIL, moved[2], moved[1]),
+                        jnp.where(lane < cells, value, near),
+                        jnp.where(lane < 2 * TAIL, near, far),
+                        jnp.where(lane < TAIL, far, near),
                     ]
                 )
-            for k in range(5):
-                back_ref[j, k] = back[k]
             for part in range(2):
                 for k in range(3):
                     contrast_ref[j, part, k] = contrast[part][k]
         else:
-            back = [back_ref[j, k] for k in range(5)]
             contrast = [[contrast_ref[j, part, k] for k in range(3)] for part in range(2)]
-        total = [sums[j, k] + back[k] for k in range(5)]
+        total = [sums[j, k] for k in range(5)]
         real, imag = contrast
         for k in range(2):
             current[j, k] = real[k] * total[k] - imag[k] * total[k + 2]
@@ -345,27 +352,19 @@
     lane = lax.broadcasted_iota(jnp.int32, (4, LANES), 1)
     sums = partial_sums(msg_ref, rows, cols)
     for j in range(cols):
-        ends = sums[j, 4]
-        coded_ends = jnp.zeros((4, LANES), F32)
+        ends = jnp.zeros((4, LANES), F32)
         for p in range(2):
             mine = (lane >= p * TAIL) & (lane < (p + 1) * TAIL)
-            main = [sums[j, 2 * p], sums[j, 2 * p + 1]]
-            most = jnp.maximum(jnp.maximum(jnp.abs(main[0]), jnp.abs(main[1])), jnp.where(mine, jnp.abs(ends), 0.0))
-            most = jnp.max(most, axis=1, keepdims=True)
-            power = jnp.floor(jnp.log2(jnp.maximum(most, SMALLEST)))
-            scale = jnp.exp2(14.0 - power)
-            for k in range(2):
-                coded = as_integers(main[k] * scale)
+            tail = jnp.where(mine, sums[j, 4], 0.0)
+            power, scale = row_power([sums[j, 2 * p], sums[j, 2 * p + 1], tail])
+            for k in range(2 * p, 2 * p + 2):
+                coded = as_integers(whole(sums[j, k] * scale))
                 for r in range(rows):
-                    out_ref[r * cols + j, :, (2 * p + k) * LANES : (2 * p + k + 1) * LANES] = coded
-            coded_ends = jnp.where(mine, ends * scale, jnp.where(lane == 2 * TAIL + p, power, coded_ends))
-        coded = as_integers(coded_ends)
+                    out_ref[r * cols + j, :, k * LANES : (k + 1) * LANES] = coded
+            ends = jnp.where(mine, whole(tail * scale), jnp.where(lane == 2 * TAIL + p, power, ends))
+        coded = as_integers(ends)
         for r in range(rows):
             out_ref[r * cols + j, :, 2 * MAIN : 2 * MAIN + LANES] = coded
-
-
-def as_integers(value):
-    return jnp.clip(jnp.round(value), -32767.0, 32767.0).astype(jnp.int32).astype(jnp.int16)
 
 
 def finish_kernel(msg_ref, back_ref, out_ref):
@@ -374,8 +373,7 @@
     groups = half // 4
 
     def rows_of(q, lanes):
-        pieces = [msg_ref[q * groups + g, :, lanes].astype(jnp.int32).astype(F32) for g in range(groups)]
-        return jnp.concatenate(pieces, axis=0)
+        return jnp.concatenate([as_floats(msg_ref[q * groups + g, :, lanes]) for g in range(groups)], axis=0)
 
     for q in range(blocks):
         ends = rows_of(q, slice(2 * MAIN, 2 * MAIN + LANES))
@@ -467,14 +465,17 @@
                     to = {a: 2 * far + p, far: 2 * a + p}.get(k, 2 * k + 1 - p)
                     pairs.append((a * cols + 2 * k + p, a * cols + to))
         arrived.append(lax.ppermute(start, both, pairs))
-    extra = whole_call(
+    marks, back_share = whole_call(
         share_kernel,
-        jax.ShapeDtypeStruct((rows * cols, 4, 3 * LANES), BF),
+        (
+            jax.ShapeDtypeStruct((blocks, 4, LANES), F32),
+            jax.ShapeDtypeStruct((blocks,) + block, F32),
+        ),
         (small, contrast, back, green),
         [],
         "share",
     )
-    extra, *arrived = lax.optimization_barrier((extra, *arrived))
+    marks, *arrived = lax.optimization_barrier((marks, *arrived))
     row_mine = start
     for hop in range(1, chips):
         row_mine = jnp.where(c // 2 == (r + hop) % chips, arrived[hop - 1], row_mine)
@@ -503,33 +504,28 @@
         mirror = whole_call(
             lambda *refs, first=first: mirror_kernel(first, *refs),
             part,
-            (table, green) + mirror_in,
+            (table, green) + mirror_in + (() if final else (back_share,)),
             [
                 pltpu.VMEM((2 * blocks, 2 * sources, 2 * entries), BF),
                 pltpu.VMEM((blocks + 1,) + block, F32),
             ],
             f"mirror_{step}",
         )
-        y_shape = jax.ShapeDtypeStruct((rows * cols, 4, WIDTH + 3 * LANES), BF) if first else message
-        operands = (mirror, own, got) + ((extra,) if first else ())
+        y_shape = jax.ShapeDtypeStruct((rows * cols, 4, WIDTH + LANES), jnp.int16)
+        operands = (mirror, own, got) + ((marks,) if first else ())
         y_msg = whole_call(pack_kernel, y_shape, operands, [], f"pack_{step}")
         y_msg = lax.all_to_all(y_msg, both, 0, 0, tiled=True)
         run = lambda *refs, first=first: update_kernel(first, rows, cols, *refs)
         if first:
-            x_msg, owner_back, owner_contrast = whole_call(
+            x_msg, owner_contrast = whole_call(
                 run,
-                (
-                    message,
-                    jax.ShapeDtypeStruct((cols, 5, 4, LANES), F32),
-                    jax.ShapeDtypeStruct((cols, 2, 3, 4, LANES), F32),
-                ),
+                (message, jax.ShapeDtypeStruct((cols, 2, 3, 4, LANES), F32)),
                 (y_msg,),
                 [],
                 f"update_{step}",
             )
         elif not final:
-            operands = (y_msg, owner_back, owner_contrast)
-            x_msg = whole_call(run, message, operands, [], f"update_{step}")
+            x_msg = whole_call(run, message, (y_msg, owner_contrast), [], f"update_{step}")
         else:
             run = lambda *refs: last_kernel(rows, cols, *refs)
             x_shape = jax.ShapeDtypeStruct((rows * cols, 4, 2 * MAIN + LANES), jnp.int16)

time: 112 us -> 113 us (level)
  no operation moved by 1% of the time
where the time goes in v7:
time: 113 us; the launch traced here: 112 us
  blocking collectives  83 us (73%)
  Pallas kernels  12.5 us (11%)
  local copies, waits for them, and re-layouts  8.21 us (7%)
  starting transfers between devices  5.68 us (5%)
    all_to_all x3, blocking collectives, local_owners(): y_msg = lax.all_to_all(y_msg, both, 0, 0, tiled=True)  44.9 us
    all_to_all x3, blocking collectives, local_owners(): x_msg = lax.all_to_all(x_msg, both, 0, 0, tiled=True)  38 us
    pallas_call x15, Pallas kernels, whole_call(): pl.pallas_call(kernel, out_shape=out_shape, in_specs=[vmem] * len(operand...  12.5 us
    unnamed x7, local copies, waits for them, and re-layouts  6.91 us
    ppermute x3, starting transfers between devices, local_owners(): arrived.append(lax.ppermute(start, both, pairs))  3.96 us
  transfers between devices with their start and end apart: 9, of which 1 were waited for; matrix products, arithmetic and copies ran while one was open for 0% of the time, Pallas kernels for 9%

profile of v7, /device:TPU:0, one launch (start us, length us, event | category | flops | bytes accessed | tf_op | source)
XLA Modules:
  0.0 112.2 jit_solution(6938266458993676719)
XLA Ops:
  0.0 1.1 copy.13
  1.1 0.8 select_select_fusion.1.refs_0_.small_ref
  1.9 0.3 start.1
  2.3 4.0 %collective-permute-start.2 = (bf16[64,1152]{1,0:T(8,128)(2,1)S(1)}, bf16[64,1152]{1,0:T(8,128)(2,1)S(1)}, u32[]{:S(2)}, u32[]{:S(2)}) collective-permute-start(bf16[64,1152]{1,0:T(8,128)(2,1)S(1)} %get-tuple-element.23.refs_2_), channel_id=1, source_target_pairs={{0,6},{1,7},{2,3},{3,2},{4,5},{5,4},{6,0},{7,1},{8,10},{9,11},{10,... | collective-permute-start | bytes 442376 | tf_op jit(solution)/shard_map/ppermute | solution.py:467
  6.2 0.0 collective-permute-start.1
  6.2 0.0 collective-permute-start
  7.0 0.0 copy-start
  7.0 2.5 %copy-done = bf16[1,1,12,2,288,288]{5,4,3,2,1,0:T(8,128)(2,1)S(1)} copy-done((bf16[1,1,12,2,288,288]{5,4,3,2,1,0:T(8,128)(2,1)S(1)}, bf16[1,1,12,2,288,288]{5,4,3,2,1,0:T(8,128)(2,1)}, u32[]{:S(2)}) %copy-start) | copy-done | bytes 3981336
  9.5 1.9 %direct_0.1 = (f32[4,64,288]{2,1,0:T(8,128)S(1)}, f32[64,1152]{1,0:T(8,128)S(1)}) custom-call(s32[4,128]{1,0:T(4,128)S(1)} %pad_add_fusion.refs_0_, bf16[12,2,288,288]{3,2,1,0:T(8,128)(2,1)S(1)} %bitcast.18, bf16[64,1152]{1,0:T(8,128)(2,1)S(1)} %get-tuple-element.23.refs_2_), custom_call_target="tpu_custom_call" | custom-call | tf_op jit(solution)/shard_map/direct_0/pallas_call | solution.py:390
  11.4 0.1 collective-permute-start.4
  11.5 0.0 copy-start.1
  11.5 2.5 %copy-done.1 = bf16[1,1,12,2,288,288]{5,4,3,2,1,0:T(8,128)(2,1)S(1)} copy-done((bf16[1,1,12,2,288,288]{5,4,3,2,1,0:T(8,128)(2,1)S(1)}, bf16[1,1,12,2,288,288]{5,4,3,2,1,0:T(8,128)(2,1)}, u32[]{:S(2)}) %copy-start.1) | copy-done | bytes 3981336
  14.0 0.1 share.1
  14.1 0.0 collective-permute-done.2
  14.1 0.0 collective-permute-done.1
  14.1 0.0 collective-permute-done
  14.2 0.5 collective-permute-start.3
  14.7 1.0 collective-permute-done.3.refs_3_
  15.7 0.8 copy-done.2
  16.5 1.3 %mirror_0.1.mirror_ref = f32[4,64,288]{2,1,0:T(8,128)S(1)} custom-call(s32[4,128]{1,0:T(4,128)S(1)} %pad_add_fusion.refs_0_, bf16[12,2,288,288]{3,2,1,0:T(8,128)(2,1)S(1)} %bitcast.20, bf16[64,1152]{1,0:T(8,128)(2,1)S(1)} %select_select_fusion.refs_2_, bf16[64,1152]{1,0:T(8,128)(2,1)S(1)} %collective-permute-done.3.refs_3_, ...), custom_call_target="tpu_custom_call" | custom-call | tf_op jit(solution)/shard_map/mirror_0/pallas_call | solution.py:390
  17.8 0.0 collective-permute-done.4.got_ref
  17.8 0.4 pack_0.1
  18.2 16.7 %all_to_all.30.refs_0_ = s16[32,4,1280]{2,1,0:T(4,128)(2,1)S(1)} all-to-all(s16[32,4,1280]{2,1,0:T(4,128)(2,1)S(1)} %pack_0.1), channel_id=1, replica_groups=mesh['row'=4,'col'=8] {'row','col'}, dimensions={0} | all-to-all | bytes 655360 | tf_op jit(solution)/shard_map/all_to_all | solution.py:517
  34.9 0.4 update_0.1
  35.3 13.6 %all_to_all.31.refs_2_ = bf16[32,4,1152]{2,1,0:T(4,128)(2,1)S(1)} all-to-all(bf16[32,4,1152]{2,1,0:T(4,128)(2,1)S(1)} %get-tuple-element.31), channel_id=1, replica_groups=mesh['row'=4,'col'=8] {'row','col'}, dimensions={0} | all-to-all | bytes 589824 | tf_op jit(solution)/shard_map/all_to_all | solution.py:533
  48.9 0.0 collective-permute-start.5
  48.9 1.9 %direct_1.1 = (f32[4,64,288]{2,1,0:T(8,128)S(1)}, f32[64,1152]{1,0:T(8,128)S(1)}) custom-call(s32[4,128]{1,0:T(4,128)S(1)} %pad_add_fusion.refs_0_, bf16[12,2,288,288]{3,2,1,0:T(8,128)(2,1)S(1)} %bitcast.21, bf16[32,4,1152]{2,1,0:T(4,128)(2,1)S(1)} %all_to_all.31.refs_2_), custom_call_target="tpu_custom_call" | custom-call | tf_op jit(solution)/shard_map/direct_1/pallas_call | solution.py:390
  50.9 0.6 collective-permute-start.6
  51.4 0.0 collective-permute-done.5.refs_3_
  51.4 1.3 %mirror_1.1.mirror_ref = f32[4,64,288]{2,1,0:T(8,128)S(1)} custom-call(s32[4,128]{1,0:T(4,128)S(1)} %pad_add_fusion.refs_0_, bf16[12,2,288,288]{3,2,1,0:T(8,128)(2,1)S(1)} %bitcast.22, bf16[32,4,1152]{2,1,0:T(4,128)(2,1)S(1)} %all_to_all.31.refs_2_, bf16[32,4,1152]{2,1,0:T(4,128)(2,1)S(1)} %collective-permute-done.5.refs_3_, ...), custom_call_target="tpu_custom_call" | custom-call | tf_op jit(solution)/shard_map/mirror_1/pallas_call | solution.py:390
  52.8 0.0 collective-permute-done.6.got_ref
  52.8 0.3 pack_1.1
  53.2 14.1 %all_to_all.32.refs_0_ = s16[32,4,1280]{2,1,0:T(4,128)(2,1)S(1)} all-to-all(s16[32,4,1280]{2,1,0:T(4,128)(2,1)S(1)} %pack_1.1), channel_id=1, replica_groups=mesh['row'=4,'col'=8] {'row','col'}, dimensions={0} | all-to-all | bytes 655360 | tf_op jit(solution)/shard_map/all_to_all | solution.py:517
  67.3 0.4 update_1.1
  67.7 13.6 %all_to_all.33.refs_2_ = bf16[32,4,1152]{2,1,0:T(4,128)(2,1)S(1)} all-to-all(bf16[32,4,1152]{2,1,0:T(4,128)(2,1)S(1)} %update_1.1), channel_id=1, replica_groups=mesh['row'=4,'col'=8] {'row','col'}, dimensions={0} | all-to-all | bytes 589824 | tf_op jit(solution)/shard_map/all_to_all | solution.py:533
  81.3 0.0 collective-permute-start.7
  81.3 1.9 %direct_2.1 = (f32[4,64,288]{2,1,0:T(8,128)S(1)}, f32[64,1152]{1,0:T(8,128)S(1)}) custom-call(s32[4,128]{1,0:T(4,128)S(1)} %pad_add_fusion.refs_0_, bf16[12,2,288,288]{3,2,1,0:T(8,128)(2,1)S(1)} %bitcast.23, bf16[32,4,1152]{2,1,0:T(4,128)(2,1)S(1)} %all_to_all.33.refs_2_), custom_call_target="tpu_custom_call" | custom-call | tf_op jit(solution)/shard_map/direct_2/pallas_call | solution.py:390
  83.3 0.6 collective-permute-start.8
  83.9 0.0 collective-permute-done.7.refs_3_
  83.9 1.3 %mirror_2.1.mirror_ref = f32[4,64,288]{2,1,0:T(8,128)S(1)} custom-call(s32[4,128]{1,0:T(4,128)S(1)} %pad_add_fusion.refs_0_, bf16[12,2,288,288]{3,2,1,0:T(8,128)(2,1)S(1)} %bitcast.24, bf16[32,4,1152]{2,1,0:T(4,128)(2,1)S(1)} %all_to_all.33.refs_2_, bf16[32,4,1152]{2,1,0:T(4,128)(2,1)S(1)} %collective-permute-done.7.refs_3_), custom_call_target="tpu_custom_call" | custom-call | tf_op jit(solution)/shard_map/mirror_2/pallas_call | solution.py:390
  85.2 0.0 collective-permute-done.8.got_ref
  85.2 0.3 pack_2.1
  85.5 14.1 %all_to_all.34.refs_0_ = s16[32,4,1280]{2,1,0:T(4,128)(2,1)S(1)} all-to-all(s16[32,4,1280]{2,1,0:T(4,128)(2,1)S(1)} %pack_2.1), channel_id=1, replica_groups=mesh['row'=4,'col'=8] {'row','col'}, dimensions={0} | all-to-all | bytes 655360 | tf_op jit(solution)/shard_map/all_to_all | solution.py:517
  99.7 0.3 last.1
  100.0 10.8 %all_to_all.35.msg_ref = s16[32,4,640]{2,1,0:T(4,128)(2,1)S(1)} all-to-all(s16[32,4,640]{2,1,0:T(4,128)(2,1)S(1)} %last.1), channel_id=1, replica_groups=mesh['row'=4,'col'=8] {'row','col'}, dimensions={0} | all-to-all | bytes 327680 | tf_op jit(solution)/shard_map/all_to_all | solution.py:533
  110.8 0.1 finish.1
  110.9 0.3 copy.14
  111.2 1.0 broadcast_in_dim.12
  (8 shorter events, 0.1 us)
Async XLA Ops:
  2.3 11.8 %collective-permute-start.2 = (bf16[64,1152]{1,0:T(8,128)(2,1)S(1)}, bf16[64,1152]{1,0:T(8,128)(2,1)S(1)}, u32[]{:S(2)}, u32[]{:S(2)}) collective-permute-start(bf16[64,1152]{1,0:T(8,128)(2,1)S(1)} %get-tuple-element.23.refs_2_), channel_id=1, source_target_pairs={{0,6},{1,7},{2,3},{3,2},{4,5},{5,4},{6,0},{7,1},{8,10},{9,11},{10,... | collective-permute-start | bytes 442376 | tf_op jit(solution)/shard_map/ppermute | solution.py:467
  6.2 7.9 %collective-permute-start.1 = (bf16[64,1152]{1,0:T(8,128)(2,1)S(1)}, bf16[64,1152]{1,0:T(8,128)(2,1)S(1)}, u32[]{:S(2)}, u32[]{:S(2)}) collective-permute-start(bf16[64,1152]{1,0:T(8,128)(2,1)S(1)} %get-tuple-element.23.refs_2_), channel_id=1, source_target_pairs={{0,4},{1,5},{2,3},{3,2},{4,0},{5,1},{6,7},{7,6},{8,9},{9,8},{10,14... | collective-permute-start | bytes 442376 | tf_op jit(solution)/shard_map/ppermute | solution.py:467
  6.2 7.9 %collective-permute-start = (bf16[64,1152]{1,0:T(8,128)(2,1)S(1)}, bf16[64,1152]{1,0:T(8,128)(2,1)S(1)}, u32[]{:S(2)}, u32[]{:S(2)}) collective-permute-start(bf16[64,1152]{1,0:T(8,128)(2,1)S(1)} %get-tuple-element.23.refs_2_), channel_id=1, source_target_pairs={{0,2},{1,3},{2,0},{3,1},{4,5},{5,4},{6,7},{7,6},{8,9},{9,8},{10,12... | collective-permute-start | bytes 442376 | tf_op jit(solution)/shard_map/ppermute | solution.py:467
  7.0 2.5 %copy-start = (bf16[1,1,12,2,288,288]{5,4,3,2,1,0:T(8,128)(2,1)S(1)}, bf16[1,1,12,2,288,288]{5,4,3,2,1,0:T(8,128)(2,1)}, u32[]{:S(2)}) copy-start(bf16[1,1,12,2,288,288]{5,4,3,2,1,0:T(8,128)(2,1)} %param.7) | copy-start | bytes 11943940
  11.4 6.5 %collective-permute-start.4 = (f32[64,1152]{1,0:T(8,128)S(1)}, f32[64,1152]{1,0:T(8,128)S(1)}, u32[]{:S(2)}, u32[]{:S(2)}) collective-permute-start(f32[64,1152]{1,0:T(8,128)S(1)} %get-tuple-element.29), channel_id=1, source_target_pairs={{0,1},{1,0},{2,3},{3,2},{4,5},{5,4},{6,7},{7,6},{8,9},{9,8},{10,11... | collective-permute-start | bytes 884744 | tf_op jit(solution)/shard_map/ppermute | solution.py:503
  11.5 2.5 %copy-start.1 = (bf16[1,1,12,2,288,288]{5,4,3,2,1,0:T(8,128)(2,1)S(1)}, bf16[1,1,12,2,288,288]{5,4,3,2,1,0:T(8,128)(2,1)}, u32[]{:S(2)}) copy-start(bf16[1,1,12,2,288,288]{5,4,3,2,1,0:T(8,128)(2,1)} %param.7) | copy-start | bytes 11943940
  14.0 2.5 %copy-start.2 = (bf16[1,1,12,2,288,288]{5,4,3,2,1,0:T(8,128)(2,1)S(1)}, bf16[1,1,12,2,288,288]{5,4,3,2,1,0:T(8,128)(2,1)}, u32[]{:S(2)}) copy-start(bf16[1,1,12,2,288,288]{5,4,3,2,1,0:T(8,128)(2,1)} %param.7) | copy-start | bytes 11943940
  14.2 1.5 %collective-permute-start.3 = (bf16[64,1152]{1,0:T(8,128)(2,1)S(1)}, bf16[64,1152]{1,0:T(8,128)(2,1)S(1)}, u32[]{:S(2)}, u32[]{:S(2)}) collective-permute-start(bf16[64,1152]{1,0:T(8,128)(2,1)S(1)} %select_select_fusion.refs_2_), channel_id=1, source_target_pairs={{0,1},{1,0},{2,3},{3,2},{4,5},{5,4},{6,7},{7,6},{8,9},{9,8},{10,11... | collective-permute-start | bytes 442376 | tf_op jit(solution)/shard_map/ppermute | solution.py:482
  48.9 2.5 %collective-permute-start.5 = (bf16[32,4,1152]{2,1,0:T(4,128)(2,1)S(1)}, bf16[32,4,1152]{2,1,0:T(4,128)(2,1)S(1)}, u32[]{:S(2)}, u32[]{:S(2)}) collective-permute-start(bf16[32,4,1152]{2,1,0:T(4,128)(2,1)S(1)} %all_to_all.31.refs_2_), channel_id=1, source_target_pairs={{0,1},{1,0},{2,3},{3,2},{4,5},{5,4},{6,7},{7,6},{8,9},{9,8},{10,11... | collective-permute-start | bytes 884744 | tf_op jit(solution)/shard_map/ppermute | solution.py:492
  50.9 1.9 %collective-permute-start.6 = (f32[64,1152]{1,0:T(8,128)S(1)}, f32[64,1152]{1,0:T(8,128)S(1)}, u32[]{:S(2)}, u32[]{:S(2)}) collective-permute-start(f32[64,1152]{1,0:T(8,128)S(1)} %get-tuple-element.33), channel_id=1, source_target_pairs={{0,1},{1,0},{2,3},{3,2},{4,5},{5,4},{6,7},{7,6},{8,9},{9,8},{10,11... | collective-permute-start | bytes 884744 | tf_op jit(solution)/shard_map/ppermute | solution.py:503
  81.3 2.5 %collective-permute-start.7 = (bf16[32,4,1152]{2,1,0:T(4,128)(2,1)S(1)}, bf16[32,4,1152]{2,1,0:T(4,128)(2,1)S(1)}, u32[]{:S(2)}, u32[]{:S(2)}) collective-permute-start(bf16[32,4,1152]{2,1,0:T(4,128)(2,1)S(1)} %all_to_all.33.refs_2_), channel_id=1, source_target_pairs={{0,1},{1,0},{2,3},{3,2},{4,5},{5,4},{6,7},{7,6},{8,9},{9,8},{10,11... | collective-permute-start | bytes 884744 | tf_op jit(solution)/shard_map/ppermute | solution.py:492
  83.3 1.9 %collective-permute-start.8 = (f32[64,1152]{1,0:T(8,128)S(1)}, f32[64,1152]{1,0:T(8,128)S(1)}, u32[]{:S(2)}, u32[]{:S(2)}) collective-permute-start(f32[64,1152]{1,0:T(8,128)S(1)} %get-tuple-element.36), channel_id=1, source_target_pairs={{0,1},{1,0},{2,3},{3,2},{4,5},{5,4},{6,7},{7,6},{8,9},{9,8},{10,11... | collective-permute-start | bytes 884744 | tf_op jit(solution)/shard_map/ppermute | solution.py:503

commit v8 on v7

--- a/solution.py
+++ b/solution.py
@@ -205,13 +205,10 @@
         marks = []
         for part in range(2):
             value = contrast_ref[part, q : q + 1] * 2.0**15
-            marks += [jnp.round(value), (value - jnp.round(value)) * 2.0**16]
-        marks = jnp.concatenate([whole(part) for part in marks], axis=0)
+            rest = (value - jnp.round(value)) * 2.0**16
+            marks += [jnp.round(value), jnp.clip(jnp.round(rest), -32767.0, 32767.0)]
+        marks = jnp.concatenate(marks, axis=0)
         marks_ref[q] = jnp.concatenate([marks, jnp.zeros((4, LANES - cells), F32)], axis=1)
-
-
-def whole(value):
-    return jnp.clip(jnp.round(value), -32767.0, 32767.0)
 
 
 def as_integers(value):
@@ -252,24 +249,28 @@
 
 def pack_kernel(mirror_ref, own_ref, got_ref, *rest):
     msg_ref = rest[-1]
+    coded = msg_ref.dtype != BF
     blocks, rows, _ = own_ref.shape
     half = rows // 2
-    lane = lax.broadcasted_iota(jnp.int32, (4, LANES), 1)
+    lane = lax.broadcasted_iota(jnp.int32, (half, LANES), 1)
     got = side_by_side(got_ref)
     for q in range(blocks):
         halves = [own_ref[q] + got[q], mirror_ref[q]]
         parts = [value[p * half : (p + 1) * half] for value in halves for p in range(2)]
-        power, scale = row_power(parts)
-        parts = [whole(part * scale) for part in parts]
-        ends = jnp.concatenate([part[:, MAIN:] for part in parts], axis=1)
-        marks = rest[0][q] if len(rest) == 2 else jnp.zeros((4, LANES), F32)
+        if coded:
+            power, scale = row_power(parts)
+            parts = [jnp.round(part * scale) for part in parts]
+        parts = [part[:, :MAIN] for part in parts] + [jnp.concatenate([part[:, MAIN:] for part in parts], axis=1)]
+        if coded:
+            marks = jnp.concatenate([rest[0][q]] * (half // 4), axis=0) if len(rest) == 2 else 0.0
+            parts.append(jnp.where(lane == POWER, power, marks))
+            parts = [part.astype(jnp.int32) for part in parts]
         for g in range(half // 4):
             at = slice(4 * g, 4 * g + 4)
             d = q * (half // 4) + g
             for k, part in enumerate(parts):
-                msg_ref[d, :, k * MAIN : (k + 1) * MAIN] = as_integers(part[at, :MAIN])
-            msg_ref[d, :, ENDS:WIDTH] = as_integers(ends[at])
-            msg_ref[d, :, WIDTH:] = as_integers(jnp.where(lane == POWER, power[at], marks))
+                lanes = slice(k * MAIN, (k + 1) * MAIN) if k < 4 else slice(ENDS + (k - 4) * LANES, ENDS + (k - 3) * LANES)
+                msg_ref[d, :, lanes] = part[at].astype(msg_ref.dtype)
 
 
 def row_power(parts):
@@ -277,13 +278,14 @@
     for part in parts[1:]:
         most = jnp.maximum(most, jnp.abs(part))
     most = jnp.max(most, axis=1, keepdims=True)
-    power = jnp.floor(jnp.log2(jnp.maximum(most, SMALLEST)))
+    power = jnp.floor(jnp.log2(jnp.maximum(most, SMALLEST)) + 2.0**-12)
     return power, jnp.exp2(14.0 - power)
 
 
 def partial_sums(msg_ref, rows, cols):
     direct = {}
     mirror = {}
+    coded = msg_ref.dtype != BF
 
     def add(store, key, value):
         store[key] = store[key] + value if key in store else value
@@ -292,9 +294,11 @@
         for c in range(cols):
             d = r * cols + c
             j = 2 * r + c % 2
-            scale = jnp.exp2(as_floats(msg_ref[d, :, WIDTH : WIDTH + LANES])[:, POWER : POWER + 1] - 14.0)
+            if coded:
+                scale = jnp.exp2(as_floats(msg_ref[d, :, WIDTH : WIDTH + LANES])[:, POWER : POWER + 1] - 14.0)
             for k in range(9):
-                value = as_floats(msg_ref[d, :, k * LANES : (k + 1) * LANES]) * scale
+                value = msg_ref[d, :, k * LANES : (k + 1) * LANES]
+                value = as_floats(value) * scale if coded else value.astype(F32)
                 if k < 4 or k == 8:
                     add(direct, (j, min(k, 4)), value)
                 if k >= 4:
@@ -358,10 +362,10 @@
             tail = jnp.where(mine, sums[j, 4], 0.0)
             power, scale = row_power([sums[j, 2 * p], sums[j, 2 * p + 1], tail])
             for k in range(2 * p, 2 * p + 2):
-                coded = as_integers(whole(sums[j, k] * scale))
+                coded = as_integers(jnp.round(sums[j, k] * scale))
                 for r in range(rows):
                     out_ref[r * cols + j, :, k * LANES : (k + 1) * LANES] = coded
-            ends = jnp.where(mine, whole(tail * scale), jnp.where(lane == 2 * TAIL + p, power, ends))
+            ends = jnp.where(mine, jnp.round(tail * scale), jnp.where(lane == 2 * TAIL + p, power, ends))
         coded = as_integers(ends)
         for r in range(rows):
             out_ref[r * cols + j, :, 2 * MAIN : 2 * MAIN + LANES] = coded
@@ -511,7 +515,7 @@
             ],
             f"mirror_{step}",
         )
-        y_shape = jax.ShapeDtypeStruct((rows * cols, 4, WIDTH + LANES), jnp.int16)
+        y_shape = message if final else jax.ShapeDtypeStruct((rows * cols, 4, WIDTH + LANES), jnp.int16)
         operands = (mirror, own, got) + ((marks,) if first else ())
         y_msg = whole_call(pack_kernel, y_shape, operands, [], f"pack_{step}")
         y_msg = lax.all_to_all(y_msg, both, 0, 0, tiled=True)

time: 113 us -> 112 us (level)
  no operation moved by 1% of the time
where the time goes in v8:
time: 112 us; the launch traced here: 111 us
  blocking collectives  82.3 us (73%)
  Pallas kernels  12.2 us (11%)
  local copies, waits for them, and re-layouts  8.21 us (7%)
  starting transfers between devices  5.69 us (5%)
    all_to_all x3, blocking collectives, local_owners(): y_msg = lax.all_to_all(y_msg, both, 0, 0, tiled=True)  44.3 us
    all_to_all x3, blocking collectives, local_owners(): x_msg = lax.all_to_all(x_msg, both, 0, 0, tiled=True)  37.9 us
    pallas_call x15, Pallas kernels, whole_call(): pl.pallas_call(kernel, out_shape=out_shape, in_specs=[vmem] * len(operand...  12.2 us
    unnamed x7, local copies, waits for them, and re-layouts  6.91 us
    ppermute x3, starting transfers between devices, local_owners(): arrived.append(lax.ppermute(start, both, pairs))  3.96 us
  transfers between devices with their start and end apart: 9, of which 1 were waited for; matrix products, arithmetic and copies ran while one was open for 0% of the time, Pallas kernels for 9%

profile of v8, /device:TPU:0, one launch (start us, length us, event | category | flops | bytes accessed | tf_op | source)
XLA Modules:
  0.0 111.2 jit_solution(13564333770859233545)
XLA Ops:
  0.0 1.1 copy.13
  1.1 0.8 select_select_fusion.1.refs_0_.small_ref
  1.9 0.3 start.1
  2.3 4.0 %collective-permute-start.2 = (bf16[64,1152]{1,0:T(8,128)(2,1)S(1)}, bf16[64,1152]{1,0:T(8,128)(2,1)S(1)}, u32[]{:S(2)}, u32[]{:S(2)}) collective-permute-start(bf16[64,1152]{1,0:T(8,128)(2,1)S(1)} %get-tuple-element.23.refs_2_), channel_id=1, source_target_pairs={{0,6},{1,7},{2,3},{3,2},{4,5},{5,4},{6,0},{7,1},{8,10},{9,11},{10,... | collective-permute-start | bytes 442376 | tf_op jit(solution)/shard_map/ppermute | solution.py:471
  6.2 0.0 collective-permute-start.1
  6.2 0.0 collective-permute-start
  7.0 0.0 copy-start
  7.0 2.5 %copy-done = bf16[1,1,12,2,288,288]{5,4,3,2,1,0:T(8,128)(2,1)S(1)} copy-done((bf16[1,1,12,2,288,288]{5,4,3,2,1,0:T(8,128)(2,1)S(1)}, bf16[1,1,12,2,288,288]{5,4,3,2,1,0:T(8,128)(2,1)}, u32[]{:S(2)}) %copy-start) | copy-done | bytes 3981336
  9.5 1.9 %direct_0.1 = (f32[4,64,288]{2,1,0:T(8,128)S(1)}, f32[64,1152]{1,0:T(8,128)S(1)}) custom-call(s32[4,128]{1,0:T(4,128)S(1)} %pad_add_fusion.refs_0_, bf16[12,2,288,288]{3,2,1,0:T(8,128)(2,1)S(1)} %bitcast.18, bf16[64,1152]{1,0:T(8,128)(2,1)S(1)} %get-tuple-element.23.refs_2_), custom_call_target="tpu_custom_call" | custom-call | tf_op jit(solution)/shard_map/direct_0/pallas_call | solution.py:394
  11.4 0.1 collective-permute-start.4
  11.5 0.0 copy-start.1
  11.5 2.5 %copy-done.1 = bf16[1,1,12,2,288,288]{5,4,3,2,1,0:T(8,128)(2,1)S(1)} copy-done((bf16[1,1,12,2,288,288]{5,4,3,2,1,0:T(8,128)(2,1)S(1)}, bf16[1,1,12,2,288,288]{5,4,3,2,1,0:T(8,128)(2,1)}, u32[]{:S(2)}) %copy-start.1) | copy-done | bytes 3981336
  14.0 0.1 share.1
  14.1 0.0 collective-permute-done.2
  14.1 0.0 collective-permute-done.1
  14.1 0.0 collective-permute-done
  14.2 0.5 collective-permute-start.3
  14.7 1.0 collective-permute-done.3.refs_3_
  15.7 0.8 copy-done.2
  16.5 1.3 %mirror_0.1.mirror_ref = f32[4,64,288]{2,1,0:T(8,128)S(1)} custom-call(s32[4,128]{1,0:T(4,128)S(1)} %pad_add_fusion.refs_0_, bf16[12,2,288,288]{3,2,1,0:T(8,128)(2,1)S(1)} %bitcast.20, bf16[64,1152]{1,0:T(8,128)(2,1)S(1)} %select_select_fusion.refs_2_, bf16[64,1152]{1,0:T(8,128)(2,1)S(1)} %collective-permute-done.3.refs_3_, ...), custom_call_target="tpu_custom_call" | custom-call | tf_op jit(solution)/shard_map/mirror_0/pallas_call | solution.py:394
  17.8 0.0 collective-permute-done.4.got_ref
  17.8 0.3 pack_0.1
  18.2 16.7 %all_to_all.30.refs_0_ = s16[32,4,1280]{2,1,0:T(4,128)(2,1)S(1)} all-to-all(s16[32,4,1280]{2,1,0:T(4,128)(2,1)S(1)} %pack_0.1), channel_id=1, replica_groups=mesh['row'=4,'col'=8] {'row','col'}, dimensions={0} | all-to-all | bytes 655360 | tf_op jit(solution)/shard_map/all_to_all | solution.py:521
  34.9 0.4 update_0.1
  35.3 13.6 %all_to_all.31.refs_2_ = bf16[32,4,1152]{2,1,0:T(4,128)(2,1)S(1)} all-to-all(bf16[32,4,1152]{2,1,0:T(4,128)(2,1)S(1)} %get-tuple-element.31), channel_id=1, replica_groups=mesh['row'=4,'col'=8] {'row','col'}, dimensions={0} | all-to-all | bytes 589824 | tf_op jit(solution)/shard_map/all_to_all | solution.py:537
  48.9 0.0 collective-permute-start.5
  48.9 1.9 %direct_1.1 = (f32[4,64,288]{2,1,0:T(8,128)S(1)}, f32[64,1152]{1,0:T(8,128)S(1)}) custom-call(s32[4,128]{1,0:T(4,128)S(1)} %pad_add_fusion.refs_0_, bf16[12,2,288,288]{3,2,1,0:T(8,128)(2,1)S(1)} %bitcast.21, bf16[32,4,1152]{2,1,0:T(4,128)(2,1)S(1)} %all_to_all.31.refs_2_), custom_call_target="tpu_custom_call" | custom-call | tf_op jit(solution)/shard_map/direct_1/pallas_call | solution.py:394
  50.8 0.6 collective-permute-start.6
  51.4 0.0 collective-permute-done.5.refs_3_
  51.4 1.3 %mirror_1.1.mirror_ref = f32[4,64,288]{2,1,0:T(8,128)S(1)} custom-call(s32[4,128]{1,0:T(4,128)S(1)} %pad_add_fusion.refs_0_, bf16[12,2,288,288]{3,2,1,0:T(8,128)(2,1)S(1)} %bitcast.22, bf16[32,4,1152]{2,1,0:T(4,128)(2,1)S(1)} %all_to_all.31.refs_2_, bf16[32,4,1152]{2,1,0:T(4,128)(2,1)S(1)} %collective-permute-done.5.refs_3_, ...), custom_call_target="tpu_custom_call" | custom-call | tf_op jit(solution)/shard_map/mirror_1/pallas_call | solution.py:394
  52.8 0.0 collective-permute-done.6.got_ref
  52.8 0.3 pack_1.1
  53.1 14.1 %all_to_all.32.refs_0_ = s16[32,4,1280]{2,1,0:T(4,128)(2,1)S(1)} all-to-all(s16[32,4,1280]{2,1,0:T(4,128)(2,1)S(1)} %pack_1.1), channel_id=1, replica_groups=mesh['row'=4,'col'=8] {'row','col'}, dimensions={0} | all-to-all | bytes 655360 | tf_op jit(solution)/shard_map/all_to_all | solution.py:521
  67.2 0.4 update_1.1
  67.7 13.6 %all_to_all.33.refs_2_ = bf16[32,4,1152]{2,1,0:T(4,128)(2,1)S(1)} all-to-all(bf16[32,4,1152]{2,1,0:T(4,128)(2,1)S(1)} %update_1.1), channel_id=1, replica_groups=mesh['row'=4,'col'=8] {'row','col'}, dimensions={0} | all-to-all | bytes 589824 | tf_op jit(solution)/shard_map/all_to_all | solution.py:537
  81.3 0.0 collective-permute-start.7
  81.3 1.9 %direct_2.1 = (f32[4,64,288]{2,1,0:T(8,128)S(1)}, f32[64,1152]{1,0:T(8,128)S(1)}) custom-call(s32[4,128]{1,0:T(4,128)S(1)} %pad_add_fusion.refs_0_, bf16[12,2,288,288]{3,2,1,0:T(8,128)(2,1)S(1)} %bitcast.23, bf16[32,4,1152]{2,1,0:T(4,128)(2,1)S(1)} %all_to_all.33.refs_2_), custom_call_target="tpu_custom_call" | custom-call | tf_op jit(solution)/shard_map/direct_2/pallas_call | solution.py:394
  83.3 0.6 collective-permute-start.8
  83.8 0.0 collective-permute-done.7.refs_3_
  83.8 1.3 %mirror_2.1.mirror_ref = f32[4,64,288]{2,1,0:T(8,128)S(1)} custom-call(s32[4,128]{1,0:T(4,128)S(1)} %pad_add_fusion.refs_0_, bf16[12,2,288,288]{3,2,1,0:T(8,128)(2,1)S(1)} %bitcast.24, bf16[32,4,1152]{2,1,0:T(4,128)(2,1)S(1)} %all_to_all.33.refs_2_, bf16[32,4,1152]{2,1,0:T(4,128)(2,1)S(1)} %collective-permute-done.7.refs_3_), custom_call_target="tpu_custom_call" | custom-call | tf_op jit(solution)/shard_map/mirror_2/pallas_call | solution.py:394
  85.2 0.0 collective-permute-done.8.got_ref
  85.2 0.2 pack_2.1
  85.4 13.5 %all_to_all.34.refs_0_ = bf16[32,4,1152]{2,1,0:T(4,128)(2,1)S(1)} all-to-all(bf16[32,4,1152]{2,1,0:T(4,128)(2,1)S(1)} %pack_2.1), channel_id=1, replica_groups=mesh['row'=4,'col'=8] {'row','col'}, dimensions={0} | all-to-all | bytes 589824 | tf_op jit(solution)/shard_map/all_to_all | solution.py:521
  98.9 0.2 last.1
  99.1 10.7 %all_to_all.35.msg_ref = s16[32,4,640]{2,1,0:T(4,128)(2,1)S(1)} all-to-all(s16[32,4,640]{2,1,0:T(4,128)(2,1)S(1)} %last.1), channel_id=1, replica_groups=mesh['row'=4,'col'=8] {'row','col'}, dimensions={0} | all-to-all | bytes 327680 | tf_op jit(solution)/shard_map/all_to_all | solution.py:537
  109.8 0.1 finish.1
  109.9 0.3 copy.14
  110.2 1.0 broadcast_in_dim.12
  (8 shorter events, 0.1 us)
Async XLA Ops:
  2.3 11.8 %collective-permute-start.2 = (bf16[64,1152]{1,0:T(8,128)(2,1)S(1)}, bf16[64,1152]{1,0:T(8,128)(2,1)S(1)}, u32[]{:S(2)}, u32[]{:S(2)}) collective-permute-start(bf16[64,1152]{1,0:T(8,128)(2,1)S(1)} %get-tuple-element.23.refs_2_), channel_id=1, source_target_pairs={{0,6},{1,7},{2,3},{3,2},{4,5},{5,4},{6,0},{7,1},{8,10},{9,11},{10,... | collective-permute-start | bytes 442376 | tf_op jit(solution)/shard_map/ppermute | solution.py:471
  6.2 7.9 %collective-permute-start.1 = (bf16[64,1152]{1,0:T(8,128)(2,1)S(1)}, bf16[64,1152]{1,0:T(8,128)(2,1)S(1)}, u32[]{:S(2)}, u32[]{:S(2)}) collective-permute-start(bf16[64,1152]{1,0:T(8,128)(2,1)S(1)} %get-tuple-element.23.refs_2_), channel_id=1, source_target_pairs={{0,4},{1,5},{2,3},{3,2},{4,0},{5,1},{6,7},{7,6},{8,9},{9,8},{10,14... | collective-permute-start | bytes 442376 | tf_op jit(solution)/shard_map/ppermute | solution.py:471
  6.2 7.9 %collective-permute-start = (bf16[64,1152]{1,0:T(8,128)(2,1)S(1)}, bf16[64,1152]{1,0:T(8,128)(2,1)S(1)}, u32[]{:S(2)}, u32[]{:S(2)}) collective-permute-start(bf16[64,1152]{1,0:T(8,128)(2,1)S(1)} %get-tuple-element.23.refs_2_), channel_id=1, source_target_pairs={{0,2},{1,3},{2,0},{3,1},{4,5},{5,4},{6,7},{7,6},{8,9},{9,8},{10,12... | collective-permute-start | bytes 442376 | tf_op jit(solution)/shard_map/ppermute | solution.py:471
  7.0 2.5 %copy-start = (bf16[1,1,12,2,288,288]{5,4,3,2,1,0:T(8,128)(2,1)S(1)}, bf16[1,1,12,2,288,288]{5,4,3,2,1,0:T(8,128)(2,1)}, u32[]{:S(2)}) copy-start(bf16[1,1,12,2,288,288]{5,4,3,2,1,0:T(8,128)(2,1)} %param.7) | copy-start | bytes 11943940
  11.4 6.5 %collective-permute-start.4 = (f32[64,1152]{1,0:T(8,128)S(1)}, f32[64,1152]{1,0:T(8,128)S(1)}, u32[]{:S(2)}, u32[]{:S(2)}) collective-permute-start(f32[64,1152]{1,0:T(8,128)S(1)} %get-tuple-element.29), channel_id=1, source_target_pairs={{0,1},{1,0},{2,3},{3,2},{4,5},{5,4},{6,7},{7,6},{8,9},{9,8},{10,11... | collective-permute-start | bytes 884744 | tf_op jit(solution)/shard_map/ppermute | solution.py:507
  11.5 2.5 %copy-start.1 = (bf16[1,1,12,2,288,288]{5,4,3,2,1,0:T(8,128)(2,1)S(1)}, bf16[1,1,12,2,288,288]{5,4,3,2,1,0:T(8,128)(2,1)}, u32[]{:S(2)}) copy-start(bf16[1,1,12,2,288,288]{5,4,3,2,1,0:T(8,128)(2,1)} %param.7) | copy-start | bytes 11943940
  14.0 2.5 %copy-start.2 = (bf16[1,1,12,2,288,288]{5,4,3,2,1,0:T(8,128)(2,1)S(1)}, bf16[1,1,12,2,288,288]{5,4,3,2,1,0:T(8,128)(2,1)}, u32[]{:S(2)}) copy-start(bf16[1,1,12,2,288,288]{5,4,3,2,1,0:T(8,128)(2,1)} %param.7) | copy-start | bytes 11943940
  14.2 1.5 %collective-permute-start.3 = (bf16[64,1152]{1,0:T(8,128)(2,1)S(1)}, bf16[64,1152]{1,0:T(8,128)(2,1)S(1)}, u32[]{:S(2)}, u32[]{:S(2)}) collective-permute-start(bf16[64,1152]{1,0:T(8,128)(2,1)S(1)} %select_select_fusion.refs_2_), channel_id=1, source_target_pairs={{0,1},{1,0},{2,3},{3,2},{4,5},{5,4},{6,7},{7,6},{8,9},{9,8},{10,11... | collective-permute-start | bytes 442376 | tf_op jit(solution)/shard_map/ppermute | solution.py:486
  48.9 2.5 %collective-permute-start.5 = (bf16[32,4,1152]{2,1,0:T(4,128)(2,1)S(1)}, bf16[32,4,1152]{2,1,0:T(4,128)(2,1)S(1)}, u32[]{:S(2)}, u32[]{:S(2)}) collective-permute-start(bf16[32,4,1152]{2,1,0:T(4,128)(2,1)S(1)} %all_to_all.31.refs_2_), channel_id=1, source_target_pairs={{0,1},{1,0},{2,3},{3,2},{4,5},{5,4},{6,7},{7,6},{8,9},{9,8},{10,11... | collective-permute-start | bytes 884744 | tf_op jit(solution)/shard_map/ppermute | solution.py:496
  50.8 1.9 %collective-permute-start.6 = (f32[64,1152]{1,0:T(8,128)S(1)}, f32[64,1152]{1,0:T(8,128)S(1)}, u32[]{:S(2)}, u32[]{:S(2)}) collective-permute-start(f32[64,1152]{1,0:T(8,128)S(1)} %get-tuple-element.33), channel_id=1, source_target_pairs={{0,1},{1,0},{2,3},{3,2},{4,5},{5,4},{6,7},{7,6},{8,9},{9,8},{10,11... | collective-permute-start | bytes 884744 | tf_op jit(solution)/shard_map/ppermute | solution.py:507
  81.3 2.5 %collective-permute-start.7 = (bf16[32,4,1152]{2,1,0:T(4,128)(2,1)S(1)}, bf16[32,4,1152]{2,1,0:T(4,128)(2,1)S(1)}, u32[]{:S(2)}, u32[]{:S(2)}) collective-permute-start(bf16[32,4,1152]{2,1,0:T(4,128)(2,1)S(1)} %all_to_all.33.refs_2_), channel_id=1, source_target_pairs={{0,1},{1,0},{2,3},{3,2},{4,5},{5,4},{6,7},{7,6},{8,9},{9,8},{10,11... | collective-permute-start | bytes 884744 | tf_op jit(solution)/shard_map/ppermute | solution.py:496
  83.3 1.9 %collective-permute-start.8 = (f32[64,1152]{1,0:T(8,128)S(1)}, f32[64,1152]{1,0:T(8,128)S(1)}, u32[]{:S(2)}, u32[]{:S(2)}) collective-permute-start(f32[64,1152]{1,0:T(8,128)S(1)} %get-tuple-element.36), channel_id=1, source_target_pairs={{0,1},{1,0},{2,3},{3,2},{4,5},{5,4},{6,7},{7,6},{8,9},{9,8},{10,11... | collective-permute-start | bytes 884744 | tf_op jit(solution)/shard_map/ppermute | solution.py:507

commit v9 on v8

--- a/solution.py
+++ b/solution.py
@@ -479,11 +479,6 @@
         [],
         "share",
     )
-    marks, *arrived = lax.optimization_barrier((marks, *arrived))
-    row_mine = start
-    for hop in range(1, chips):
-        row_mine = jnp.where(c // 2 == (r + hop) % chips, arrived[hop - 1], row_mine)
-    row_other = lax.ppermute(row_mine, "col", core_pairs)
 
     part = jax.ShapeDtypeStruct((blocks,) + block, F32)
     message = jax.ShapeDtypeStruct((rows * cols, 4, WIDTH), BF)
@@ -491,7 +486,7 @@
         first = step == 0
         final = step + 1 == PRODUCTS
         if first:
-            direct_in, mirror_in = start, (row_mine, row_other)
+            direct_in = start
         else:
             direct_in, mirror_in = x_msg, (x_msg, lax.ppermute(x_msg, "col", core_pairs))
         own, other = whole_call(
@@ -504,6 +499,16 @@
             ],
             f"direct_{step}",
         )
+        if first:
+            marks, other, *arrived = lax.optimization_barrier((marks, other, *arrived))
+            row_mine = start
+            for hop in range(1, chips):
+                row_mine = jnp.where(c // 2 == (r + hop) % chips, arrived[hop - 1], row_mine)
+            row_other = lax.ppermute(row_mine, "col", core_pairs)
+            mirror_in = (row_mine, row_other)
+        if first:
+            other, *mirror_in = lax.optimization_barrier((other, *mirror_in))
+            mirror_in = tuple(mirror_in)
         got = lax.ppermute(other, "col", core_pairs)
         mirror = whole_call(
             lambda *refs, first=first: mirror_kernel(first, *refs),

time: 112 us -> 111 us (level)
    unnamed x7 -> x5, local copies, waits for them, and re-layouts: 6.91 us -> 5.99 us
  transfers between devices with their start and end apart: 9 -> 9, of which waited for: 1 -> 2; matrix products, arithmetic and copies ran while one was open for 0% -> 0% of each run, Pallas kernels for 9% -> 9%
where the time goes in v9:
time: 111 us; the launch traced here: 110 us
  blocking collectives  82.1 us (74%)
  Pallas kernels  12.2 us (11%)
  local copies, waits for them, and re-layouts  7.29 us (7%)
  starting transfers between devices  5.33 us (5%)
  waiting for transfers between devices  1.5 us (1%)
    all_to_all x3, blocking collectives, local_owners(): y_msg = lax.all_to_all(y_msg, both, 0, 0, tiled=True)  44.2 us
    all_to_all x3, blocking collectives, local_owners(): x_msg = lax.all_to_all(x_msg, both, 0, 0, tiled=True)  37.9 us
    pallas_call x15, Pallas kernels, whole_call(): pl.pallas_call(kernel, out_shape=out_shape, in_specs=[vmem] * len(operand...  12.2 us
    unnamed x5, local copies, waits for them, and re-layouts  5.99 us
    ppermute x3, starting transfers between devices, local_owners(): arrived.append(lax.ppermute(start, both, pairs))  3.96 us
  transfers between devices with their start and end apart: 9, of which 2 were waited for; matrix products, arithmetic and copies ran while one was open for 0% of the time, Pallas kernels for 9%

profile of v9, /device:TPU:0, one launch (start us, length us, event | category | flops | bytes accessed | tf_op | source)
XLA Modules:
  0.0 110.2 jit_solution(13556262630660588707)
XLA Ops:
  0.0 1.1 copy.13
  1.1 0.8 select_select_fusion.1.refs_0_.small_ref
  1.9 0.3 start.1
  2.3 4.0 %collective-permute-start.2 = (bf16[64,1152]{1,0:T(8,128)(2,1)S(1)}, bf16[64,1152]{1,0:T(8,128)(2,1)S(1)}, u32[]{:S(2)}, u32[]{:S(2)}) collective-permute-start(bf16[64,1152]{1,0:T(8,128)(2,1)S(1)} %get-tuple-element.27.refs_2_), channel_id=1, source_target_pairs={{0,6},{1,7},{2,3},{3,2},{4,5},{5,4},{6,0},{7,1},{8,10},{9,11},{10,... | collective-permute-start | bytes 442376 | tf_op jit(solution)/shard_map/ppermute | solution.py:471
  6.2 0.0 collective-permute-start.1
  6.2 0.0 collective-permute-start
  7.0 0.0 copy-start
  7.0 2.5 %copy-done = bf16[1,1,12,2,288,288]{5,4,3,2,1,0:T(8,128)(2,1)S(1)} copy-done((bf16[1,1,12,2,288,288]{5,4,3,2,1,0:T(8,128)(2,1)S(1)}, bf16[1,1,12,2,288,288]{5,4,3,2,1,0:T(8,128)(2,1)}, u32[]{:S(2)}) %copy-start) | copy-done | bytes 3981336
  9.5 0.0 copy-start.1
  9.5 0.1 share.1
  9.6 2.4 %copy-done.1 = bf16[1,1,12,2,288,288]{5,4,3,2,1,0:T(8,128)(2,1)S(1)} copy-done((bf16[1,1,12,2,288,288]{5,4,3,2,1,0:T(8,128)(2,1)S(1)}, bf16[1,1,12,2,288,288]{5,4,3,2,1,0:T(8,128)(2,1)}, u32[]{:S(2)}) %copy-start.1) | copy-done | bytes 3981336
  12.0 2.0 %direct_0.1 = (f32[4,64,288]{2,1,0:T(8,128)S(1)}, f32[64,1152]{1,0:T(8,128)S(1)}) custom-call(s32[4,128]{1,0:T(4,128)S(1)} %pad_add_fusion.refs_0_, bf16[12,2,288,288]{3,2,1,0:T(8,128)(2,1)S(1)} %bitcast.19, bf16[64,1152]{1,0:T(8,128)(2,1)S(1)} %get-tuple-element.27.refs_2_), custom_call_target="tpu_custom_call" | custom-call | tf_op jit(solution)/shard_map/direct_0/pallas_call | solution.py:394
  14.0 0.0 collective-permute-done.2
  14.0 0.0 collective-permute-done.1
  14.0 0.0 collective-permute-done
  14.0 0.1 collective-permute-start.3
  14.1 1.4 %collective-permute-done.3.refs_3_ = bf16[64,1152]{1,0:T(8,128)(2,1)S(1)} collective-permute-done((bf16[64,1152]{1,0:T(8,128)(2,1)S(1)}, bf16[64,1152]{1,0:T(8,128)(2,1)S(1)}, u32[]{:S(2)}, u32[]{:S(2)}) %collective-permute-start.3) | collective-permute-done | bytes 147488 | tf_op jit(solution)/shard_map/ppermute | solution.py:507
  15.5 0.1 collective-permute-start.4
  15.6 1.3 %mirror_0.1.mirror_ref = f32[4,64,288]{2,1,0:T(8,128)S(1)} custom-call(s32[4,128]{1,0:T(4,128)S(1)} %pad_add_fusion.refs_0_, bf16[12,2,288,288]{3,2,1,0:T(8,128)(2,1)S(1)} %bitcast.20, bf16[64,1152]{1,0:T(8,128)(2,1)S(1)} %select_select_fusion.refs_2_, bf16[64,1152]{1,0:T(8,128)(2,1)S(1)} %collective-permute-done.3.refs_3_, ...), custom_call_target="tpu_custom_call" | custom-call | tf_op jit(solution)/shard_map/mirror_0/pallas_call | solution.py:394
  16.9 0.1 collective-permute-done.4.got_ref
  17.0 0.3 pack_0.1
  17.4 16.5 %all_to_all.30.refs_0_ = s16[32,4,1280]{2,1,0:T(4,128)(2,1)S(1)} all-to-all(s16[32,4,1280]{2,1,0:T(4,128)(2,1)S(1)} %pack_0.1), channel_id=1, replica_groups=mesh['row'=4,'col'=8] {'row','col'}, dimensions={0} | all-to-all | bytes 655360 | tf_op jit(solution)/shard_map/all_to_all | solution.py:526
  33.9 0.4 update_0.1
  34.3 13.6 %all_to_all.31.refs_2_ = bf16[32,4,1152]{2,1,0:T(4,128)(2,1)S(1)} all-to-all(bf16[32,4,1152]{2,1,0:T(4,128)(2,1)S(1)} %get-tuple-element.39), channel_id=1, replica_groups=mesh['row'=4,'col'=8] {'row','col'}, dimensions={0} | all-to-all | bytes 589824 | tf_op jit(solution)/shard_map/all_to_all | solution.py:542
  47.9 0.0 collective-permute-start.5
  47.9 1.9 %direct_1.1 = (f32[4,64,288]{2,1,0:T(8,128)S(1)}, f32[64,1152]{1,0:T(8,128)S(1)}) custom-call(s32[4,128]{1,0:T(4,128)S(1)} %pad_add_fusion.refs_0_, bf16[12,2,288,288]{3,2,1,0:T(8,128)(2,1)S(1)} %bitcast.21, bf16[32,4,1152]{2,1,0:T(4,128)(2,1)S(1)} %all_to_all.31.refs_2_), custom_call_target="tpu_custom_call" | custom-call | tf_op jit(solution)/shard_map/direct_1/pallas_call | solution.py:394
  49.9 0.6 collective-permute-start.6
  50.4 0.0 collective-permute-done.5.refs_3_
  50.5 1.3 %mirror_1.1.mirror_ref = f32[4,64,288]{2,1,0:T(8,128)S(1)} custom-call(s32[4,128]{1,0:T(4,128)S(1)} %pad_add_fusion.refs_0_, bf16[12,2,288,288]{3,2,1,0:T(8,128)(2,1)S(1)} %bitcast.22, bf16[32,4,1152]{2,1,0:T(4,128)(2,1)S(1)} %all_to_all.31.refs_2_, bf16[32,4,1152]{2,1,0:T(4,128)(2,1)S(1)} %collective-permute-done.5.refs_3_, ...), custom_call_target="tpu_custom_call" | custom-call | tf_op jit(solution)/shard_map/mirror_1/pallas_call | solution.py:394
  51.8 0.0 collective-permute-done.6.got_ref
  51.8 0.3 pack_1.1
  52.2 14.1 %all_to_all.32.refs_0_ = s16[32,4,1280]{2,1,0:T(4,128)(2,1)S(1)} all-to-all(s16[32,4,1280]{2,1,0:T(4,128)(2,1)S(1)} %pack_1.1), channel_id=1, replica_groups=mesh['row'=4,'col'=8] {'row','col'}, dimensions={0} | all-to-all | bytes 655360 | tf_op jit(solution)/shard_map/all_to_all | solution.py:526
  66.3 0.4 update_1.1
  66.7 13.6 %all_to_all.33.refs_2_ = bf16[32,4,1152]{2,1,0:T(4,128)(2,1)S(1)} all-to-all(bf16[32,4,1152]{2,1,0:T(4,128)(2,1)S(1)} %update_1.1), channel_id=1, replica_groups=mesh['row'=4,'col'=8] {'row','col'}, dimensions={0} | all-to-all | bytes 589824 | tf_op jit(solution)/shard_map/all_to_all | solution.py:542
  80.3 0.0 collective-permute-start.7
  80.3 1.9 %direct_2.1 = (f32[4,64,288]{2,1,0:T(8,128)S(1)}, f32[64,1152]{1,0:T(8,128)S(1)}) custom-call(s32[4,128]{1,0:T(4,128)S(1)} %pad_add_fusion.refs_0_, bf16[12,2,288,288]{3,2,1,0:T(8,128)(2,1)S(1)} %bitcast.23, bf16[32,4,1152]{2,1,0:T(4,128)(2,1)S(1)} %all_to_all.33.refs_2_), custom_call_target="tpu_custom_call" | custom-call | tf_op jit(solution)/shard_map/direct_2/pallas_call | solution.py:394
  82.3 0.6 collective-permute-start.8
  82.9 0.0 collective-permute-done.7.refs_3_
  82.9 1.3 %mirror_2.1.mirror_ref = f32[4,64,288]{2,1,0:T(8,128)S(1)} custom-call(s32[4,128]{1,0:T(4,128)S(1)} %pad_add_fusion.refs_0_, bf16[12,2,288,288]{3,2,1,0:T(8,128)(2,1)S(1)} %bitcast.24, bf16[32,4,1152]{2,1,0:T(4,128)(2,1)S(1)} %all_to_all.33.refs_2_, bf16[32,4,1152]{2,1,0:T(4,128)(2,1)S(1)} %collective-permute-done.7.refs_3_), custom_call_target="tpu_custom_call" | custom-call | tf_op jit(solution)/shard_map/mirror_2/pallas_call | solution.py:394
  84.2 0.0 collective-permute-done.8.got_ref
  84.2 0.2 pack_2.1
  84.4 13.5 %all_to_all.34.refs_0_ = bf16[32,4,1152]{2,1,0:T(4,128)(2,1)S(1)} all-to-all(bf16[32,4,1152]{2,1,0:T(4,128)(2,1)S(1)} %pack_2.1), channel_id=1, replica_groups=mesh['row'=4,'col'=8] {'row','col'}, dimensions={0} | all-to-all | bytes 589824 | tf_op jit(solution)/shard_map/all_to_all | solution.py:526
  97.9 0.2 last.1
  98.1 10.7 %all_to_all.35.msg_ref = s16[32,4,640]{2,1,0:T(4,128)(2,1)S(1)} all-to-all(s16[32,4,640]{2,1,0:T(4,128)(2,1)S(1)} %last.1), channel_id=1, replica_groups=mesh['row'=4,'col'=8] {'row','col'}, dimensions={0} | all-to-all | bytes 327680 | tf_op jit(solution)/shard_map/all_to_all | solution.py:542
  108.8 0.1 finish.1
  109.0 0.3 copy.14
  109.2 1.0 broadcast_in_dim.12
  (7 shorter events, 0.1 us)
Async XLA Ops:
  2.3 11.7 %collective-permute-start.2 = (bf16[64,1152]{1,0:T(8,128)(2,1)S(1)}, bf16[64,1152]{1,0:T(8,128)(2,1)S(1)}, u32[]{:S(2)}, u32[]{:S(2)}) collective-permute-start(bf16[64,1152]{1,0:T(8,128)(2,1)S(1)} %get-tuple-element.27.refs_2_), channel_id=1, source_target_pairs={{0,6},{1,7},{2,3},{3,2},{4,5},{5,4},{6,0},{7,1},{8,10},{9,11},{10,... | collective-permute-start | bytes 442376 | tf_op jit(solution)/shard_map/ppermute | solution.py:471
  6.2 7.7 %collective-permute-start.1 = (bf16[64,1152]{1,0:T(8,128)(2,1)S(1)}, bf16[64,1152]{1,0:T(8,128)(2,1)S(1)}, u32[]{:S(2)}, u32[]{:S(2)}) collective-permute-start(bf16[64,1152]{1,0:T(8,128)(2,1)S(1)} %get-tuple-element.27.refs_2_), channel_id=1, source_target_pairs={{0,4},{1,5},{2,3},{3,2},{4,0},{5,1},{6,7},{7,6},{8,9},{9,8},{10,14... | collective-permute-start | bytes 442376 | tf_op jit(solution)/shard_map/ppermute | solution.py:471
  6.2 7.8 %collective-permute-start = (bf16[64,1152]{1,0:T(8,128)(2,1)S(1)}, bf16[64,1152]{1,0:T(8,128)(2,1)S(1)}, u32[]{:S(2)}, u32[]{:S(2)}) collective-permute-start(bf16[64,1152]{1,0:T(8,128)(2,1)S(1)} %get-tuple-element.27.refs_2_), channel_id=1, source_target_pairs={{0,2},{1,3},{2,0},{3,1},{4,5},{5,4},{6,7},{7,6},{8,9},{9,8},{10,12... | collective-permute-start | bytes 442376 | tf_op jit(solution)/shard_map/ppermute | solution.py:471
  7.0 2.5 %copy-start = (bf16[1,1,12,2,288,288]{5,4,3,2,1,0:T(8,128)(2,1)S(1)}, bf16[1,1,12,2,288,288]{5,4,3,2,1,0:T(8,128)(2,1)}, u32[]{:S(2)}) copy-start(bf16[1,1,12,2,288,288]{5,4,3,2,1,0:T(8,128)(2,1)} %param.7) | copy-start | bytes 11943940
  9.5 2.5 %copy-start.1 = (bf16[1,1,12,2,288,288]{5,4,3,2,1,0:T(8,128)(2,1)S(1)}, bf16[1,1,12,2,288,288]{5,4,3,2,1,0:T(8,128)(2,1)}, u32[]{:S(2)}) copy-start(bf16[1,1,12,2,288,288]{5,4,3,2,1,0:T(8,128)(2,1)} %param.7) | copy-start | bytes 11943940
  14.0 1.4 %collective-permute-start.3 = (bf16[64,1152]{1,0:T(8,128)(2,1)S(1)}, bf16[64,1152]{1,0:T(8,128)(2,1)S(1)}, u32[]{:S(2)}, u32[]{:S(2)}) collective-permute-start(bf16[64,1152]{1,0:T(8,128)(2,1)S(1)} %select_select_fusion.refs_2_), channel_id=1, source_target_pairs={{0,1},{1,0},{2,3},{3,2},{4,5},{5,4},{6,7},{7,6},{8,9},{9,8},{10,11... | collective-permute-start | bytes 442376 | tf_op jit(solution)/shard_map/ppermute | solution.py:507
  15.5 1.6 %collective-permute-start.4 = (f32[64,1152]{1,0:T(8,128)S(1)}, f32[64,1152]{1,0:T(8,128)S(1)}, u32[]{:S(2)}, u32[]{:S(2)}) collective-permute-start(f32[64,1152]{1,0:T(8,128)S(1)} %get-tuple-element.37), channel_id=1, source_target_pairs={{0,1},{1,0},{2,3},{3,2},{4,5},{5,4},{6,7},{7,6},{8,9},{9,8},{10,11... | collective-permute-start | bytes 884744 | tf_op jit(solution)/shard_map/ppermute | solution.py:512
  47.9 2.5 %collective-permute-start.5 = (bf16[32,4,1152]{2,1,0:T(4,128)(2,1)S(1)}, bf16[32,4,1152]{2,1,0:T(4,128)(2,1)S(1)}, u32[]{:S(2)}, u32[]{:S(2)}) collective-permute-start(bf16[32,4,1152]{2,1,0:T(4,128)(2,1)S(1)} %all_to_all.31.refs_2_), channel_id=1, source_target_pairs={{0,1},{1,0},{2,3},{3,2},{4,5},{5,4},{6,7},{7,6},{8,9},{9,8},{10,11... | collective-permute-start | bytes 884744 | tf_op jit(solution)/shard_map/ppermute | solution.py:491
  49.9 1.9 %collective-permute-start.6 = (f32[64,1152]{1,0:T(8,128)S(1)}, f32[64,1152]{1,0:T(8,128)S(1)}, u32[]{:S(2)}, u32[]{:S(2)}) collective-permute-start(f32[64,1152]{1,0:T(8,128)S(1)} %get-tuple-element.41), channel_id=1, source_target_pairs={{0,1},{1,0},{2,3},{3,2},{4,5},{5,4},{6,7},{7,6},{8,9},{9,8},{10,11... | collective-permute-start | bytes 884744 | tf_op jit(solution)/shard_map/ppermute | solution.py:512
  80.3 2.5 %collective-permute-start.7 = (bf16[32,4,1152]{2,1,0:T(4,128)(2,1)S(1)}, bf16[32,4,1152]{2,1,0:T(4,128)(2,1)S(1)}, u32[]{:S(2)}, u32[]{:S(2)}) collective-permute-start(bf16[32,4,1152]{2,1,0:T(4,128)(2,1)S(1)} %all_to_all.33.refs_2_), channel_id=1, source_target_pairs={{0,1},{1,0},{2,3},{3,2},{4,5},{5,4},{6,7},{7,6},{8,9},{9,8},{10,11... | collective-permute-start | bytes 884744 | tf_op jit(solution)/shard_map/ppermute | solution.py:491
  82.3 1.9 %collective-permute-start.8 = (f32[64,1152]{1,0:T(8,128)S(1)}, f32[64,1152]{1,0:T(8,128)S(1)}, u32[]{:S(2)}, u32[]{:S(2)}) collective-permute-start(f32[64,1152]{1,0:T(8,128)S(1)} %get-tuple-element.44), channel_id=1, source_target_pairs={{0,1},{1,0},{2,3},{3,2},{4,5},{5,4},{6,7},{7,6},{8,9},{9,8},{10,11... | collective-permute-start | bytes 884744 | tf_op jit(solution)/shard_map/ppermute | solution.py:512

commit v10 on v9

--- a/solution.py
+++ b/solution.py
@@ -197,7 +197,7 @@
     put_side_by_side(out_ref, values)
 
 
-def share_kernel(small_ref, contrast_ref, back_ref, _, marks_ref, share_ref):
+def share_kernel(small_ref, contrast_ref, back_ref, marks_ref, share_ref):
     r = small_ref[2:3, 0:1]
     cells = contrast_ref.shape[2]
     for q in range(back_ref.shape[0]):
@@ -475,7 +475,7 @@
             jax.ShapeDtypeStruct((blocks, 4, LANES), F32),
             jax.ShapeDtypeStruct((blocks,) + block, F32),
         ),
-        (small, contrast, back, green),
+        (small, contrast, back),
         [],
         "share",
     )

time: 111 us -> 110 us (level)
  local copies, waits for them, and re-layouts: 7.29 us -> 4.9 us
  waiting for transfers between devices: 1.5 us -> 3.14 us
    unnamed x5, local copies, waits for them, and re-layouts: 5.99 us -> 3.6 us
    ppermute x3, waiting for transfers between devices: 0.01 us -> 1.66 us  [local_owners(): arrived.append(lax.ppermute(start, both, pairs))]
  transfers between devices with their start and end apart: 9 -> 9, of which waited for: 2 -> 3; matrix products, arithmetic and copies ran while one was open for 0% -> 0% of each run, Pallas kernels for 9% -> 9%
where the time goes in v10:
time: 110 us
  blocking collectives  82.8 us (75%)
  Pallas kernels  12.2 us (11%)
  starting transfers between devices  5.34 us (5%)
  local copies, waits for them, and re-layouts  4.9 us (4%)
  waiting for transfers between devices  3.14 us (3%)
    all_to_all x3, blocking collectives, local_owners(): y_msg = lax.all_to_all(y_msg, both, 0, 0, tiled=True)  44.8 us
    all_to_all x3, blocking collectives, local_owners(): x_msg = lax.all_to_all(x_msg, both, 0, 0, tiled=True)  37.9 us
    pallas_call x15, Pallas kernels, whole_call(): pl.pallas_call(kernel, out_shape=out_shape, in_specs=[vmem] * len(operand...  12.2 us
    ppermute x3, starting transfers between devices, local_owners(): arrived.append(lax.ppermute(start, both, pairs))  3.96 us
    unnamed x5, local copies, waits for them, and re-layouts  3.6 us
  transfers between devices with their start and end apart: 9, of which 3 were waited for; matrix products, arithmetic and copies ran while one was open for 0% of the time, Pallas kernels for 9%

profile of v10, /device:TPU:0, one launch (start us, length us, event | category | flops | bytes accessed | tf_op | source)
XLA Modules:
  0.0 110.1 jit_solution(16817289619504391575)
XLA Ops:
  0.0 1.1 copy.13
  1.1 0.8 select_select_fusion.1.refs_0_.small_ref
  1.9 0.3 start.1
  2.3 4.0 %collective-permute-start.2 = (bf16[64,1152]{1,0:T(8,128)(2,1)S(1)}, bf16[64,1152]{1,0:T(8,128)(2,1)S(1)}, u32[]{:S(2)}, u32[]{:S(2)}) collective-permute-start(bf16[64,1152]{1,0:T(8,128)(2,1)S(1)} %get-tuple-element.27.refs_2_), channel_id=1, source_target_pairs={{0,6},{1,7},{2,3},{3,2},{4,5},{5,4},{6,0},{7,1},{8,10},{9,11},{10,... | collective-permute-start | bytes 442376 | tf_op jit(solution)/shard_map/ppermute | solution.py:471
  6.2 0.0 collective-permute-start.1
  6.2 0.0 collective-permute-start
  7.0 0.1 share.1
  7.1 0.0 copy-start
  7.1 2.5 %copy-done = bf16[1,1,12,2,288,288]{5,4,3,2,1,0:T(8,128)(2,1)S(1)} copy-done((bf16[1,1,12,2,288,288]{5,4,3,2,1,0:T(8,128)(2,1)S(1)}, bf16[1,1,12,2,288,288]{5,4,3,2,1,0:T(8,128)(2,1)}, u32[]{:S(2)}) %copy-start) | copy-done | bytes 3981336
  9.6 0.0 copy-start.1
  9.6 2.0 %direct_0.1 = (f32[4,64,288]{2,1,0:T(8,128)S(1)}, f32[64,1152]{1,0:T(8,128)S(1)}) custom-call(s32[4,128]{1,0:T(4,128)S(1)} %pad_add_fusion.refs_0_, bf16[12,2,288,288]{3,2,1,0:T(8,128)(2,1)S(1)} %bitcast.18, bf16[64,1152]{1,0:T(8,128)(2,1)S(1)} %get-tuple-element.27.refs_2_), custom_call_target="tpu_custom_call" | custom-call | tf_op jit(solution)/shard_map/direct_0/pallas_call | solution.py:394
  11.6 0.0 collective-permute-done.2
  11.6 1.7 %collective-permute-done.1 = bf16[64,1152]{1,0:T(8,128)(2,1)S(1)} collective-permute-done((bf16[64,1152]{1,0:T(8,128)(2,1)S(1)}, bf16[64,1152]{1,0:T(8,128)(2,1)S(1)}, u32[]{:S(2)}, u32[]{:S(2)}) %collective-permute-start.1) | collective-permute-done | bytes 147488 | tf_op jit(solution)/shard_map/ppermute | solution.py:471
  13.2 0.0 collective-permute-done
  13.3 0.1 collective-permute-start.3
  13.4 1.4 %collective-permute-done.3.refs_3_ = bf16[64,1152]{1,0:T(8,128)(2,1)S(1)} collective-permute-done((bf16[64,1152]{1,0:T(8,128)(2,1)S(1)}, bf16[64,1152]{1,0:T(8,128)(2,1)S(1)}, u32[]{:S(2)}, u32[]{:S(2)}) %collective-permute-start.3) | collective-permute-done | bytes 147488 | tf_op jit(solution)/shard_map/ppermute | solution.py:507
  14.7 0.1 collective-permute-start.4
  14.9 0.0 copy-done.1
  14.9 1.3 %mirror_0.1.mirror_ref = f32[4,64,288]{2,1,0:T(8,128)S(1)} custom-call(s32[4,128]{1,0:T(4,128)S(1)} %pad_add_fusion.refs_0_, bf16[12,2,288,288]{3,2,1,0:T(8,128)(2,1)S(1)} %bitcast.19, bf16[64,1152]{1,0:T(8,128)(2,1)S(1)} %select_select_fusion.refs_2_, bf16[64,1152]{1,0:T(8,128)(2,1)S(1)} %collective-permute-done.3.refs_3_, ...), custom_call_target="tpu_custom_call" | custom-call | tf_op jit(solution)/shard_map/mirror_0/pallas_call | solution.py:394
  16.2 0.1 collective-permute-done.4.got_ref
  16.3 0.3 pack_0.1
  16.6 17.2 %all_to_all.30.refs_0_ = s16[32,4,1280]{2,1,0:T(4,128)(2,1)S(1)} all-to-all(s16[32,4,1280]{2,1,0:T(4,128)(2,1)S(1)} %pack_0.1), channel_id=1, replica_groups=mesh['row'=4,'col'=8] {'row','col'}, dimensions={0} | all-to-all | bytes 655360 | tf_op jit(solution)/shard_map/all_to_all | solution.py:526
  33.8 0.4 update_0.1
  34.2 13.6 %all_to_all.31.refs_2_ = bf16[32,4,1152]{2,1,0:T(4,128)(2,1)S(1)} all-to-all(bf16[32,4,1152]{2,1,0:T(4,128)(2,1)S(1)} %get-tuple-element.39), channel_id=1, replica_groups=mesh['row'=4,'col'=8] {'row','col'}, dimensions={0} | all-to-all | bytes 589824 | tf_op jit(solution)/shard_map/all_to_all | solution.py:542
  47.8 0.0 collective-permute-start.5
  47.8 1.9 %direct_1.1 = (f32[4,64,288]{2,1,0:T(8,128)S(1)}, f32[64,1152]{1,0:T(8,128)S(1)}) custom-call(s32[4,128]{1,0:T(4,128)S(1)} %pad_add_fusion.refs_0_, bf16[12,2,288,288]{3,2,1,0:T(8,128)(2,1)S(1)} %bitcast.20, bf16[32,4,1152]{2,1,0:T(4,128)(2,1)S(1)} %all_to_all.31.refs_2_), custom_call_target="tpu_custom_call" | custom-call | tf_op jit(solution)/shard_map/direct_1/pallas_call | solution.py:394
  49.8 0.6 collective-permute-start.6
  50.3 0.0 collective-permute-done.5.refs_3_
  50.3 1.3 %mirror_1.1.mirror_ref = f32[4,64,288]{2,1,0:T(8,128)S(1)} custom-call(s32[4,128]{1,0:T(4,128)S(1)} %pad_add_fusion.refs_0_, bf16[12,2,288,288]{3,2,1,0:T(8,128)(2,1)S(1)} %bitcast.21, bf16[32,4,1152]{2,1,0:T(4,128)(2,1)S(1)} %all_to_all.31.refs_2_, bf16[32,4,1152]{2,1,0:T(4,128)(2,1)S(1)} %collective-permute-done.5.refs_3_, ...), custom_call_target="tpu_custom_call" | custom-call | tf_op jit(solution)/shard_map/mirror_1/pallas_call | solution.py:394
  51.7 0.0 collective-permute-done.6.got_ref
  51.7 0.3 pack_1.1
  52.0 14.1 %all_to_all.32.refs_0_ = s16[32,4,1280]{2,1,0:T(4,128)(2,1)S(1)} all-to-all(s16[32,4,1280]{2,1,0:T(4,128)(2,1)S(1)} %pack_1.1), channel_id=1, replica_groups=mesh['row'=4,'col'=8] {'row','col'}, dimensions={0} | all-to-all | bytes 655360 | tf_op jit(solution)/shard_map/all_to_all | solution.py:526
  66.2 0.4 update_1.1
  66.6 13.6 %all_to_all.33.refs_2_ = bf16[32,4,1152]{2,1,0:T(4,128)(2,1)S(1)} all-to-all(bf16[32,4,1152]{2,1,0:T(4,128)(2,1)S(1)} %update_1.1), channel_id=1, replica_groups=mesh['row'=4,'col'=8] {'row','col'}, dimensions={0} | all-to-all | bytes 589824 | tf_op jit(solution)/shard_map/all_to_all | solution.py:542
  80.2 0.0 collective-permute-start.7
  80.2 1.9 %direct_2.1 = (f32[4,64,288]{2,1,0:T(8,128)S(1)}, f32[64,1152]{1,0:T(8,128)S(1)}) custom-call(s32[4,128]{1,0:T(4,128)S(1)} %pad_add_fusion.refs_0_, bf16[12,2,288,288]{3,2,1,0:T(8,128)(2,1)S(1)} %bitcast.22, bf16[32,4,1152]{2,1,0:T(4,128)(2,1)S(1)} %all_to_all.33.refs_2_), custom_call_target="tpu_custom_call" | custom-call | tf_op jit(solution)/shard_map/direct_2/pallas_call | solution.py:394
  82.2 0.6 collective-permute-start.8
  82.7 0.0 collective-permute-done.7.refs_3_
  82.7 1.3 %mirror_2.1.mirror_ref = f32[4,64,288]{2,1,0:T(8,128)S(1)} custom-call(s32[4,128]{1,0:T(4,128)S(1)} %pad_add_fusion.refs_0_, bf16[12,2,288,288]{3,2,1,0:T(8,128)(2,1)S(1)} %bitcast.23, bf16[32,4,1152]{2,1,0:T(4,128)(2,1)S(1)} %all_to_all.33.refs_2_, bf16[32,4,1152]{2,1,0:T(4,128)(2,1)S(1)} %collective-permute-done.7.refs_3_), custom_call_target="tpu_custom_call" | custom-call | tf_op jit(solution)/shard_map/mirror_2/pallas_call | solution.py:394
  84.1 0.0 collective-permute-done.8.got_ref
  84.1 0.2 pack_2.1
  84.3 13.5 %all_to_all.34.refs_0_ = bf16[32,4,1152]{2,1,0:T(4,128)(2,1)S(1)} all-to-all(bf16[32,4,1152]{2,1,0:T(4,128)(2,1)S(1)} %pack_2.1), channel_id=1, replica_groups=mesh['row'=4,'col'=8] {'row','col'}, dimensions={0} | all-to-all | bytes 589824 | tf_op jit(solution)/shard_map/all_to_all | solution.py:526
  97.8 0.2 last.1
  98.0 10.7 %all_to_all.35.msg_ref = s16[32,4,640]{2,1,0:T(4,128)(2,1)S(1)} all-to-all(s16[32,4,640]{2,1,0:T(4,128)(2,1)S(1)} %last.1), channel_id=1, replica_groups=mesh['row'=4,'col'=8] {'row','col'}, dimensions={0} | all-to-all | bytes 327680 | tf_op jit(solution)/shard_map/all_to_all | solution.py:542
  108.7 0.1 finish.1
  108.8 0.3 copy.14
  109.1 1.0 broadcast_in_dim.12
  (7 shorter events, 0.1 us)
Async XLA Ops:
  2.3 9.3 %collective-permute-start.2 = (bf16[64,1152]{1,0:T(8,128)(2,1)S(1)}, bf16[64,1152]{1,0:T(8,128)(2,1)S(1)}, u32[]{:S(2)}, u32[]{:S(2)}) collective-permute-start(bf16[64,1152]{1,0:T(8,128)(2,1)S(1)} %get-tuple-element.27.refs_2_), channel_id=1, source_target_pairs={{0,6},{1,7},{2,3},{3,2},{4,5},{5,4},{6,0},{7,1},{8,10},{9,11},{10,... | collective-permute-start | bytes 442376 | tf_op jit(solution)/shard_map/ppermute | solution.py:471
  6.2 7.0 %collective-permute-start.1 = (bf16[64,1152]{1,0:T(8,128)(2,1)S(1)}, bf16[64,1152]{1,0:T(8,128)(2,1)S(1)}, u32[]{:S(2)}, u32[]{:S(2)}) collective-permute-start(bf16[64,1152]{1,0:T(8,128)(2,1)S(1)} %get-tuple-element.27.refs_2_), channel_id=1, source_target_pairs={{0,4},{1,5},{2,3},{3,2},{4,0},{5,1},{6,7},{7,6},{8,9},{9,8},{10,14... | collective-permute-start | bytes 442376 | tf_op jit(solution)/shard_map/ppermute | solution.py:471
  6.2 7.0 %collective-permute-start = (bf16[64,1152]{1,0:T(8,128)(2,1)S(1)}, bf16[64,1152]{1,0:T(8,128)(2,1)S(1)}, u32[]{:S(2)}, u32[]{:S(2)}) collective-permute-start(bf16[64,1152]{1,0:T(8,128)(2,1)S(1)} %get-tuple-element.27.refs_2_), channel_id=1, source_target_pairs={{0,2},{1,3},{2,0},{3,1},{4,5},{5,4},{6,7},{7,6},{8,9},{9,8},{10,12... | collective-permute-start | bytes 442376 | tf_op jit(solution)/shard_map/ppermute | solution.py:471
  7.1 2.5 %copy-start = (bf16[1,1,12,2,288,288]{5,4,3,2,1,0:T(8,128)(2,1)S(1)}, bf16[1,1,12,2,288,288]{5,4,3,2,1,0:T(8,128)(2,1)}, u32[]{:S(2)}) copy-start(bf16[1,1,12,2,288,288]{5,4,3,2,1,0:T(8,128)(2,1)} %param.7) | copy-start | bytes 11943940
  9.6 5.3 %copy-start.1 = (bf16[1,1,12,2,288,288]{5,4,3,2,1,0:T(8,128)(2,1)S(1)}, bf16[1,1,12,2,288,288]{5,4,3,2,1,0:T(8,128)(2,1)}, u32[]{:S(2)}) copy-start(bf16[1,1,12,2,288,288]{5,4,3,2,1,0:T(8,128)(2,1)} %param.7) | copy-start | bytes 11943940
  13.3 1.4 %collective-permute-start.3 = (bf16[64,1152]{1,0:T(8,128)(2,1)S(1)}, bf16[64,1152]{1,0:T(8,128)(2,1)S(1)}, u32[]{:S(2)}, u32[]{:S(2)}) collective-permute-start(bf16[64,1152]{1,0:T(8,128)(2,1)S(1)} %select_select_fusion.refs_2_), channel_id=1, source_target_pairs={{0,1},{1,0},{2,3},{3,2},{4,5},{5,4},{6,7},{7,6},{8,9},{9,8},{10,11... | collective-permute-start | bytes 442376 | tf_op jit(solution)/shard_map/ppermute | solution.py:507
  14.7 1.6 %collective-permute-start.4 = (f32[64,1152]{1,0:T(8,128)S(1)}, f32[64,1152]{1,0:T(8,128)S(1)}, u32[]{:S(2)}, u32[]{:S(2)}) collective-permute-start(f32[64,1152]{1,0:T(8,128)S(1)} %get-tuple-element.37), channel_id=1, source_target_pairs={{0,1},{1,0},{2,3},{3,2},{4,5},{5,4},{6,7},{7,6},{8,9},{9,8},{10,11... | collective-permute-start | bytes 884744 | tf_op jit(solution)/shard_map/ppermute | solution.py:512
  47.8 2.5 %collective-permute-start.5 = (bf16[32,4,1152]{2,1,0:T(4,128)(2,1)S(1)}, bf16[32,4,1152]{2,1,0:T(4,128)(2,1)S(1)}, u32[]{:S(2)}, u32[]{:S(2)}) collective-permute-start(bf16[32,4,1152]{2,1,0:T(4,128)(2,1)S(1)} %all_to_all.31.refs_2_), channel_id=1, source_target_pairs={{0,1},{1,0},{2,3},{3,2},{4,5},{5,4},{6,7},{7,6},{8,9},{9,8},{10,11... | collective-permute-start | bytes 884744 | tf_op jit(solution)/shard_map/ppermute | solution.py:491
  49.8 1.9 %collective-permute-start.6 = (f32[64,1152]{1,0:T(8,128)S(1)}, f32[64,1152]{1,0:T(8,128)S(1)}, u32[]{:S(2)}, u32[]{:S(2)}) collective-permute-start(f32[64,1152]{1,0:T(8,128)S(1)} %get-tuple-element.41), channel_id=1, source_target_pairs={{0,1},{1,0},{2,3},{3,2},{4,5},{5,4},{6,7},{7,6},{8,9},{9,8},{10,11... | collective-permute-start | bytes 884744 | tf_op jit(solution)/shard_map/ppermute | solution.py:512
  80.2 2.5 %collective-permute-start.7 = (bf16[32,4,1152]{2,1,0:T(4,128)(2,1)S(1)}, bf16[32,4,1152]{2,1,0:T(4,128)(2,1)S(1)}, u32[]{:S(2)}, u32[]{:S(2)}) collective-permute-start(bf16[32,4,1152]{2,1,0:T(4,128)(2,1)S(1)} %all_to_all.33.refs_2_), channel_id=1, source_target_pairs={{0,1},{1,0},{2,3},{3,2},{4,5},{5,4},{6,7},{7,6},{8,9},{9,8},{10,11... | collective-permute-start | bytes 884744 | tf_op jit(solution)/shard_map/ppermute | solution.py:491
  82.2 1.9 %collective-permute-start.8 = (f32[64,1152]{1,0:T(8,128)S(1)}, f32[64,1152]{1,0:T(8,128)S(1)}, u32[]{:S(2)}, u32[]{:S(2)}) collective-permute-start(f32[64,1152]{1,0:T(8,128)S(1)} %get-tuple-element.44), channel_id=1, source_target_pairs={{0,1},{1,0},{2,3},{3,2},{4,5},{5,4},{6,7},{7,6},{8,9},{9,8},{10,11... | collective-permute-start | bytes 884744 | tf_op jit(solution)/shard_map/ppermute | solution.py:512

commit v11 on v10

--- a/solution.py
+++ b/solution.py
@@ -491,7 +491,7 @@
             direct_in, mirror_in = x_msg, (x_msg, lax.ppermute(x_msg, "col", core_pairs))
         own, other = whole_call(
             lambda *refs, first=first: direct_kernel(first, *refs),
-            (part, jax.ShapeDtypeStruct((2 * sources, WIDTH), F32)),
+            (part, jax.ShapeDtypeStruct((2 * sources, WIDTH), BF if final else F32)),
             (table, green, direct_in),
             [
                 pltpu.VMEM((blocks, 2 * sources, 2 * entries), BF),

time: 110 us -> 110 us (level)
  no operation moved by 1% of the time
where the time goes in v11:
time: 110 us
  blocking collectives  82.8 us (75%)
  Pallas kernels  12.2 us (11%)
  starting transfers between devices  5.34 us (5%)
  local copies, waits for them, and re-layouts  4.9 us (4%)
  waiting for transfers between devices  3.14 us (3%)
    all_to_all x3, blocking collectives, local_owners(): y_msg = lax.all_to_all(y_msg, both, 0, 0, tiled=True)  44.8 us
    all_to_all x3, blocking collectives, local_owners(): x_msg = lax.all_to_all(x_msg, both, 0, 0, tiled=True)  37.9 us
    pallas_call x15, Pallas kernels, whole_call(): pl.pallas_call(kernel, out_shape=out_shape, in_specs=[vmem] * len(operand...  12.2 us
    ppermute x3, starting transfers between devices, local_owners(): arrived.append(lax.ppermute(start, both, pairs))  3.96 us
    unnamed x5, local copies, waits for them, and re-layouts  3.6 us
  transfers between devices with their start and end apart: 9, of which 3 were waited for; matrix products, arithmetic and copies ran while one was open for 0% of the time, Pallas kernels for 9%

profile of v11, /device:TPU:0, one launch (start us, length us, event | category | flops | bytes accessed | tf_op | source)
XLA Modules:
  0.0 110.1 jit_solution(1696918144306679391)
XLA Ops:
  0.0 1.1 copy.13
  1.1 0.8 select_select_fusion.1.refs_0_.small_ref
  1.9 0.3 start.1
  2.3 4.0 %collective-permute-start.2 = (bf16[64,1152]{1,0:T(8,128)(2,1)S(1)}, bf16[64,1152]{1,0:T(8,128)(2,1)S(1)}, u32[]{:S(2)}, u32[]{:S(2)}) collective-permute-start(bf16[64,1152]{1,0:T(8,128)(2,1)S(1)} %get-tuple-element.27.refs_2_), channel_id=1, source_target_pairs={{0,6},{1,7},{2,3},{3,2},{4,5},{5,4},{6,0},{7,1},{8,10},{9,11},{10,... | collective-permute-start | bytes 442376 | tf_op jit(solution)/shard_map/ppermute | solution.py:471
  6.2 0.0 collective-permute-start.1
  6.2 0.0 collective-permute-start
  7.0 0.1 share.1
  7.1 0.0 copy-start
  7.1 2.5 %copy-done = bf16[1,1,12,2,288,288]{5,4,3,2,1,0:T(8,128)(2,1)S(1)} copy-done((bf16[1,1,12,2,288,288]{5,4,3,2,1,0:T(8,128)(2,1)S(1)}, bf16[1,1,12,2,288,288]{5,4,3,2,1,0:T(8,128)(2,1)}, u32[]{:S(2)}) %copy-start) | copy-done | bytes 3981336
  9.6 0.0 copy-start.1
  9.6 2.0 %direct_0.1 = (f32[4,64,288]{2,1,0:T(8,128)S(1)}, f32[64,1152]{1,0:T(8,128)S(1)}) custom-call(s32[4,128]{1,0:T(4,128)S(1)} %pad_add_fusion.refs_0_, bf16[12,2,288,288]{3,2,1,0:T(8,128)(2,1)S(1)} %bitcast.18, bf16[64,1152]{1,0:T(8,128)(2,1)S(1)} %get-tuple-element.27.refs_2_), custom_call_target="tpu_custom_call" | custom-call | tf_op jit(solution)/shard_map/direct_0/pallas_call | solution.py:394
  11.6 0.0 collective-permute-done.2
  11.6 1.7 %collective-permute-done.1 = bf16[64,1152]{1,0:T(8,128)(2,1)S(1)} collective-permute-done((bf16[64,1152]{1,0:T(8,128)(2,1)S(1)}, bf16[64,1152]{1,0:T(8,128)(2,1)S(1)}, u32[]{:S(2)}, u32[]{:S(2)}) %collective-permute-start.1) | collective-permute-done | bytes 147488 | tf_op jit(solution)/shard_map/ppermute | solution.py:471
  13.2 0.0 collective-permute-done
  13.3 0.1 collective-permute-start.3
  13.4 1.4 %collective-permute-done.3.refs_3_ = bf16[64,1152]{1,0:T(8,128)(2,1)S(1)} collective-permute-done((bf16[64,1152]{1,0:T(8,128)(2,1)S(1)}, bf16[64,1152]{1,0:T(8,128)(2,1)S(1)}, u32[]{:S(2)}, u32[]{:S(2)}) %collective-permute-start.3) | collective-permute-done | bytes 147488 | tf_op jit(solution)/shard_map/ppermute | solution.py:507
  14.7 0.1 collective-permute-start.4
  14.9 0.0 copy-done.1
  14.9 1.3 %mirror_0.1.mirror_ref = f32[4,64,288]{2,1,0:T(8,128)S(1)} custom-call(s32[4,128]{1,0:T(4,128)S(1)} %pad_add_fusion.refs_0_, bf16[12,2,288,288]{3,2,1,0:T(8,128)(2,1)S(1)} %bitcast.19, bf16[64,1152]{1,0:T(8,128)(2,1)S(1)} %select_select_fusion.refs_2_, bf16[64,1152]{1,0:T(8,128)(2,1)S(1)} %collective-permute-done.3.refs_3_, ...), custom_call_target="tpu_custom_call" | custom-call | tf_op jit(solution)/shard_map/mirror_0/pallas_call | solution.py:394
  16.2 0.1 collective-permute-done.4.got_ref
  16.3 0.3 pack_0.1
  16.6 17.2 %all_to_all.30.refs_0_ = s16[32,4,1280]{2,1,0:T(4,128)(2,1)S(1)} all-to-all(s16[32,4,1280]{2,1,0:T(4,128)(2,1)S(1)} %pack_0.1), channel_id=1, replica_groups=mesh['row'=4,'col'=8] {'row','col'}, dimensions={0} | all-to-all | bytes 655360 | tf_op jit(solution)/shard_map/all_to_all | solution.py:526
  33.8 0.4 update_0.1
  34.2 13.6 %all_to_all.31.refs_2_ = bf16[32,4,1152]{2,1,0:T(4,128)(2,1)S(1)} all-to-all(bf16[32,4,1152]{2,1,0:T(4,128)(2,1)S(1)} %get-tuple-element.39), channel_id=1, replica_groups=mesh['row'=4,'col'=8] {'row','col'}, dimensions={0} | all-to-all | bytes 589824 | tf_op jit(solution)/shard_map/all_to_all | solution.py:542
  47.8 0.0 collective-permute-start.5
  47.8 1.9 %direct_1.1 = (f32[4,64,288]{2,1,0:T(8,128)S(1)}, f32[64,1152]{1,0:T(8,128)S(1)}) custom-call(s32[4,128]{1,0:T(4,128)S(1)} %pad_add_fusion.refs_0_, bf16[12,2,288,288]{3,2,1,0:T(8,128)(2,1)S(1)} %bitcast.20, bf16[32,4,1152]{2,1,0:T(4,128)(2,1)S(1)} %all_to_all.31.refs_2_), custom_call_target="tpu_custom_call" | custom-call | tf_op jit(solution)/shard_map/direct_1/pallas_call | solution.py:394
  49.8 0.6 collective-permute-start.6
  50.3 0.0 collective-permute-done.5.refs_3_
  50.3 1.3 %mirror_1.1.mirror_ref = f32[4,64,288]{2,1,0:T(8,128)S(1)} custom-call(s32[4,128]{1,0:T(4,128)S(1)} %pad_add_fusion.refs_0_, bf16[12,2,288,288]{3,2,1,0:T(8,128)(2,1)S(1)} %bitcast.21, bf16[32,4,1152]{2,1,0:T(4,128)(2,1)S(1)} %all_to_all.31.refs_2_, bf16[32,4,1152]{2,1,0:T(4,128)(2,1)S(1)} %collective-permute-done.5.refs_3_, ...), custom_call_target="tpu_custom_call" | custom-call | tf_op jit(solution)/shard_map/mirror_1/pallas_call | solution.py:394
  51.7 0.0 collective-permute-done.6.got_ref
  51.7 0.3 pack_1.1
  52.0 14.1 %all_to_all.32.refs_0_ = s16[32,4,1280]{2,1,0:T(4,128)(2,1)S(1)} all-to-all(s16[32,4,1280]{2,1,0:T(4,128)(2,1)S(1)} %pack_1.1), channel_id=1, replica_groups=mesh['row'=4,'col'=8] {'row','col'}, dimensions={0} | all-to-all | bytes 655360 | tf_op jit(solution)/shard_map/all_to_all | solution.py:526
  66.2 0.4 update_1.1
  66.6 13.6 %all_to_all.33.refs_2_ = bf16[32,4,1152]{2,1,0:T(4,128)(2,1)S(1)} all-to-all(bf16[32,4,1152]{2,1,0:T(4,128)(2,1)S(1)} %update_1.1), channel_id=1, replica_groups=mesh['row'=4,'col'=8] {'row','col'}, dimensions={0} | all-to-all | bytes 589824 | tf_op jit(solution)/shard_map/all_to_all | solution.py:542
  80.2 0.0 collective-permute-start.7
  80.2 1.9 %direct_2.1 = (f32[4,64,288]{2,1,0:T(8,128)S(1)}, bf16[64,1152]{1,0:T(8,128)(2,1)S(1)}) custom-call(s32[4,128]{1,0:T(4,128)S(1)} %pad_add_fusion.refs_0_, bf16[12,2,288,288]{3,2,1,0:T(8,128)(2,1)S(1)} %bitcast.22, bf16[32,4,1152]{2,1,0:T(4,128)(2,1)S(1)} %all_to_all.33.refs_2_), custom_call_target="tpu_custom_call" | custom-call | tf_op jit(solution)/shard_map/direct_2/pallas_call | solution.py:394
  82.2 0.6 collective-permute-start.8
  82.7 0.0 collective-permute-done.7.refs_3_
  82.7 1.3 %mirror_2.1.mirror_ref = f32[4,64,288]{2,1,0:T(8,128)S(1)} custom-call(s32[4,128]{1,0:T(4,128)S(1)} %pad_add_fusion.refs_0_, bf16[12,2,288,288]{3,2,1,0:T(8,128)(2,1)S(1)} %bitcast.23, bf16[32,4,1152]{2,1,0:T(4,128)(2,1)S(1)} %all_to_all.33.refs_2_, bf16[32,4,1152]{2,1,0:T(4,128)(2,1)S(1)} %collective-permute-done.7.refs_3_), custom_call_target="tpu_custom_call" | custom-call | tf_op jit(solution)/shard_map/mirror_2/pallas_call | solution.py:394
  84.1 0.0 collective-permute-done.8.got_ref
  84.1 0.2 pack_2.1
  84.3 13.5 %all_to_all.34.refs_0_ = bf16[32,4,1152]{2,1,0:T(4,128)(2,1)S(1)} all-to-all(bf16[32,4,1152]{2,1,0:T(4,128)(2,1)S(1)} %pack_2.1), channel_id=1, replica_groups=mesh['row'=4,'col'=8] {'row','col'}, dimensions={0} | all-to-all | bytes 589824 | tf_op jit(solution)/shard_map/all_to_all | solution.py:526
  97.8 0.2 last.1
  98.0 10.7 %all_to_all.35.msg_ref = s16[32,4,640]{2,1,0:T(4,128)(2,1)S(1)} all-to-all(s16[32,4,640]{2,1,0:T(4,128)(2,1)S(1)} %last.1), channel_id=1, replica_groups=mesh['row'=4,'col'=8] {'row','col'}, dimensions={0} | all-to-all | bytes 327680 | tf_op jit(solution)/shard_map/all_to_all | solution.py:542
  108.7 0.1 finish.1
  108.9 0.3 copy.14
  109.1 1.0 broadcast_in_dim.12
  (7 shorter events, 0.1 us)
Async XLA Ops:
  2.3 9.3 %collective-permute-start.2 = (bf16[64,1152]{1,0:T(8,128)(2,1)S(1)}, bf16[64,1152]{1,0:T(8,128)(2,1)S(1)}, u32[]{:S(2)}, u32[]{:S(2)}) collective-permute-start(bf16[64,1152]{1,0:T(8,128)(2,1)S(1)} %get-tuple-element.27.refs_2_), channel_id=1, source_target_pairs={{0,6},{1,7},{2,3},{3,2},{4,5},{5,4},{6,0},{7,1},{8,10},{9,11},{10,... | collective-permute-start | bytes 442376 | tf_op jit(solution)/shard_map/ppermute | solution.py:471
  6.2 7.0 %collective-permute-start.1 = (bf16[64,1152]{1,0:T(8,128)(2,1)S(1)}, bf16[64,1152]{1,0:T(8,128)(2,1)S(1)}, u32[]{:S(2)}, u32[]{:S(2)}) collective-permute-start(bf16[64,1152]{1,0:T(8,128)(2,1)S(1)} %get-tuple-element.27.refs_2_), channel_id=1, source_target_pairs={{0,4},{1,5},{2,3},{3,2},{4,0},{5,1},{6,7},{7,6},{8,9},{9,8},{10,14... | collective-permute-start | bytes 442376 | tf_op jit(solution)/shard_map/ppermute | solution.py:471
  6.2 7.0 %collective-permute-start = (bf16[64,1152]{1,0:T(8,128)(2,1)S(1)}, bf16[64,1152]{1,0:T(8,128)(2,1)S(1)}, u32[]{:S(2)}, u32[]{:S(2)}) collective-permute-start(bf16[64,1152]{1,0:T(8,128)(2,1)S(1)} %get-tuple-element.27.refs_2_), channel_id=1, source_target_pairs={{0,2},{1,3},{2,0},{3,1},{4,5},{5,4},{6,7},{7,6},{8,9},{9,8},{10,12... | collective-permute-start | bytes 442376 | tf_op jit(solution)/shard_map/ppermute | solution.py:471
  7.1 2.5 %copy-start = (bf16[1,1,12,2,288,288]{5,4,3,2,1,0:T(8,128)(2,1)S(1)}, bf16[1,1,12,2,288,288]{5,4,3,2,1,0:T(8,128)(2,1)}, u32[]{:S(2)}) copy-start(bf16[1,1,12,2,288,288]{5,4,3,2,1,0:T(8,128)(2,1)} %param.7) | copy-start | bytes 11943940
  9.6 5.3 %copy-start.1 = (bf16[1,1,12,2,288,288]{5,4,3,2,1,0:T(8,128)(2,1)S(1)}, bf16[1,1,12,2,288,288]{5,4,3,2,1,0:T(8,128)(2,1)}, u32[]{:S(2)}) copy-start(bf16[1,1,12,2,288,288]{5,4,3,2,1,0:T(8,128)(2,1)} %param.7) | copy-start | bytes 11943940
  13.3 1.4 %collective-permute-start.3 = (bf16[64,1152]{1,0:T(8,128)(2,1)S(1)}, bf16[64,1152]{1,0:T(8,128)(2,1)S(1)}, u32[]{:S(2)}, u32[]{:S(2)}) collective-permute-start(bf16[64,1152]{1,0:T(8,128)(2,1)S(1)} %select_select_fusion.refs_2_), channel_id=1, source_target_pairs={{0,1},{1,0},{2,3},{3,2},{4,5},{5,4},{6,7},{7,6},{8,9},{9,8},{10,11... | collective-permute-start | bytes 442376 | tf_op jit(solution)/shard_map/ppermute | solution.py:507
  14.7 1.6 %collective-permute-start.4 = (f32[64,1152]{1,0:T(8,128)S(1)}, f32[64,1152]{1,0:T(8,128)S(1)}, u32[]{:S(2)}, u32[]{:S(2)}) collective-permute-start(f32[64,1152]{1,0:T(8,128)S(1)} %get-tuple-element.37), channel_id=1, source_target_pairs={{0,1},{1,0},{2,3},{3,2},{4,5},{5,4},{6,7},{7,6},{8,9},{9,8},{10,11... | collective-permute-start | bytes 884744 | tf_op jit(solution)/shard_map/ppermute | solution.py:512
  47.8 2.5 %collective-permute-start.5 = (bf16[32,4,1152]{2,1,0:T(4,128)(2,1)S(1)}, bf16[32,4,1152]{2,1,0:T(4,128)(2,1)S(1)}, u32[]{:S(2)}, u32[]{:S(2)}) collective-permute-start(bf16[32,4,1152]{2,1,0:T(4,128)(2,1)S(1)} %all_to_all.31.refs_2_), channel_id=1, source_target_pairs={{0,1},{1,0},{2,3},{3,2},{4,5},{5,4},{6,7},{7,6},{8,9},{9,8},{10,11... | collective-permute-start | bytes 884744 | tf_op jit(solution)/shard_map/ppermute | solution.py:491
  49.8 1.9 %collective-permute-start.6 = (f32[64,1152]{1,0:T(8,128)S(1)}, f32[64,1152]{1,0:T(8,128)S(1)}, u32[]{:S(2)}, u32[]{:S(2)}) collective-permute-start(f32[64,1152]{1,0:T(8,128)S(1)} %get-tuple-element.41), channel_id=1, source_target_pairs={{0,1},{1,0},{2,3},{3,2},{4,5},{5,4},{6,7},{7,6},{8,9},{9,8},{10,11... | collective-permute-start | bytes 884744 | tf_op jit(solution)/shard_map/ppermute | solution.py:512
  80.2 2.5 %collective-permute-start.7 = (bf16[32,4,1152]{2,1,0:T(4,128)(2,1)S(1)}, bf16[32,4,1152]{2,1,0:T(4,128)(2,1)S(1)}, u32[]{:S(2)}, u32[]{:S(2)}) collective-permute-start(bf16[32,4,1152]{2,1,0:T(4,128)(2,1)S(1)} %all_to_all.33.refs_2_), channel_id=1, source_target_pairs={{0,1},{1,0},{2,3},{3,2},{4,5},{5,4},{6,7},{7,6},{8,9},{9,8},{10,11... | collective-permute-start | bytes 884744 | tf_op jit(solution)/shard_map/ppermute | solution.py:491
  82.2 1.9 %collective-permute-start.8 = (bf16[64,1152]{1,0:T(8,128)(2,1)S(1)}, bf16[64,1152]{1,0:T(8,128)(2,1)S(1)}, u32[]{:S(2)}, u32[]{:S(2)}) collective-permute-start(bf16[64,1152]{1,0:T(8,128)(2,1)S(1)} %get-tuple-element.44), channel_id=1, source_target_pairs={{0,1},{1,0},{2,3},{3,2},{4,5},{5,4},{6,7},{7,6},{8,9},{9,8},{10,11... | collective-permute-start | bytes 442376 | tf_op jit(solution)/shard_map/ppermute | solution.py:512
